TPU v7x, 128 devices: a whole 4x4x4 slice. The times are simulated.
128 devices in a mesh: level: 4 (over z), space: 32 (over x, y, core).
Axes of the slice: x: 4, y: 4, z: 4, core: 2. Of those that a mesh axis runs over, the one named last changes fastest.
Arguments:
- features: bfloat16 [2048, 96, 512], P(('level', 'space')), may hold values from -6 to 6
- occupancy: int32 [2048, 512], P(('level', 'space')), may hold values from 0 to 1
- brick_coords: int32 [3, 2048], P(None, ('level', 'space')), may hold values from 0 to 15, as said below
- coarse_owner: int32 [256, 1], P(('level', 'space')), may hold values from 0 to 3; in each aligned block of 2 rows (0 to 1, 2 to 3, ...) at most 2 rows name the same one
- conv_weight: bfloat16 [27, 96, 96], replicated, may hold values from -0.125 to 0.125
- conv_gain: float32 [96], replicated, may hold values from 0.25 to 1.75
- conv_shift: float32 [96], replicated, may hold values from -2.5 to 2.5
- reduce_weight: bfloat16 [8, 192, 96], replicated, may hold values from -0.21875 to 0.21875
- down_gain: float32 [192], replicated, may hold values from 0.25 to 1.75
- down_shift: float32 [192], replicated, may hold values from -2.5 to 2.5
Outputs:
- coarse_map: bfloat16 [1024, 192, 512], P(('level', 'space'))
Inputs may be any that keep to these rules, and one draw needn't show every extreme that they name: `brick_coords`: device s of level group l holds, in some order, all 2 x 4 x 2 bricks of tile (s // 4, s mod 4) of region l: x from 2 * (s // 4), y from 4 * (s mod 4), z from 0. `coarse_owner`: in the 2 rows of one device, no owner group is named more than 2 times.
All inputs are finite; a program needn't handle non-finite values.
Results may differ from a plain program's by a relative error of at most 0.0054.
Values may be sent and summed in bfloat16 or wider, within the bound.
No kernel may reach another device: no remote copies, remote signals or barrier semaphores. Data moves between devices by JAX's collectives and lax.ppermute only.
A program may use at most 192 MiB of HBM per device.

v0:
```python
import jax
import jax.numpy as jnp
from jax import lax
from jax.sharding import PartitionSpec as P

BRICK = 8
TX = 2
TY = 4
TZ = 2
CAPC = 2


epsilon = 1e-05


def passed_along(block, axis, distance):
    devices = range(lax.axis_size(axis))
    route = [(i - distance, i) for i in devices if i - distance in devices]
    return lax.ppermute(block, axis, route)


def moments(values, weights):
    total_count, first = lax.psum(
        (jnp.sum(weights), jnp.sum(values * weights, axis=1)), ("level", "space")
    )
    mean = first / total_count
    centered = values - mean[:, None]
    second = lax.psum(jnp.sum(weights * centered * centered, axis=1), ("level", "space"))
    spread = second / total_count
    return (mean, spread)


def edge_range(step, length, width):
    if step == -1:
        return slice(length - width, length)
    if step == 1:
        return slice(0, width)
    return slice(0, length)


def rim_range(step, length):
    if step == -1:
        return slice(0, 1)
    if step == 1:
        return slice(length + 1, length + 2)
    return slice(1, length + 1)


def send_coarse(outgoing, outgoing_mask):
    return (
        lax.all_to_all(outgoing, "level", split_axis=0, concat_axis=0, tiled=True),
        lax.all_to_all(outgoing_mask, "level", split_axis=0, concat_axis=0, tiled=True),
    )


def shards(
    features,
    occupancy,
    brick_coords,
    coarse_owner,
    conv_weight,
    conv_gain,
    conv_shift,
    reduce_weight,
    down_gain,
    down_shift,
):
    space_count = lax.axis_size("space")
    grid_y = min(4, space_count // 4)
    grid_x = space_count // grid_y
    space_place = lax.axis_index("space")
    tile_x = space_place // grid_y
    tile_y = space_place % grid_y
    bricks_here, depth, cells = features.shape
    size_x, size_y, size_z = (TX * BRICK, TY * BRICK, TZ * BRICK)
    position = (brick_coords[0] % TX * TY + brick_coords[1] % TY) * TZ + brick_coords[2]
    slots = jnp.arange(bricks_here, dtype=jnp.int32)
    chooser = (position[None, :] == slots[:, None]).astype(jnp.int32)
    slot_of = jnp.sum(chooser * slots[None, :], axis=1)
    gate = occupancy.astype(jnp.bfloat16)
    active_rows = (features * gate[:, None, :])[slot_of]
    gate_rows = occupancy.astype(jnp.float32)[slot_of]
    active = (
        active_rows.reshape(TX, TY, TZ, depth, BRICK, BRICK, BRICK)
        .transpose(3, 0, 4, 1, 5, 2, 6)
        .reshape(depth, size_x, size_y, size_z)
    )
    region_mask = (
        gate_rows.reshape(TX, TY, TZ, BRICK, BRICK, BRICK)
        .transpose(0, 3, 1, 4, 2, 5)
        .reshape(size_x, size_y, size_z)
    )
    padded_grid = jnp.pad(active, ((0, 0), (1, 1), (1, 1), (1, 1)))
    for step_x, step_y in ((-1, -1), (-1, 0), (-1, 1), (0, -1), (0, 1), (1, -1), (1, 0), (1, 1)):
        inside = (
            (tile_x + step_x >= 0)
            & (tile_x + step_x < grid_x)
            & (tile_y + step_y >= 0)
            & (tile_y + step_y < grid_y)
        )
        offset = -(step_x * grid_y + step_y)
        piece = active[:, edge_range(step_x, size_x, BRICK), edge_range(step_y, size_y, BRICK)]
        arrived = passed_along(piece, "space", offset)
        arrived = arrived[
            :, edge_range(step_x, arrived.shape[1], 1), edge_range(step_y, arrived.shape[2], 1)
        ]
        arrived = jnp.where(inside, arrived, jnp.zeros_like(arrived))
        padded_grid = padded_grid.at[
            :, rim_range(step_x, size_x), rim_range(step_y, size_y), 1 : size_z + 1
        ].set(arrived)
    total = jnp.zeros((depth, size_x * size_y * size_z), jnp.float32)
    for pair_index in range(9):
        shift_a, shift_b = (pair_index // 3, pair_index % 3)
        column = padded_grid[:, shift_a : shift_a + size_x, shift_b : shift_b + size_y, :]
        stacked = jnp.concatenate(
            [
                column[:, :, :, shift_c : shift_c + size_z].reshape(depth, -1)
                for shift_c in range(3)
            ],
            axis=0,
        )
        taps = conv_weight[3 * pair_index : 3 * pair_index + 3]
        joined = taps.transpose(1, 0, 2).reshape(taps.shape[1], -1)
        total = total + jnp.dot(joined, stacked, preferred_element_type=jnp.float32)
    flat_mask = region_mask.reshape(-1)
    conv_out = total * flat_mask
    mean1, var1 = moments(conv_out, flat_mask)
    first_scale = conv_gain / jnp.sqrt(var1 + epsilon)
    normed = (conv_out - mean1[:, None]) * first_scale[:, None] + conv_shift[:, None]
    brick_section = (
        active.reshape(depth, -1).astype(jnp.float32) + flat_mask * jnp.maximum(normed, 0.0)
    ).astype(jnp.bfloat16)
    split_view = brick_section.reshape(depth, size_x // 2, 2, size_y // 2, 2, size_z // 2, 2)
    wide = reduce_weight.shape[1]
    down_total = jnp.zeros((wide, size_x // 2 * (size_y // 2) * (size_z // 2)), jnp.float32)
    for offset_index in range(8):
        off_a, off_b, off_c = (offset_index // 4, offset_index // 2 % 2, offset_index % 2)
        window = split_view[:, :, off_a, :, off_b, :, off_c].reshape(depth, -1)
        down_total = down_total + jnp.dot(
            reduce_weight[offset_index], window, preferred_element_type=jnp.float32
        )
    down = down_total.astype(jnp.bfloat16)
    coarse_mask = region_mask.reshape(size_x // 2, 2, size_y // 2, 2, size_z // 2, 2).max(
        axis=(1, 3, 5)
    )
    blocks_x, blocks_y, blocks_z = (TX // 2, TY // 2, TZ // 2)
    coarse_rows = (
        down.reshape(wide, blocks_x, BRICK, blocks_y, BRICK, blocks_z, BRICK)
        .transpose(1, 3, 5, 0, 2, 4, 6)
        .reshape(-1, wide, cells)
    )
    mask_rows = (
        coarse_mask.reshape(blocks_x, BRICK, blocks_y, BRICK, blocks_z, BRICK)
        .transpose(0, 2, 4, 1, 3, 5)
        .reshape(-1, cells)
    )
    owners = coarse_owner[:, 0]
    quarter = jnp.arange(owners.shape[0], dtype=jnp.int32)
    earlier = (quarter[None, :] < quarter[:, None]) & (owners[None, :] == owners[:, None])
    ranks = jnp.sum(earlier.astype(jnp.int32), axis=1)
    groups = lax.axis_size("level")
    selector = (
        (owners[None, None, :] == jnp.arange(groups, dtype=jnp.int32)[:, None, None])
        & (ranks[None, None, :] == jnp.arange(CAPC, dtype=jnp.int32)[None, :, None])
    ).astype(jnp.bfloat16)
    outgoing = jnp.einsum(
        "dkq,qcn->dkcn", selector, coarse_rows, preferred_element_type=jnp.float32
    ).astype(jnp.bfloat16)
    outgoing_mask = jnp.einsum(
        "dkq,qn->dkn", selector, mask_rows.astype(jnp.bfloat16), preferred_element_type=jnp.float32
    ).astype(jnp.bfloat16)
    arrived_rows, arrived_mask = send_coarse(outgoing, outgoing_mask)
    wide_values = arrived_rows.astype(jnp.float32).transpose(2, 0, 1, 3).reshape(wide, -1)
    mean2, var2 = moments(wide_values, arrived_mask.astype(jnp.float32).reshape(-1))
    scale2 = down_gain / jnp.sqrt(var2 + epsilon)
    normed2 = (arrived_rows.astype(jnp.float32) - mean2[None, None, :, None]) * scale2[
        None, None, :, None
    ] + down_shift[None, None, :, None]
    settled = arrived_mask.astype(jnp.float32)[:, :, None, :] * jnp.maximum(normed2, 0.0)
    return settled.reshape(-1, wide, cells).astype(jnp.bfloat16)


def solution(mesh):
    in_specs = (
        P(("level", "space"), None, None),
        P(("level", "space"), None),
        P(None, ("level", "space")),
        P(("level", "space"), None),
        P(),
        P(),
        P(),
        P(),
        P(),
        P(),
    )
    out_specs = P(("level", "space"), None, None)
    return jax.shard_map(shards, mesh=mesh, in_specs=in_specs, out_specs=out_specs, check_vma=False)
```

profile of v0, /device:TPU:0, one launch (start us, length us, event | category | flops | bytes accessed | tf_op | source)
XLA Modules:
  0.0 507.9 jit_solution(8932357553949293692)
XLA Ops:
  7.1 5.4 %all-to-all-start = ((bf16[4,2,512]{2,1,0:T(2,128)(2,1)}), bf16[4,2,512]{2,1,0:T(2,128)(2,1)S(1)}, u32[]{:S(2)}, u32[]{:S(2)}) async-start(bf16[4,2,512]{2,1,0:T(2,128)(2,1)} %copy.98), calls=%async_computation | async-start | bytes 16384 | tf_op jit(solution)/shard_map/all_to_all | solution.py:52
  12.5 1.5 broadcast_multiply_fusion
  14.7 2.5 copy.99
  17.2 2.0 copy.101
  20.2 1.3 collective-permute-start.7
  21.5 1.3 collective-permute-start.5
  22.8 5.0 collective-permute-start.2
  27.8 8.2 %collective-permute-start = (bf16[96,8,8,16]{0,3,2,1:T(8,128)(2,1)}, bf16[96,8,8,16]{0,3,2,1:T(8,128)(2,1)}, u32[]{:S(2)}, u32[]{:S(2)}) collective-permute-start(bf16[96,8,8,16]{0,3,2,1:T(8,128)(2,1)} %get-tuple-element.143), channel_id=1, source_target_pairs={{0,5},{1,6},{2,7},{3,8},{4,9},{5,10},{6,11},{7,12},{8,13},{9,14},{... | collective-permute-start | bytes 589832 | tf_op jit(solution)/shard_map/ppermute | solution.py:19
  39.3 4.1 copy.100
  48.3 5.3 %copy.111 = f32[96,8192]{1,0:T(8,128)} copy(f32[96,8192]{0,1:T(8,128)} %bitcast.168) | data formatting | bytes 6291456 | tf_op jit(solution)/shard_map/convert_element_type | solution.py:131
  53.5 2.9 pad.36
  56.5 1.4 fusion.105
  57.9 3.1 collective-permute-start.3
  61.6 1.3 collective-permute-start.6
  63.6 7.2 %collective-permute-start.1 = (bf16[96,8,32,16]{0,3,2,1:T(8,128)(2,1)}, bf16[96,8,32,16]{0,3,2,1:T(8,128)(2,1)}, u32[]{:S(2)}, u32[]{:S(2)}) collective-permute-start(bf16[96,8,32,16]{0,3,2,1:T(8,128)(2,1)} %get-tuple-element.145), channel_id=1, source_target_pairs={{0,4},{1,5},{2,6},{3,7},{4,8},{5,9},{6,10},{7,11},{8,12},{9,13},{1... | collective-permute-start | bytes 2359304 | tf_op jit(solution)/shard_map/ppermute | solution.py:19
  72.2 1.3 scatter.26
  74.4 38.7 %collective-permute-done.1 = bf16[96,8,32,16]{0,3,2,1:T(8,128)(2,1)} collective-permute-done((bf16[96,8,32,16]{0,3,2,1:T(8,128)(2,1)}, bf16[96,8,32,16]{0,3,2,1:T(8,128)(2,1)}, u32[]{:S(2)}, u32[]{:S(2)}) %collective-permute-start.1) | collective-permute-done | bytes 786464 | tf_op jit(solution)/shard_map/ppermute | solution.py:19
  114.0 1.7 scatter.29
  115.7 1.3 scatter.30
  117.0 1.6 scatter.31
  118.6 1.6 scatter.34
  120.1 1.3 scatter.35
  121.5 1.7 scatter.36
  123.2 1.3 scatter.39
  124.5 14.7 %fusion.102 = (bf16[96,16,32,16]{0,3,2,1:T(8,128)(2,1)}, bf16[96,16,32,16]{0,3,2,1:T(8,128)(2,1)}, bf16[96,16,32,16]{0,3,2,1:T(8,128)(2,1)}, bf16[96,16,32,16]{0...) fusion(bf16[96,18,34,18]{0,3,2,1:T(8,128)(2,1)} %scatter.39), kind=kLoop, calls=%fused_computation.157 | loop fusion | bytes 25165824 | tf_op jit(solution)/shard_map/slice | solution.py:117
  139.3 14.3 %fusion.101 = (bf16[96,16,32,16]{0,3,2,1:T(8,128)(2,1)S(1)}, bf16[96,16,32,16]{0,3,2,1:T(8,128)(2,1)S(1)}, bf16[96,16,32,16]{0,3,2,1:T(8,128)(2,1)}, bf16[96,16,...) fusion(bf16[96,18,34,18]{0,3,2,1:T(8,128)(2,1)S(1)} %copy-done), kind=kLoop, calls=%fused_computation.156 | loop fusion | bytes 59768832 | tf_op jit(solution)/shard_map/slice | solution.py:117
  153.6 6.8 %fusion.1 = f32[8192,96]{0,1:T(8,128)S(1)} fusion(bf16[96,288]{0,1:T(8,128)(2,1)} %bitcast.217, bf16[96,8192]{0,1:T(8,128)(2,1)} %bitcast.195, bf16[96,8192]{0,1:T(8,128)(2,1)} %bitcast.196, bf16[96,8192]{0,1:T(8,128)(2,1)} %bitcast.197), kind=kOutput, calls=%fused_computation.11 | convolution fusion | flops 467140608 | bytes 7919616 | tf_op jit(solution)/shard_map/dot_general | solution.py:124
  160.4 4.8 convolution_add_fusion.7
  165.3 4.8 convolution_add_fusion.6
  170.1 5.0 convolution_add_fusion.5
  175.2 4.8 convolution_add_fusion.4
  180.0 4.8 convolution_add_fusion.3
  184.8 4.7 convolution_add_fusion.2
  189.6 4.8 convolution_add_fusion.1
  194.4 5.5 %multiply_reduce_fusion = (f32[96]{0:T(128)S(1)}, f32[8192,96]{0,1:T(8,128)}) fusion(f32[8192]{0:T(1024)S(1)} %mul.107, f32[8192,96]{0,1:T(8,128)S(1)} %convolution_add_fusion.1, bf16[96,288]{0,1:T(8,128)(2,1)S(1)} %bitcast.209, bf16[96,8192]{0,1:T(8,128)(2,1)S(1)} %bitcast.172, bf16[96,8192]{0,1:T(8,128)(2,1)S(1)} %bitcast.173, ...), kind=kOutput, calls=%fused_computation.76 | convolution fusion | flops 470286240 | bytes 11098496 | tf_op jit(solution)/shard_map/dot_general | solution.py:124
  200.0 67.0 %all-reduce.2 = (f32[96]{0:T(128)S(1)}, f32[]{:T(128)}) all-reduce(f32[96]{0:T(128)S(1)} %get-tuple-element.159, f32[]{:T(128)} %reduce_sum.78), channel_id=1, replica_groups=mesh['level'=4,'space'=32] {'level','space'}, use_global_device_ids=true, to_apply=%region_4.5 | all-reduce | flops 97 | bytes 776 | tf_op jit(solution)/shard_map/psum | solution.py:23
  267.6 2.5 fusion.54
  270.1 64.8 %psum.44 = f32[96]{0:T(128)S(1)} all-reduce(f32[96]{0:T(128)S(1)} %fusion.54), channel_id=1, replica_groups=mesh['level'=4,'space'=32] {'level','space'}, use_global_device_ids=true, to_apply=%region_8.9 | all-reduce | flops 96 | bytes 768 | tf_op jit(solution)/shard_map/psum | solution.py:28
  335.5 3.8 fusion.60
  339.4 3.1 copy.112
  342.5 4.5 fusion.103
  350.8 1.4 convolution_convert_fusion
  352.2 1.4 copy.116
  353.7 3.7 all-to-all-start.1
  358.0 19.9 %all-to-all-done.1 = bf16[4,2,192,512]{3,2,1,0:T(8,128)(2,1)S(1)} async-done(((bf16[4,2,192,512]{3,2,1,0:T(8,128)(2,1)}), bf16[4,2,192,512]{3,2,1,0:T(8,128)(2,1)S(1)}, u32[]{:S(2)}, u32[]{:S(2)}) %all-to-all-start.1) | async-done | bytes 1572896 | tf_op jit(solution)/shard_map/all_to_all | solution.py:51
  378.3 62.7 %all-reduce.1 = (f32[192]{0:T(256)S(1)}, f32[]{:T(128)}) all-reduce(f32[192]{0:T(256)S(1)} %fusion.53, f32[]{:T(128)} %convert_reduce_fusion), channel_id=1, replica_groups=mesh['level'=4,'space'=32] {'level','space'}, use_global_device_ids=true, to_apply=%region_10.11 | all-reduce | flops 193 | bytes 1544 | tf_op jit(solution)/shard_map/psum | solution.py:23
  442.4 62.5 %psum.47 = f32[192]{0:T(256)S(1)} all-reduce(f32[192]{0:T(256)S(1)} %fusion.55), channel_id=1, replica_groups=mesh['level'=4,'space'=32] {'level','space'}, use_global_device_ids=true, to_apply=%region_14.15 | all-reduce | flops 192 | bytes 1536 | tf_op jit(solution)/shard_map/psum | solution.py:28
  505.5 1.9 fusion.52
  (150 shorter events, 29.6 us)
Async XLA Ops:
  4.7 7.8 %copy-start.2 = (f32[2,4,2,8,8,8]{5,2,4,1,3,0:T(2,128)}, f32[2,4,2,8,8,8]{5,2,4,1,3,0:T(2,128)S(1)}, u32[]{:S(2)}) copy-start(f32[2,4,2,8,8,8]{5,2,4,1,3,0:T(2,128)S(1)} %copy.136) | copy-start | bytes 98308
  7.1 346.5 %all-to-all-start = ((bf16[4,2,512]{2,1,0:T(2,128)(2,1)}), bf16[4,2,512]{2,1,0:T(2,128)(2,1)S(1)}, u32[]{:S(2)}, u32[]{:S(2)}) async-start(bf16[4,2,512]{2,1,0:T(2,128)(2,1)} %copy.98), calls=%async_computation | async-start | bytes 16384 | tf_op jit(solution)/shard_map/all_to_all | solution.py:52
  19.1 19.4 %copy-start.3 = (f32[2,4,2,8,8,8]{5,2,4,1,3,0:T(2,128)S(1)}, f32[2,4,2,8,8,8]{5,2,4,1,3,0:T(2,128)}, u32[]{:S(2)}) copy-start(f32[2,4,2,8,8,8]{5,2,4,1,3,0:T(2,128)} %copy-done.2) | copy-start | bytes 98308
  20.2 37.6 %collective-permute-start.7 = (bf16[96,8,8,16]{0,3,2,1:T(8,128)(2,1)}, bf16[96,8,8,16]{0,3,2,1:T(8,128)(2,1)}, u32[]{:S(2)}, u32[]{:S(2)}) collective-permute-start(bf16[96,8,8,16]{0,3,2,1:T(8,128)(2,1)} %get-tuple-element.140), channel_id=1, source_target_pairs={{5,0},{6,1},{7,2},{8,3},{9,4},{10,5},{11,6},{12,7},{13,8},{14,9},{... | collective-permute-start | bytes 589832 | tf_op jit(solution)/shard_map/ppermute | solution.py:19
  21.5 40.1 %collective-permute-start.5 = (bf16[96,8,8,16]{0,3,2,1:T(8,128)(2,1)}, bf16[96,8,8,16]{0,3,2,1:T(8,128)(2,1)}, u32[]{:S(2)}, u32[]{:S(2)}) collective-permute-start(bf16[96,8,8,16]{0,3,2,1:T(8,128)(2,1)} %get-tuple-element.141), channel_id=1, source_target_pairs={{3,0},{4,1},{5,2},{6,3},{7,4},{8,5},{9,6},{10,7},{11,8},{12,9},{13... | collective-permute-start | bytes 589832 | tf_op jit(solution)/shard_map/ppermute | solution.py:19
  22.8 40.8 %collective-permute-start.2 = (bf16[96,8,8,16]{0,3,2,1:T(8,128)(2,1)}, bf16[96,8,8,16]{0,3,2,1:T(8,128)(2,1)}, u32[]{:S(2)}, u32[]{:S(2)}) collective-permute-start(bf16[96,8,8,16]{0,3,2,1:T(8,128)(2,1)} %get-tuple-element.142), channel_id=1, source_target_pairs={{0,3},{1,4},{2,5},{3,6},{4,7},{5,8},{6,9},{7,10},{8,11},{9,12},{10... | collective-permute-start | bytes 589832 | tf_op jit(solution)/shard_map/ppermute | solution.py:19
  27.8 43.7 %collective-permute-start = (bf16[96,8,8,16]{0,3,2,1:T(8,128)(2,1)}, bf16[96,8,8,16]{0,3,2,1:T(8,128)(2,1)}, u32[]{:S(2)}, u32[]{:S(2)}) collective-permute-start(bf16[96,8,8,16]{0,3,2,1:T(8,128)(2,1)} %get-tuple-element.143), channel_id=1, source_target_pairs={{0,5},{1,6},{2,7},{3,8},{4,9},{5,10},{6,11},{7,12},{8,13},{9,14},{... | collective-permute-start | bytes 589832 | tf_op jit(solution)/shard_map/ppermute | solution.py:19
  37.2 36.3 %collective-permute-start.4 = (bf16[96,16,8,16]{0,3,2,1:T(8,128)(2,1)}, bf16[96,16,8,16]{0,3,2,1:T(8,128)(2,1)}, u32[]{:S(2)}, u32[]{:S(2)}) collective-permute-start(bf16[96,16,8,16]{0,3,2,1:T(8,128)(2,1)} %get-tuple-element.146), channel_id=1, source_target_pairs={{1,0},{2,1},{3,2},{4,3},{5,4},{6,5},{7,6},{8,7},{9,8},{10,9},{11,1... | collective-permute-start | bytes 1179656 | tf_op jit(solution)/shard_map/ppermute | solution.py:19
  39.3 4.8 copy-start.26
  57.9 16.5 %collective-permute-start.3 = (bf16[96,16,8,16]{0,3,2,1:T(8,128)(2,1)}, bf16[96,16,8,16]{0,3,2,1:T(8,128)(2,1)S(1)}, u32[]{:S(2)}, u32[]{:S(2)}) collective-permute-start(bf16[96,16,8,16]{0,3,2,1:T(8,128)(2,1)} %get-tuple-element.147), channel_id=1, source_target_pairs={{0,1},{1,2},{2,3},{3,4},{4,5},{5,6},{6,7},{7,8},{8,9},{9,10},{10,1... | collective-permute-start | bytes 1179656 | tf_op jit(solution)/shard_map/ppermute | solution.py:19
  61.6 59.8 %collective-permute-start.6 = (bf16[96,8,32,16]{0,3,2,1:T(8,128)(2,1)S(1)}, bf16[96,8,32,16]{0,3,2,1:T(8,128)(2,1)S(1)}, u32[]{:S(2)}, u32[]{:S(2)}) collective-permute-start(bf16[96,8,32,16]{0,3,2,1:T(8,128)(2,1)S(1)} %get-tuple-element.144), channel_id=1, source_target_pairs={{4,0},{5,1},{6,2},{7,3},{8,4},{9,5},{10,6},{11,7},{12,8},{13,9},{1... | collective-permute-start | bytes 2359304 | tf_op jit(solution)/shard_map/ppermute | solution.py:19
  63.6 49.5 %collective-permute-start.1 = (bf16[96,8,32,16]{0,3,2,1:T(8,128)(2,1)}, bf16[96,8,32,16]{0,3,2,1:T(8,128)(2,1)}, u32[]{:S(2)}, u32[]{:S(2)}) collective-permute-start(bf16[96,8,32,16]{0,3,2,1:T(8,128)(2,1)} %get-tuple-element.145), channel_id=1, source_target_pairs={{0,4},{1,5},{2,6},{3,7},{4,8},{5,9},{6,10},{7,11},{8,12},{9,13},{1... | collective-permute-start | bytes 2359304 | tf_op jit(solution)/shard_map/ppermute | solution.py:19
  124.5 14.7 %copy-start = (bf16[96,18,34,18]{0,3,2,1:T(8,128)(2,1)S(1)}, bf16[96,18,34,18]{0,3,2,1:T(8,128)(2,1)}, u32[]{:S(2)}) copy-start(bf16[96,18,34,18]{0,3,2,1:T(8,128)(2,1)} %scatter.39) | copy-start | bytes 6345220
  153.5 6.8 %copy-start.23 = (bf16[96,16,32,16]{0,3,2,1:T(8,128)(2,1)S(1)}, bf16[96,16,32,16]{0,3,2,1:T(8,128)(2,1)}, u32[]{:S(2)}) copy-start(bf16[96,16,32,16]{0,3,2,1:T(8,128)(2,1)} %get-tuple-element.126) | copy-start | bytes 4718596
  153.5 6.8 %copy-start.24 = (bf16[96,16,32,16]{0,3,2,1:T(8,128)(2,1)S(1)}, bf16[96,16,32,16]{0,3,2,1:T(8,128)(2,1)}, u32[]{:S(2)}) copy-start(bf16[96,16,32,16]{0,3,2,1:T(8,128)(2,1)} %get-tuple-element.127) | copy-start | bytes 4718596
  153.6 6.8 %copy-start.25 = (bf16[96,16,32,16]{0,3,2,1:T(8,128)(2,1)S(1)}, bf16[96,16,32,16]{0,3,2,1:T(8,128)(2,1)}, u32[]{:S(2)}) copy-start(bf16[96,16,32,16]{0,3,2,1:T(8,128)(2,1)} %get-tuple-element.128) | copy-start | bytes 4718596
  153.6 6.8 %copy-start.31 = (bf16[3,96,96]{1,2,0:T(8,128)(2,1)S(1)}, bf16[3,96,96]{1,2,0:T(8,128)(2,1)}, u32[]{:S(2)}) copy-start(bf16[3,96,96]{1,2,0:T(8,128)(2,1)} %copy.127) | copy-start | bytes 165892
  160.4 4.8 copy-start.20
  160.4 4.8 copy-start.21
  160.4 4.8 copy-start.22
  160.4 4.8 copy-start.30
  165.2 4.8 copy-start.17
  165.3 4.8 copy-start.18
  165.3 4.8 copy-start.19
  165.3 4.8 copy-start.29
  170.1 5.0 copy-start.14
  170.1 5.0 copy-start.15
  170.1 5.0 copy-start.16
  175.1 4.8 copy-start.11
  175.1 4.8 copy-start.12
  175.2 4.8 copy-start.13
  180.0 4.8 copy-start.8
  180.0 4.8 copy-start.9
  180.0 4.8 copy-start.10
  184.8 4.8 copy-start.5
  184.8 4.8 copy-start.6
  184.8 4.8 copy-start.7
  189.6 4.8 copy-start.4
  189.6 4.8 copy-start.28
  199.9 134.9 %copy-start.35 = (f32[96]{0:T(128)S(1)}, f32[96]{0:T(128)}, u32[]{:S(2)}) copy-start(f32[96]{0:T(128)} %param.31) | copy-start | bytes 1156
  199.9 135.6 %copy-start.1 = (f32[96,8192]{1,0:T(8,128)S(1)}, f32[96,8192]{1,0:T(8,128)}, u32[]{:S(2)}) copy-start(f32[96,8192]{1,0:T(8,128)} %copy.111) | copy-start | bytes 9437188
  200.0 135.6 %copy-start.34 = (f32[96]{0:T(128)S(1)}, f32[96]{0:T(128)}, u32[]{:S(2)}) copy-start(f32[96]{0:T(128)} %param.32) | copy-start | bytes 1156
  346.9 1.0 copy-start.27
  353.7 151.2 %copy-start.33 = (f32[192]{0:T(256)S(1)}, f32[192]{0:T(256)}, u32[]{:S(2)}) copy-start(f32[192]{0:T(256)} %param.34) | copy-start | bytes 2308
  353.7 151.8 %copy-start.32 = (f32[192]{0:T(256)S(1)}, f32[192]{0:T(256)}, u32[]{:S(2)}) copy-start(f32[192]{0:T(256)} %param.35) | copy-start | bytes 2308
  353.7 24.2 %all-to-all-start.1 = ((bf16[4,2,192,512]{3,2,1,0:T(8,128)(2,1)}), bf16[4,2,192,512]{3,2,1,0:T(8,128)(2,1)S(1)}, u32[]{:S(2)}, u32[]{:S(2)}) async-start(bf16[4,2,192,512]{3,2,1,0:T(8,128)(2,1)} %copy.116), calls=%async_computation.1 | async-start | bytes 3145728 | tf_op jit(solution)/shard_map/all_to_all | solution.py:51
where the time goes:
time: 516 us; the launch traced here: 508 us
  blocking collectives  257 us (50%)
  local copies, waits for them, and re-layouts  80.7 us (16%)
  waiting for transfers between devices  58.6 us (11%)
  matrix products  49.5 us (10%)
  starting transfers between devices  37.7 us (7%)
  other arithmetic  23 us (4%)
    psum x2, blocking collectives, moments(): lax.psum((jnp.sum(weights), jnp.sum(values * weights, axis=1)), ('level',...  130 us
    psum x2, blocking collectives, moments(): lax.psum(jnp.sum(weights * centered * centered, axis=1), ('level', 'space'))  127 us
    dot_general x9, matrix products, shards(): total = total + jnp.dot(joined, stacked, preferred_element_type=jnp.float32)  45.8 us
    ppermute x8, waiting for transfers between devices, passed_along(): return lax.ppermute(block, axis, route)  38.7 us
    slice x2, local copies, waits for them, and re-layouts, shards(): column[:, :, :, shift_c:shift_c + size_z].reshape(depth, -1)  29 us
    ppermute x8, starting transfers between devices, passed_along(): return lax.ppermute(block, axis, route)  28.6 us
    all_to_all x1, waiting for transfers between devices, send_coarse(): lax.all_to_all(outgoing, 'level', split_axis=0, concat_axis=0, tiled=True)  19.9 us
    scatter x8, local copies, waits for them, and re-layouts, shards(): padded_grid = padded_grid.at[:, rim_range(step_x, size_x), rim_range(step...  11.8 us
  transfers between devices with their start and end apart: 10, of which 2 were waited for; matrix products, arithmetic and copies ran while one was open for 28% of the time, Pallas kernels for 0%

commit v1 on v0

--- a/solution.py
+++ b/solution.py
@@ -20,14 +20,25 @@
 
 
 def moments(values, weights):
-    total_count, first = lax.psum(
-        (jnp.sum(weights), jnp.sum(values * weights, axis=1)), ("level", "space")
+    local_count = jnp.sum(weights)
+    local_mean = jnp.sum(values * weights, axis=1) / jnp.maximum(local_count, 1.0)
+    centered = values - local_mean[:, None]
+    local_square = jnp.sum(weights * centered * centered, axis=1)
+    width = local_mean.shape[0]
+    padded = 128 * ((2 * width + 1 + 127) // 128)
+    row = jnp.concatenate(
+        [local_mean, local_square, local_count[None], jnp.zeros(padded - 2 * width - 1, jnp.float32)]
     )
-    mean = first / total_count
-    centered = values - mean[:, None]
-    second = lax.psum(jnp.sum(weights * centered * centered, axis=1), ("level", "space"))
-    spread = second / total_count
-    return (mean, spread)
+    devices = lax.axis_size("level") * lax.axis_size("space")
+    table = lax.all_to_all(
+        jnp.broadcast_to(row, (devices, padded)), ("level", "space"), 0, 0, tiled=True
+    )
+    means = table[:, :width]
+    counts = table[:, 2 * width][:, None]
+    total_count = jnp.sum(counts)
+    mean = jnp.sum(means * counts, axis=0) / total_count
+    square = jnp.sum(table[:, width : 2 * width] + counts * (means - mean) ** 2, axis=0)
+    return (mean, square / total_count)
 
 
 def edge_range(step, length, width):
@@ -44,13 +55,6 @@
     if step == 1:
         return slice(length + 1, length + 2)
     return slice(1, length + 1)
-
-
-def send_coarse(outgoing, outgoing_mask):
-    return (
-        lax.all_to_all(outgoing, "level", split_axis=0, concat_axis=0, tiled=True),
-        lax.all_to_all(outgoing_mask, "level", split_axis=0, concat_axis=0, tiled=True),
-    )
 
 
 def shards(
@@ -99,11 +103,8 @@
             & (tile_y + step_y < grid_y)
         )
         offset = -(step_x * grid_y + step_y)
-        piece = active[:, edge_range(step_x, size_x, BRICK), edge_range(step_y, size_y, BRICK)]
+        piece = active[:, edge_range(step_x, size_x, 1), edge_range(step_y, size_y, 1)]
         arrived = passed_along(piece, "space", offset)
-        arrived = arrived[
-            :, edge_range(step_x, arrived.shape[1], 1), edge_range(step_y, arrived.shape[2], 1)
-        ]
         arrived = jnp.where(inside, arrived, jnp.zeros_like(arrived))
         padded_grid = padded_grid.at[
             :, rim_range(step_x, size_x), rim_range(step_y, size_y), 1 : size_z + 1
@@ -163,20 +164,19 @@
         (owners[None, None, :] == jnp.arange(groups, dtype=jnp.int32)[:, None, None])
         & (ranks[None, None, :] == jnp.arange(CAPC, dtype=jnp.int32)[None, :, None])
     ).astype(jnp.bfloat16)
-    outgoing = jnp.einsum(
-        "dkq,qcn->dkcn", selector, coarse_rows, preferred_element_type=jnp.float32
-    ).astype(jnp.bfloat16)
-    outgoing_mask = jnp.einsum(
-        "dkq,qn->dkn", selector, mask_rows.astype(jnp.bfloat16), preferred_element_type=jnp.float32
-    ).astype(jnp.bfloat16)
-    arrived_rows, arrived_mask = send_coarse(outgoing, outgoing_mask)
-    wide_values = arrived_rows.astype(jnp.float32).transpose(2, 0, 1, 3).reshape(wide, -1)
-    mean2, var2 = moments(wide_values, arrived_mask.astype(jnp.float32).reshape(-1))
+    sent = jnp.where(mask_rows[:, None, :] > 0, coarse_rows, -jnp.inf)
+    gathered = lax.all_gather(sent, "level")
+    choosers = lax.all_gather(selector, "level")
+    mean2, var2 = moments(down.astype(jnp.float32), coarse_mask.reshape(-1))
     scale2 = down_gain / jnp.sqrt(var2 + epsilon)
-    normed2 = (arrived_rows.astype(jnp.float32) - mean2[None, None, :, None]) * scale2[
+    chooser = lax.dynamic_index_in_dim(choosers, lax.axis_index("level"), 1, keepdims=False)
+    slot = jnp.argmax(chooser, axis=2)
+    filled = jnp.max(chooser, axis=2) > 0
+    rows = jnp.take_along_axis(gathered, slot[:, :, None, None], axis=1)
+    normed2 = (rows.astype(jnp.float32) - mean2[None, None, :, None]) * scale2[
         None, None, :, None
     ] + down_shift[None, None, :, None]
-    settled = arrived_mask.astype(jnp.float32)[:, :, None, :] * jnp.maximum(normed2, 0.0)
+    settled = jnp.where(filled[:, :, None, None], jnp.maximum(normed2, 0.0), 0.0)
     return settled.reshape(-1, wide, cells).astype(jnp.bfloat16)
 
 

time: 516 us -> 251 us (0.49); the launches traced: 508 us -> 249 us
  blocking collectives: 257 us -> 7.85 us
  waiting for transfers between devices: 58.6 us -> 22.5 us
  between operations: 1.47 us -> 16 us
  starting transfers between devices: 37.7 us -> 45.5 us
  local copies, waits for them, and re-layouts: 80.7 us -> 87.5 us
    psum x4 -> x0, blocking collectives: 257 us -> none  [the longest x2 130 us: moments(): lax.psum((jnp.sum(weights), jnp.sum(values * weights, axis=1)), ('level',...]
    ppermute x8, waiting for transfers between devices: 38.7 us -> 2.88 us  [passed_along(): return lax.ppermute(block, axis, route)]
    all_to_all x2, starting transfers between devices: 9.09 us -> 17.4 us  [moments(): lax.all_to_all(jnp.broadcast_to(row, (devices, padded)), ('level', 'space...]
    all_gather x0 -> x1, blocking collectives: none -> 7.85 us  [shards(): choosers = lax.all_gather(selector, 'level')]
  transfers between devices with their start and end apart: 10 -> 11, of which waited for: 2 -> 3; matrix products, arithmetic and copies ran while one was open for 28% -> 18% of each run, Pallas kernels for 0% -> 0%
where the time goes in v1:
time: 251 us; the launch traced here: 249 us
  local copies, waits for them, and re-layouts  87.5 us (35%)
  matrix products  46.8 us (19%)
  starting transfers between devices  45.5 us (18%)
  waiting for transfers between devices  22.5 us (9%)
  other arithmetic  22.4 us (9%)
  between operations  16 us (6%)
  blocking collectives  7.85 us (3%)
    dot_general x9, matrix products, shards(): total = total + jnp.dot(joined, stacked, preferred_element_type=jnp.float32)  44.6 us
    slice x2, local copies, waits for them, and re-layouts, shards(): column[:, :, :, shift_c:shift_c + size_z].reshape(depth, -1)  29.4 us
    ppermute x8, starting transfers between devices, passed_along(): return lax.ppermute(block, axis, route)  28 us
    all_to_all x2, waiting for transfers between devices, moments(): lax.all_to_all(jnp.broadcast_to(row, (devices, padded)), ('level', 'space...  19.6 us
    all_to_all x2, starting transfers between devices, moments(): lax.all_to_all(jnp.broadcast_to(row, (devices, padded)), ('level', 'space...  17.4 us
    scatter x8, local copies, waits for them, and re-layouts, shards(): padded_grid = padded_grid.at[:, rim_range(step_x, size_x), rim_range(step...  11.8 us
    unnamed x109, local copies, waits for them, and re-layouts  9.34 us
    all_gather x1, blocking collectives, shards(): choosers = lax.all_gather(selector, 'level')  7.85 us
  transfers between devices with their start and end apart: 11, of which 3 were waited for; matrix products, arithmetic and copies ran while one was open for 18% of the time, Pallas kernels for 0%

profile of v1, /device:TPU:0, one launch (start us, length us, event | category | flops | bytes accessed | tf_op | source)
XLA Modules:
  0.0 248.5 jit_solution(3047512279724566497)
XLA Ops:
  8.3 1.5 broadcast_multiply_fusion
  9.8 1.8 gather_fusion.1
  11.6 2.9 %copy.118 = bf16[16,96,512]{1,2,0:T(8,128)(2,1)S(1)} copy(bf16[16,96,512]{2,1,0:T(8,128)(2,1)} %gather_fusion.1) | data formatting | bytes 3145728 | tf_op jit(solution)/shard_map/gather | solution.py:85
  15.0 1.3 collective-permute-start.7
  16.3 1.3 collective-permute-start.5
  17.6 4.3 %collective-permute-start.2 = (bf16[96,1,1,16]{0,3,2,1:T(8,128)(2,1)S(1)}, bf16[96,1,1,16]{0,3,2,1:T(8,128)(2,1)S(1)}, u32[]{:S(2)}, u32[]{:S(2)}) collective-permute-start(bf16[96,1,1,16]{0,3,2,1:T(8,128)(2,1)S(1)} %get-tuple-element.146), channel_id=1, source_target_pairs={{0,3},{1,4},{2,5},{3,6},{4,7},{5,8},{6,9},{7,10},{8,11},{9,12},{10... | collective-permute-start | bytes 9224 | tf_op jit(solution)/shard_map/ppermute | solution.py:19
  21.9 8.2 %collective-permute-start = (bf16[96,1,1,16]{0,3,2,1:T(8,128)(2,1)S(1)}, bf16[96,1,1,16]{0,3,2,1:T(8,128)(2,1)S(1)}, u32[]{:S(2)}, u32[]{:S(2)}) collective-permute-start(bf16[96,1,1,16]{0,3,2,1:T(8,128)(2,1)S(1)} %get-tuple-element.147), channel_id=1, source_target_pairs={{0,5},{1,6},{2,7},{3,8},{4,9},{5,10},{6,11},{7,12},{8,13},{9,14},{... | collective-permute-start | bytes 9224 | tf_op jit(solution)/shard_map/ppermute | solution.py:19
  30.8 1.3 collective-permute-start.4
  33.4 1.7 fusion.92
  37.7 2.2 reshape_reshape.2
  39.8 1.8 reduce_max.19
  42.5 2.5 copy.119
  52.4 4.7 %pad.36 = bf16[96,18,34,18]{0,3,2,1:T(8,128)(2,1)} pad(bf16[96,16,32,16]{0,3,2,1:T(8,128)(2,1)} %bitcast.163, bf16[]{:T(256)} %constant.358.clone.1), padding=0_0x1_1x1_1x1_1 | pad | bytes 3687938 | tf_op jit(solution)/shard_map/jit(_pad)/pad | solution.py:97
  57.0 3.8 %copy.130 = f32[96,8192]{1,0:T(8,128)S(1)} copy(f32[96,8192]{0,1:T(8,128)} %bitcast.159) | data formatting | bytes 6291456 | tf_op jit(solution)/shard_map/convert_element_type | solution.py:132
  61.5 3.7 %collective-permute-start.3 = (bf16[96,16,1,16]{0,3,2,1:T(8,128)(2,1)}, bf16[96,16,1,16]{0,3,2,1:T(8,128)(2,1)}, u32[]{:S(2)}, u32[]{:S(2)}) collective-permute-start(bf16[96,16,1,16]{0,3,2,1:T(8,128)(2,1)} %get-tuple-element.151), channel_id=1, source_target_pairs={{0,1},{1,2},{2,3},{3,4},{4,5},{5,6},{6,7},{7,8},{8,9},{9,10},{10,1... | collective-permute-start | bytes 147464 | tf_op jit(solution)/shard_map/ppermute | solution.py:19
  65.1 1.3 collective-permute-start.6
  66.5 6.7 %collective-permute-start.1 = (bf16[96,1,32,16]{0,3,2,1:T(8,128)(2,1)S(1)}, bf16[96,1,32,16]{0,3,2,1:T(8,128)(2,1)}, u32[]{:S(2)}, u32[]{:S(2)}) collective-permute-start(bf16[96,1,32,16]{0,3,2,1:T(8,128)(2,1)S(1)} %copy-done.28), channel_id=1, source_target_pairs={{0,4},{1,5},{2,6},{3,7},{4,8},{5,9},{6,10},{7,11},{8,12},{9,13},{1... | collective-permute-start | bytes 294920 | tf_op jit(solution)/shard_map/ppermute | solution.py:19
  73.2 1.3 scatter.26
  74.6 2.9 %collective-permute-done.1 = bf16[96,1,32,16]{0,3,2,1:T(8,128)(2,1)} collective-permute-done((bf16[96,1,32,16]{0,3,2,1:T(8,128)(2,1)S(1)}, bf16[96,1,32,16]{0,3,2,1:T(8,128)(2,1)}, u32[]{:S(2)}, u32[]{:S(2)}) %collective-permute-start.1) | collective-permute-done | bytes 98336 | tf_op jit(solution)/shard_map/ppermute | solution.py:19
  77.5 1.7 scatter.29
  79.2 1.3 scatter.30
  80.5 1.6 scatter.31
  82.1 1.6 scatter.34
  83.7 1.3 scatter.35
  85.9 1.8 scatter.36
  87.6 1.3 scatter.39
  88.9 14.6 %fusion.89 = (bf16[96,16,32,16]{0,3,2,1:T(8,128)(2,1)}, bf16[96,16,32,16]{0,3,2,1:T(8,128)(2,1)}, bf16[96,16,32,16]{0,3,2,1:T(8,128)(2,1)}, bf16[96,16,32,16]{0,...) fusion(bf16[96,18,34,18]{0,3,2,1:T(8,128)(2,1)} %scatter.39), kind=kLoop, calls=%fused_computation.166 | loop fusion | bytes 25165824 | tf_op jit(solution)/shard_map/slice | solution.py:118
  103.6 14.7 %fusion.88 = (bf16[96,16,32,16]{0,3,2,1:T(8,128)(2,1)}, bf16[96,16,32,16]{0,3,2,1:T(8,128)(2,1)}, bf16[96,16,32,16]{0,3,2,1:T(8,128)(2,1)}, bf16[96,16,32,16]{0,...) fusion(bf16[96,18,34,18]{0,3,2,1:T(8,128)(2,1)S(1)} %copy-done), kind=kLoop, calls=%fused_computation.165 | loop fusion | bytes 59768832 | tf_op jit(solution)/shard_map/slice | solution.py:118
  118.4 6.2 %fusion.1 = f32[8192,96]{0,1:T(8,128)S(1)} fusion(bf16[96,288]{0,1:T(8,128)(2,1)S(1)} %bitcast.217, bf16[96,8192]{0,1:T(8,128)(2,1)} %bitcast.190, bf16[96,8192]{0,1:T(8,128)(2,1)} %bitcast.191, bf16[96,8192]{0,1:T(8,128)(2,1)} %bitcast.192), kind=kOutput, calls=%fused_computation.12 | convolution fusion | flops 467140608 | bytes 7919616 | tf_op jit(solution)/shard_map/dot_general | solution.py:125
  124.6 4.8 %convolution_add_fusion.7 = f32[8192,96]{0,1:T(8,128)S(1)} fusion(f32[8192,96]{0,1:T(8,128)S(1)} %fusion.1, bf16[96,288]{0,1:T(8,128)(2,1)S(1)} %bitcast.216, bf16[96,8192]{0,1:T(8,128)(2,1)S(1)} %bitcast.187, bf16[96,8192]{0,1:T(8,128)(2,1)S(1)} %bitcast.188, bf16[96,8192]{0,1:T(8,128)(2,1)S(1)} %bitcast.189), kind=kOutput, calls=%fused_computation.11 | convolution fusion | flops 467927040 | bytes 11065344 | tf_op jit(solution)/shard_map/dot_general | solution.py:125
  129.5 4.8 %convolution_add_fusion.6 = f32[8192,96]{0,1:T(8,128)S(1)} fusion(f32[8192,96]{0,1:T(8,128)S(1)} %convolution_add_fusion.7, bf16[96,288]{0,1:T(8,128)(2,1)S(1)} %bitcast.215, bf16[96,8192]{0,1:T(8,128)(2,1)S(1)} %bitcast.186, bf16[96,8192]{0,1:T(8,128)(2,1)S(1)} %bitcast.185, bf16[96,8192]{0,1:T(8,128)(2,1)S(1)} %bitcast.184), kind=kOutput, calls=%fused_computation.10 | convolution fusion | flops 467927040 | bytes 11065344 | tf_op jit(solution)/shard_map/dot_general | solution.py:125
  134.3 5.0 %convolution_add_fusion.5 = f32[8192,96]{0,1:T(8,128)S(1)} fusion(f32[8192,96]{0,1:T(8,128)S(1)} %convolution_add_fusion.6, bf16[96,288]{0,1:T(8,128)(2,1)S(1)} %bitcast.214, bf16[96,8192]{0,1:T(8,128)(2,1)S(1)} %bitcast.181, bf16[96,8192]{0,1:T(8,128)(2,1)S(1)} %bitcast.182, bf16[96,8192]{0,1:T(8,128)(2,1)S(1)} %bitcast.183), kind=kOutput, calls=%fused_computation.9 | convolution fusion | flops 467927040 | bytes 11065344 | tf_op jit(solution)/shard_map/dot_general | solution.py:125
  139.4 4.8 %convolution_add_fusion.4 = f32[8192,96]{0,1:T(8,128)S(1)} fusion(f32[8192,96]{0,1:T(8,128)S(1)} %convolution_add_fusion.5, bf16[96,288]{0,1:T(8,128)(2,1)S(1)} %bitcast.213, bf16[96,8192]{0,1:T(8,128)(2,1)S(1)} %bitcast.178, bf16[96,8192]{0,1:T(8,128)(2,1)S(1)} %bitcast.179, bf16[96,8192]{0,1:T(8,128)(2,1)S(1)} %bitcast.180), kind=kOutput, calls=%fused_computation.8 | convolution fusion | flops 467927040 | bytes 11065344 | tf_op jit(solution)/shard_map/dot_general | solution.py:125
  144.2 4.8 %convolution_add_fusion.3 = f32[8192,96]{0,1:T(8,128)S(1)} fusion(f32[8192,96]{0,1:T(8,128)S(1)} %convolution_add_fusion.4, bf16[96,288]{0,1:T(8,128)(2,1)S(1)} %bitcast.212, bf16[96,8192]{0,1:T(8,128)(2,1)S(1)} %bitcast.175, bf16[96,8192]{0,1:T(8,128)(2,1)S(1)} %bitcast.176, bf16[96,8192]{0,1:T(8,128)(2,1)S(1)} %bitcast.177), kind=kOutput, calls=%fused_computation.7 | convolution fusion | flops 467927040 | bytes 11065344 | tf_op jit(solution)/shard_map/dot_general | solution.py:125
  149.1 4.8 %convolution_add_fusion.2 = f32[8192,96]{0,1:T(8,128)S(1)} fusion(f32[8192,96]{0,1:T(8,128)S(1)} %convolution_add_fusion.3, bf16[96,288]{0,1:T(8,128)(2,1)S(1)} %bitcast.211, bf16[96,8192]{0,1:T(8,128)(2,1)S(1)} %bitcast.172, bf16[96,8192]{0,1:T(8,128)(2,1)S(1)} %bitcast.173, bf16[96,8192]{0,1:T(8,128)(2,1)S(1)} %bitcast.174), kind=kOutput, calls=%fused_computation.6 | convolution fusion | flops 467927040 | bytes 11065344 | tf_op jit(solution)/shard_map/dot_general | solution.py:125
  153.9 4.8 %convolution_add_fusion.1 = f32[8192,96]{0,1:T(8,128)S(1)} fusion(f32[8192,96]{0,1:T(8,128)S(1)} %convolution_add_fusion.2, bf16[96,288]{0,1:T(8,128)(2,1)S(1)} %bitcast.210, bf16[96,8192]{0,1:T(8,128)(2,1)S(1)} %bitcast.169, bf16[96,8192]{0,1:T(8,128)(2,1)S(1)} %bitcast.170, bf16[96,8192]{0,1:T(8,128)(2,1)S(1)} %bitcast.171), kind=kOutput, calls=%fused_computation.5 | convolution fusion | flops 467927040 | bytes 11065344 | tf_op jit(solution)/shard_map/dot_general | solution.py:125
  158.8 4.9 %multiply_reduce_fusion = (f32[96]{0:T(128)S(1)}, f32[8192,96]{0,1:T(8,128)S(1)}) fusion(f32[8192]{0:T(1024)S(1)} %mul.129, f32[8192,96]{0,1:T(8,128)S(1)} %convolution_add_fusion.1, bf16[96,288]{0,1:T(8,128)(2,1)S(1)} %bitcast.209, bf16[96,8192]{0,1:T(8,128)(2,1)S(1)} %bitcast.167, bf16[96,8192]{0,1:T(8,128)(2,1)S(1)} %bitcast.168, ...), kind=kOutput, calls=%fused_computation.62 | convolution fusion | flops 470286240 | bytes 11098496 | tf_op jit(solution)/shard_map/dot_general | solution.py:125
  163.7 1.6 copy-done.1
  167.4 12.8 %all-to-all-start = ((f32[128,1,256]{2,1,0:T(1,128)}), f32[128,1,256]{2,1,0:T(1,128)S(1)}, u32[]{:S(2)}, u32[]{:S(2)}) async-start(f32[128,1,256]{2,1,0:T(1,128)} %broadcast_in_dim.79), calls=%async_computation | async-start | bytes 262144 | tf_op jit(solution)/shard_map/all_to_all | solution.py:33
  180.3 9.4 %all-to-all-done = f32[128,1,256]{2,1,0:T(1,128)S(1)} async-done(((f32[128,1,256]{2,1,0:T(1,128)}), f32[128,1,256]{2,1,0:T(1,128)S(1)}, u32[]{:S(2)}, u32[]{:S(2)}) %all-to-all-start) | async-done | bytes 131104 | tf_op jit(solution)/shard_map/all_to_all | solution.py:33
  191.9 3.8 %fusion.48 = bf16[96,8192]{1,0:T(8,128)(2,1)} fusion(f32[96,8192]{1,0:T(8,128)S(1)} %copy.130, f32[8192,96]{0,1:T(8,128)} %copy-done.1, f32[8192]{0:T(1024)S(1)} %mul.129, f32[96]{0:T(128)S(1)} %copy-done.40, f32[96]{0:T(128)S(1)} %rsqrt_multiply_fusion.1, f32[96]{0:T(128)S(1)} %broadcast_divide_fusion.2), kind=kLoop, calls=%fused_computation.61 | loop fusion | flops 5505024 | bytes 7898240 | tf_op jit(solution)/shard_map/convert_element_type | solution.py:133
  195.7 3.1 %copy.131 = bf16[96,8192]{0,1:T(8,128)(2,1)S(1)} copy(bf16[96,8192]{1,0:T(8,128)(2,1)} %fusion.48) | data formatting | bytes 3145728 | tf_op jit(solution)/shard_map/convert_element_type | solution.py:133
  198.8 4.5 %fusion.90 = (bf16[96,8,1,16,1,8,1]{0,6,5,4,3,2,1:T(2,128)(2,1)S(1)}, bf16[96,8,1,16,1,8,1]{0,6,5,4,3,2,1:T(2,128)(2,1)S(1)}, bf16[96,8,1,16,1,8,1]{0,6,5,4,3,2,...) fusion(bf16[96,8,2,16,2,8,2]{0,6,5,4,3,2,1:T(2,128)(2,1)S(1)} %, ...), kind=kLoop, calls=%fused_computation.167 | loop fusion | bytes 3145728 | tf_op jit(solution)/shard_map/slice | solution.py:139
  208.1 7.9 %all_gather.8 = bf16[4,4,2,2]{1,3,2,0:T(2,128)(2,1)S(1)} all-gather(bf16[1,4,2,2]{1,3,2,0:T(2,128)(2,1)S(1)} %and_convert_fusion), channel_id=1, replica_groups=mesh['level'=4,'space'=32] {'level'}, dimensions={0}, use_global_device_ids=true | all-gather | bytes 160 | tf_op jit(solution)/shard_map/all_gather | solution.py:169
  220.0 4.6 %all-to-all-start.1 = ((f32[128,1,512]{2,1,0:T(1,128)}), f32[128,1,512]{2,1,0:T(1,128)S(1)}, u32[]{:S(2)}, u32[]{:S(2)}) async-start(f32[128,1,512]{2,1,0:T(1,128)} %broadcast_in_dim.84), calls=%async_computation.1 | async-start | bytes 524288 | tf_op jit(solution)/shard_map/all_to_all | solution.py:33
  225.1 10.2 %all-to-all-done.1 = f32[128,1,512]{2,1,0:T(1,128)S(1)} async-done(((f32[128,1,512]{2,1,0:T(1,128)}), f32[128,1,512]{2,1,0:T(1,128)S(1)}, u32[]{:S(2)}, u32[]{:S(2)}) %all-to-all-start.1) | async-done | bytes 262176 | tf_op jit(solution)/shard_map/all_to_all | solution.py:33
  237.6 2.1 gather_fusion.2
  239.7 2.0 select_convert_fusion
  (191 shorter events, 31.2 us)
Async XLA Ops:
  14.6 17.5 %copy-start.43 = (s32[2,1]{0,1:T(1,128)S(1)}, s32[2,1]{0,1:T(1,128)}, u32[]{:S(2)}) copy-start(s32[2,1]{0,1:T(1,128)} %param.29) | copy-start | bytes 28
  15.0 15.1 %copy-start.2 = (bf16[96,2,8,4,8,2,8]{0,6,5,4,3,2,1:T(8,128)(2,1)}, bf16[96,2,8,4,8,2,8]{0,6,5,4,3,2,1:T(8,128)(2,1)S(1)}, u32[]{:S(2)}) copy-start(bf16[96,2,8,4,8,2,8]{0,6,5,4,3,2,1:T(8,128)(2,1)S(1)} %copy.120) | copy-start | bytes 4718596
  15.0 46.5 %collective-permute-start.7 = (bf16[96,1,1,16]{0,3,2,1:T(8,128)(2,1)S(1)}, bf16[96,1,1,16]{0,3,2,1:T(8,128)(2,1)S(1)}, u32[]{:S(2)}, u32[]{:S(2)}) collective-permute-start(bf16[96,1,1,16]{0,3,2,1:T(8,128)(2,1)S(1)} %get-tuple-element.144), channel_id=1, source_target_pairs={{5,0},{6,1},{7,2},{8,3},{9,4},{10,5},{11,6},{12,7},{13,8},{14,9},{... | collective-permute-start | bytes 9224 | tf_op jit(solution)/shard_map/ppermute | solution.py:19
  16.3 48.8 %collective-permute-start.5 = (bf16[96,1,1,16]{0,3,2,1:T(8,128)(2,1)S(1)}, bf16[96,1,1,16]{0,3,2,1:T(8,128)(2,1)S(1)}, u32[]{:S(2)}, u32[]{:S(2)}) collective-permute-start(bf16[96,1,1,16]{0,3,2,1:T(8,128)(2,1)S(1)} %get-tuple-element.145), channel_id=1, source_target_pairs={{3,0},{4,1},{5,2},{6,3},{7,4},{8,5},{9,6},{10,7},{11,8},{12,9},{13... | collective-permute-start | bytes 9224 | tf_op jit(solution)/shard_map/ppermute | solution.py:19
  17.6 48.9 %collective-permute-start.2 = (bf16[96,1,1,16]{0,3,2,1:T(8,128)(2,1)S(1)}, bf16[96,1,1,16]{0,3,2,1:T(8,128)(2,1)S(1)}, u32[]{:S(2)}, u32[]{:S(2)}) collective-permute-start(bf16[96,1,1,16]{0,3,2,1:T(8,128)(2,1)S(1)} %get-tuple-element.146), channel_id=1, source_target_pairs={{0,3},{1,4},{2,5},{3,6},{4,7},{5,8},{6,9},{7,10},{8,11},{9,12},{10... | collective-permute-start | bytes 9224 | tf_op jit(solution)/shard_map/ppermute | solution.py:19
  21.9 51.3 %collective-permute-start = (bf16[96,1,1,16]{0,3,2,1:T(8,128)(2,1)S(1)}, bf16[96,1,1,16]{0,3,2,1:T(8,128)(2,1)S(1)}, u32[]{:S(2)}, u32[]{:S(2)}) collective-permute-start(bf16[96,1,1,16]{0,3,2,1:T(8,128)(2,1)S(1)} %get-tuple-element.147), channel_id=1, source_target_pairs={{0,5},{1,6},{2,7},{3,8},{4,9},{5,10},{6,11},{7,12},{8,13},{9,14},{... | collective-permute-start | bytes 9224 | tf_op jit(solution)/shard_map/ppermute | solution.py:19
  30.8 43.8 %collective-permute-start.4 = (bf16[96,16,1,16]{0,3,2,1:T(8,128)(2,1)}, bf16[96,16,1,16]{0,3,2,1:T(8,128)(2,1)S(1)}, u32[]{:S(2)}, u32[]{:S(2)}) collective-permute-start(bf16[96,16,1,16]{0,3,2,1:T(8,128)(2,1)} %get-tuple-element.150), channel_id=1, source_target_pairs={{1,0},{2,1},{3,2},{4,3},{5,4},{6,5},{7,6},{8,7},{9,8},{10,9},{11,1... | collective-permute-start | bytes 147464 | tf_op jit(solution)/shard_map/ppermute | solution.py:19
  57.0 9.4 %copy-start.28 = (bf16[96,1,32,16]{0,3,2,1:T(8,128)(2,1)S(1)}, bf16[96,1,32,16]{0,3,2,1:T(8,128)(2,1)}, u32[]{:S(2)}) copy-start(bf16[96,1,32,16]{0,3,2,1:T(8,128)(2,1)} %get-tuple-element.149) | copy-start | bytes 294916
  61.5 13.1 %collective-permute-start.3 = (bf16[96,16,1,16]{0,3,2,1:T(8,128)(2,1)}, bf16[96,16,1,16]{0,3,2,1:T(8,128)(2,1)}, u32[]{:S(2)}, u32[]{:S(2)}) collective-permute-start(bf16[96,16,1,16]{0,3,2,1:T(8,128)(2,1)} %get-tuple-element.151), channel_id=1, source_target_pairs={{0,1},{1,2},{2,3},{3,4},{4,5},{5,6},{6,7},{7,8},{8,9},{9,10},{10,1... | collective-permute-start | bytes 147464 | tf_op jit(solution)/shard_map/ppermute | solution.py:19
  65.1 19.8 %collective-permute-start.6 = (bf16[96,1,32,16]{0,3,2,1:T(8,128)(2,1)}, bf16[96,1,32,16]{0,3,2,1:T(8,128)(2,1)}, u32[]{:S(2)}, u32[]{:S(2)}) collective-permute-start(bf16[96,1,32,16]{0,3,2,1:T(8,128)(2,1)} %get-tuple-element.148), channel_id=1, source_target_pairs={{4,0},{5,1},{6,2},{7,3},{8,4},{9,5},{10,6},{11,7},{12,8},{13,9},{1... | collective-permute-start | bytes 294920 | tf_op jit(solution)/shard_map/ppermute | solution.py:19
  66.5 11.0 %collective-permute-start.1 = (bf16[96,1,32,16]{0,3,2,1:T(8,128)(2,1)S(1)}, bf16[96,1,32,16]{0,3,2,1:T(8,128)(2,1)}, u32[]{:S(2)}, u32[]{:S(2)}) collective-permute-start(bf16[96,1,32,16]{0,3,2,1:T(8,128)(2,1)S(1)} %copy-done.28), channel_id=1, source_target_pairs={{0,4},{1,5},{2,6},{3,7},{4,8},{5,9},{6,10},{7,11},{8,12},{9,13},{1... | collective-permute-start | bytes 294920 | tf_op jit(solution)/shard_map/ppermute | solution.py:19
  88.9 14.7 %copy-start = (bf16[96,18,34,18]{0,3,2,1:T(8,128)(2,1)S(1)}, bf16[96,18,34,18]{0,3,2,1:T(8,128)(2,1)}, u32[]{:S(2)}) copy-start(bf16[96,18,34,18]{0,3,2,1:T(8,128)(2,1)} %scatter.39) | copy-start | bytes 6345220
  103.6 14.8 %copy-start.37 = (bf16[3,96,96]{1,2,0:T(8,128)(2,1)S(1)}, bf16[3,96,96]{1,2,0:T(8,128)(2,1)}, u32[]{:S(2)}) copy-start(bf16[3,96,96]{1,2,0:T(8,128)(2,1)} %copy.147) | copy-start | bytes 165892
  118.3 6.2 %copy-start.24 = (bf16[96,16,32,16]{0,3,2,1:T(8,128)(2,1)S(1)}, bf16[96,16,32,16]{0,3,2,1:T(8,128)(2,1)}, u32[]{:S(2)}) copy-start(bf16[96,16,32,16]{0,3,2,1:T(8,128)(2,1)} %get-tuple-element.130) | copy-start | bytes 4718596
  118.3 6.2 %copy-start.25 = (bf16[96,16,32,16]{0,3,2,1:T(8,128)(2,1)S(1)}, bf16[96,16,32,16]{0,3,2,1:T(8,128)(2,1)}, u32[]{:S(2)}) copy-start(bf16[96,16,32,16]{0,3,2,1:T(8,128)(2,1)} %get-tuple-element.131) | copy-start | bytes 4718596
  118.4 6.2 %copy-start.26 = (bf16[96,16,32,16]{0,3,2,1:T(8,128)(2,1)S(1)}, bf16[96,16,32,16]{0,3,2,1:T(8,128)(2,1)}, u32[]{:S(2)}) copy-start(bf16[96,16,32,16]{0,3,2,1:T(8,128)(2,1)} %get-tuple-element.132) | copy-start | bytes 4718596
  118.4 6.2 %copy-start.36 = (bf16[3,96,96]{1,2,0:T(8,128)(2,1)S(1)}, bf16[3,96,96]{1,2,0:T(8,128)(2,1)}, u32[]{:S(2)}) copy-start(bf16[3,96,96]{1,2,0:T(8,128)(2,1)} %copy.148) | copy-start | bytes 165892
  124.6 4.8 %copy-start.21 = (bf16[96,16,32,16]{0,3,2,1:T(8,128)(2,1)S(1)}, bf16[96,16,32,16]{0,3,2,1:T(8,128)(2,1)}, u32[]{:S(2)}) copy-start(bf16[96,16,32,16]{0,3,2,1:T(8,128)(2,1)} %get-tuple-element.128) | copy-start | bytes 4718596
  124.6 4.8 %copy-start.22 = (bf16[96,16,32,16]{0,3,2,1:T(8,128)(2,1)S(1)}, bf16[96,16,32,16]{0,3,2,1:T(8,128)(2,1)}, u32[]{:S(2)}) copy-start(bf16[96,16,32,16]{0,3,2,1:T(8,128)(2,1)} %get-tuple-element.129) | copy-start | bytes 4718596
  124.6 4.8 %copy-start.23 = (bf16[96,16,32,16]{0,3,2,1:T(8,128)(2,1)S(1)}, bf16[96,16,32,16]{0,3,2,1:T(8,128)(2,1)}, u32[]{:S(2)}) copy-start(bf16[96,16,32,16]{0,3,2,1:T(8,128)(2,1)} %get-tuple-element.127) | copy-start | bytes 4718596
  124.6 4.8 %copy-start.35 = (bf16[3,96,96]{1,2,0:T(8,128)(2,1)S(1)}, bf16[3,96,96]{1,2,0:T(8,128)(2,1)}, u32[]{:S(2)}) copy-start(bf16[3,96,96]{1,2,0:T(8,128)(2,1)} %copy.149) | copy-start | bytes 165892
  129.4 4.8 %copy-start.18 = (bf16[96,16,32,16]{0,3,2,1:T(8,128)(2,1)S(1)}, bf16[96,16,32,16]{0,3,2,1:T(8,128)(2,1)}, u32[]{:S(2)}) copy-start(bf16[96,16,32,16]{0,3,2,1:T(8,128)(2,1)} %get-tuple-element.124) | copy-start | bytes 4718596
  129.4 4.8 %copy-start.19 = (bf16[96,16,32,16]{0,3,2,1:T(8,128)(2,1)S(1)}, bf16[96,16,32,16]{0,3,2,1:T(8,128)(2,1)}, u32[]{:S(2)}) copy-start(bf16[96,16,32,16]{0,3,2,1:T(8,128)(2,1)} %get-tuple-element.125) | copy-start | bytes 4718596
  129.5 4.8 %copy-start.20 = (bf16[96,16,32,16]{0,3,2,1:T(8,128)(2,1)S(1)}, bf16[96,16,32,16]{0,3,2,1:T(8,128)(2,1)}, u32[]{:S(2)}) copy-start(bf16[96,16,32,16]{0,3,2,1:T(8,128)(2,1)} %get-tuple-element.126) | copy-start | bytes 4718596
  129.5 4.8 %copy-start.34 = (bf16[3,96,96]{1,2,0:T(8,128)(2,1)S(1)}, bf16[3,96,96]{1,2,0:T(8,128)(2,1)}, u32[]{:S(2)}) copy-start(bf16[3,96,96]{1,2,0:T(8,128)(2,1)} %copy.150) | copy-start | bytes 165892
  134.3 5.0 %copy-start.15 = (bf16[96,16,32,16]{0,3,2,1:T(8,128)(2,1)S(1)}, bf16[96,16,32,16]{0,3,2,1:T(8,128)(2,1)}, u32[]{:S(2)}) copy-start(bf16[96,16,32,16]{0,3,2,1:T(8,128)(2,1)} %get-tuple-element.121) | copy-start | bytes 4718596
  134.3 5.0 %copy-start.16 = (bf16[96,16,32,16]{0,3,2,1:T(8,128)(2,1)S(1)}, bf16[96,16,32,16]{0,3,2,1:T(8,128)(2,1)}, u32[]{:S(2)}) copy-start(bf16[96,16,32,16]{0,3,2,1:T(8,128)(2,1)} %get-tuple-element.122) | copy-start | bytes 4718596
  134.3 5.0 %copy-start.17 = (bf16[96,16,32,16]{0,3,2,1:T(8,128)(2,1)S(1)}, bf16[96,16,32,16]{0,3,2,1:T(8,128)(2,1)}, u32[]{:S(2)}) copy-start(bf16[96,16,32,16]{0,3,2,1:T(8,128)(2,1)} %get-tuple-element.123) | copy-start | bytes 4718596
  134.3 5.0 %copy-start.33 = (bf16[3,96,96]{1,2,0:T(8,128)(2,1)S(1)}, bf16[3,96,96]{1,2,0:T(8,128)(2,1)}, u32[]{:S(2)}) copy-start(bf16[3,96,96]{1,2,0:T(8,128)(2,1)} %copy.151) | copy-start | bytes 165892
  139.4 4.8 %copy-start.12 = (bf16[96,16,32,16]{0,3,2,1:T(8,128)(2,1)S(1)}, bf16[96,16,32,16]{0,3,2,1:T(8,128)(2,1)}, u32[]{:S(2)}) copy-start(bf16[96,16,32,16]{0,3,2,1:T(8,128)(2,1)} %get-tuple-element.118) | copy-start | bytes 4718596
  139.4 4.8 %copy-start.13 = (bf16[96,16,32,16]{0,3,2,1:T(8,128)(2,1)S(1)}, bf16[96,16,32,16]{0,3,2,1:T(8,128)(2,1)}, u32[]{:S(2)}) copy-start(bf16[96,16,32,16]{0,3,2,1:T(8,128)(2,1)} %get-tuple-element.119) | copy-start | bytes 4718596
  139.4 4.8 %copy-start.14 = (bf16[96,16,32,16]{0,3,2,1:T(8,128)(2,1)S(1)}, bf16[96,16,32,16]{0,3,2,1:T(8,128)(2,1)}, u32[]{:S(2)}) copy-start(bf16[96,16,32,16]{0,3,2,1:T(8,128)(2,1)} %get-tuple-element.120) | copy-start | bytes 4718596
  149.1 4.8 %copy-start.6 = (bf16[96,16,32,16]{0,3,2,1:T(8,128)(2,1)S(1)}, bf16[96,16,32,16]{0,3,2,1:T(8,128)(2,1)}, u32[]{:S(2)}) copy-start(bf16[96,16,32,16]{0,3,2,1:T(8,128)(2,1)} %get-tuple-element.112) | copy-start | bytes 4718596
  149.1 4.8 %copy-start.7 = (bf16[96,16,32,16]{0,3,2,1:T(8,128)(2,1)S(1)}, bf16[96,16,32,16]{0,3,2,1:T(8,128)(2,1)}, u32[]{:S(2)}) copy-start(bf16[96,16,32,16]{0,3,2,1:T(8,128)(2,1)} %get-tuple-element.113) | copy-start | bytes 4718596
  149.1 4.8 %copy-start.8 = (bf16[96,16,32,16]{0,3,2,1:T(8,128)(2,1)S(1)}, bf16[96,16,32,16]{0,3,2,1:T(8,128)(2,1)}, u32[]{:S(2)}) copy-start(bf16[96,16,32,16]{0,3,2,1:T(8,128)(2,1)} %get-tuple-element.114) | copy-start | bytes 4718596
  149.1 4.8 %copy-start.30 = (bf16[3,96,96]{1,2,0:T(8,128)(2,1)S(1)}, bf16[3,96,96]{1,2,0:T(8,128)(2,1)}, u32[]{:S(2)}) copy-start(bf16[3,96,96]{1,2,0:T(8,128)(2,1)} %copy.154) | copy-start | bytes 165892
  153.9 4.8 %copy-start.3 = (bf16[96,16,32,16]{0,3,2,1:T(8,128)(2,1)S(1)}, bf16[96,16,32,16]{0,3,2,1:T(8,128)(2,1)}, u32[]{:S(2)}) copy-start(bf16[96,16,32,16]{0,3,2,1:T(8,128)(2,1)} %get-tuple-element.109) | copy-start | bytes 4718596
  153.9 4.8 %copy-start.4 = (bf16[96,16,32,16]{0,3,2,1:T(8,128)(2,1)S(1)}, bf16[96,16,32,16]{0,3,2,1:T(8,128)(2,1)}, u32[]{:S(2)}) copy-start(bf16[96,16,32,16]{0,3,2,1:T(8,128)(2,1)} %get-tuple-element.110) | copy-start | bytes 4718596
  153.9 4.8 %copy-start.5 = (bf16[96,16,32,16]{0,3,2,1:T(8,128)(2,1)S(1)}, bf16[96,16,32,16]{0,3,2,1:T(8,128)(2,1)}, u32[]{:S(2)}) copy-start(bf16[96,16,32,16]{0,3,2,1:T(8,128)(2,1)} %get-tuple-element.111) | copy-start | bytes 4718596
  153.9 4.8 %copy-start.29 = (bf16[3,96,96]{1,2,0:T(8,128)(2,1)S(1)}, bf16[3,96,96]{1,2,0:T(8,128)(2,1)}, u32[]{:S(2)}) copy-start(bf16[3,96,96]{1,2,0:T(8,128)(2,1)} %copy.155) | copy-start | bytes 165892
  163.7 16.6 %copy-start.44 = (s32[2]{0:T(128)S(1)}, s32[2]{0:T(128)}, u32[]{:S(2)}) copy-start(s32[2]{0:T(128)} %fusion.72) | copy-start | bytes 28
  163.7 27.6 %copy-start.41 = (f32[96]{0:T(128)S(1)}, f32[96]{0:T(128)}, u32[]{:S(2)}) copy-start(f32[96]{0:T(128)} %param.31) | copy-start | bytes 1156
  163.7 28.2 %copy-start.40 = (f32[96]{0:T(128)S(1)}, f32[96]{0:T(128)}, u32[]{:S(2)}) copy-start(f32[96]{0:T(128)} %param.32) | copy-start | bytes 1156
  167.4 22.3 %all-to-all-start = ((f32[128,1,256]{2,1,0:T(1,128)}), f32[128,1,256]{2,1,0:T(1,128)S(1)}, u32[]{:S(2)}, u32[]{:S(2)}) async-start(f32[128,1,256]{2,1,0:T(1,128)} %broadcast_in_dim.79), calls=%async_computation | async-start | bytes 262144 | tf_op jit(solution)/shard_map/all_to_all | solution.py:33
  180.2 57.4 %all-gather.2.cloned.1.call-start = ((), (), s32[]{:S(2)}) async-start(), calls=%async_computation.2 | async-start | bytes 1966080 | tf_op jit(solution)/shard_map/all_gather | solution.py:168
  206.6 30.3 %copy-start.39 = (f32[192]{0:T(256)S(1)}, f32[192]{0:T(256)}, u32[]{:S(2)}) copy-start(f32[192]{0:T(256)} %param.34) | copy-start | bytes 2308
  208.0 31.7 %copy-start.38 = (f32[192]{0:T(256)S(1)}, f32[192]{0:T(256)}, u32[]{:S(2)}) copy-start(f32[192]{0:T(256)} %param.35) | copy-start | bytes 2308
  220.0 15.3 %all-to-all-start.1 = ((f32[128,1,512]{2,1,0:T(1,128)}), f32[128,1,512]{2,1,0:T(1,128)S(1)}, u32[]{:S(2)}, u32[]{:S(2)}) async-start(f32[128,1,512]{2,1,0:T(1,128)} %broadcast_in_dim.84), calls=%async_computation.1 | async-start | bytes 524288 | tf_op jit(solution)/shard_map/all_to_all | solution.py:33
  (8 other events, 28.5 us)
Sparse Core Ops, SparseCore 0:
  208.2 24.2 all-gather.1

commit v2 on v0

v2 whole, which is shorter than its diff:
```python
import jax
import jax.numpy as jnp
import numpy as np
from jax import lax
from jax.experimental import pallas as pl
from jax.experimental.pallas import tpu as pltpu
from jax.sharding import PartitionSpec as P

BRICK = 8
TX = 2
TY = 4
TZ = 2
CAPC = 2
C = 96
C2 = 192
LANES = 128
SX = TX * BRICK
SY = TY * BRICK
SZ = TZ * BRICK
PAIRS = SY // 2
GRID_Y = 4
EMPTY = -3e38
epsilon = 1e-05

bf16 = jnp.bfloat16
f32 = jnp.float32
VMEM = pl.BlockSpec(memory_space=pltpu.VMEM)
SMEM = pl.BlockSpec(memory_space=pltpu.SMEM)


def params(mib=56):
    return pltpu.CompilerParams(vmem_limit_bytes=mib << 20)


def cell_chooser():
    chosen = np.zeros((256, 256), np.float32)
    for row in range(256):
        i2, j, c, half = row >> 7, (row >> 4) & 7, (row >> 3) & 1, row & 7
        z = 2 * half + c
        chosen[row, (z // 8) * 128 + i2 * 64 + j * 8 + z % 8] = 1
    return jnp.asarray(chosen, bf16)


def rows_dot(left, right):
    return lax.dot_general(left, right, (((1,), (1,)), ((), ())), preferred_element_type=f32)


def plain_dot(left, right):
    return lax.dot_general(left, right, (((1,), (0,)), ((), ())), preferred_element_type=f32)


def pack_kernel(coords, features, occupancy, chooser, act, x_low, x_high, y_low, y_high, order):
    for n in range(16):
        place = ((coords[0, n] % TX) * TY + coords[1, n] % TY) * TZ + coords[2, n]
        order[place] = n
    zero_column = jnp.zeros((SX, SZ, LANES), bf16)
    act[:, 0, 0] = zero_column
    act[:, PAIRS, 1] = zero_column
    picks = chooser[...]
    for tx in range(TX):
        for ty in range(TY):
            halves = []
            for tz in range(TZ):
                n = order[(tx * TY + ty) * TZ + tz]
                gate = occupancy[pl.ds(n, 1), :].astype(f32)
                gate = jnp.broadcast_to(gate, (LANES, 512)).astype(bf16)
                halves.append(jnp.concatenate([features[n] * gate[:C], gate[C:]], axis=0))
            for h in range(4):
                lanes = slice(128 * h, 128 * h + 128)
                source = jnp.concatenate([half[:, lanes] for half in halves], axis=1)
                cells = rows_dot(picks, source).reshape(2, 4, 2, SZ, LANES).astype(bf16)
                x = 8 * tx + 2 * h
                act[x : x + 2, 4 * ty : 4 * ty + 4, 1] = cells[:, :, 0]
                act[x : x + 2, 4 * ty + 1 : 4 * ty + 5, 0] = cells[:, :, 1]
    x_low[...] = act[0]
    x_high[...] = act[SX - 1]
    y_low[...] = act[:, 0, 1]
    y_high[...] = act[:, PAIRS, 0]


def pack(coords, features, occupancy):
    face = jax.ShapeDtypeStruct((PAIRS + 1, 2, SZ, LANES), bf16)
    side = jax.ShapeDtypeStruct((SX, SZ, LANES), bf16)
    return pl.pallas_call(
        pack_kernel,
        out_shape=(
            jax.ShapeDtypeStruct((SX, PAIRS + 1, 2, SZ, LANES), bf16),
            face,
            face,
            side,
            side,
        ),
        in_specs=[SMEM, VMEM, VMEM, VMEM],
        out_specs=(VMEM,) * 5,
        scratch_shapes=[pltpu.SMEM((16,), jnp.int32)],
        compiler_params=params(),
        name="pack",
    )(coords, features, occupancy, cell_chooser())


def z_shifted(cells):
    shape = cells.shape[:-2]
    wide = cells.astype(f32).reshape(-1, 2, 8, LANES)
    even, odd = wide[:, 0], wide[:, 1]
    place = lax.broadcasted_iota(jnp.int32, odd.shape, 1)
    before = jnp.where(place == 0, 0.0, pltpu.roll(odd, 1, 1))
    after = jnp.where(place == 7, 0.0, pltpu.roll(even, 7, 1))
    low = jnp.stack([before, even], axis=1).reshape(*shape, SZ, LANES).astype(bf16)
    high = jnp.stack([odd, after], axis=1).reshape(*shape, SZ, LANES).astype(bf16)
    return low, high


def lane_spread():
    row = lax.broadcasted_iota(jnp.int32, (LANES, LANES), 0)
    return jnp.where(row == LANES - 1, 1.0, 0.0).astype(bf16)


def conv_kernel(act, x_low, x_high, y_low, y_high, weight, out, stats, grid, taps, masks):
    space = lax.axis_index("space")
    tile_x, tile_y = space // GRID_Y, space % GRID_Y
    last_x = lax.axis_size("space") // GRID_Y - 1

    def kept(value, inside):
        return value * jnp.where(inside, 1.0, 0.0).astype(bf16)

    def place(x, plane):
        low, high = z_shifted(plane)
        grid[0, x] = low
        grid[1, x] = plane
        grid[2, x] = high

    place(0, kept(x_low[...], tile_x > 0))
    place(SX + 1, kept(x_high[...], tile_x < last_x))

    def fill(x, carry):
        place(x + 1, act[x])
        return carry

    lax.fori_loop(0, SX, fill, 0)
    for c, side in zip((0, 1, 2), (z_shifted(y_low[...])[0], y_low[...], z_shifted(y_low[...])[1])):
        grid[c, 1 : SX + 1, 0, 0] = kept(side, tile_y > 0)
    for c, side in zip((0, 1, 2), (z_shifted(y_high[...])[0], y_high[...], z_shifted(y_high[...])[1])):
        grid[c, 1 : SX + 1, PAIRS, 1] = kept(side, tile_y < GRID_Y - 1)
    taps[...] = jnp.zeros(taps.shape, bf16)
    for a in range(3):
        for b in range(3):
            for c in range(3):
                for parity in range(2):
                    first = (a * 3 + c) * 512 + (b + parity) * LANES
                    taps[first : first + C, parity * LANES : parity * LANES + C] = weight[(a * 3 + b) * 3 + c].T

    def convolve(x, carry):
        total, count = carry
        pieces = []
        for a in range(3):
            for c in range(3):
                for d in range(4):
                    rows = grid[c, x + a, d // 2 : d // 2 + PAIRS, d % 2]
                    pieces.append(rows.reshape(PAIRS * SZ, LANES))
        value = plain_dot(jnp.concatenate(pieces, axis=1), taps[...])
        spread = lane_spread()
        even = grid[1, x + 1, 0:PAIRS, 1].reshape(PAIRS * SZ, LANES)
        odd = grid[1, x + 1, 1 : PAIRS + 1, 0].reshape(PAIRS * SZ, LANES)
        mask = jnp.concatenate([plain_dot(even, spread), plain_dot(odd, spread)], axis=1)
        masks[x] = mask.astype(bf16)
        out[x] = value
        total = total + jnp.sum(value * mask, axis=0, keepdims=True)
        return total, count + jnp.sum(mask, axis=0, keepdims=True)

    zero = jnp.zeros((1, 2 * LANES), f32)
    total, count = lax.fori_loop(0, SX, convolve, (zero, zero))
    total = total[:, :LANES] + total[:, LANES:]
    count = count[:, :LANES] + count[:, LANES:]
    mean = total / jnp.maximum(count, 1.0)
    both = jnp.concatenate([mean, mean], axis=1)

    def spread_out(x, carry):
        gap = (out[x] - both) * masks[x].astype(f32)
        return carry + jnp.sum(gap * gap, axis=0, keepdims=True)

    square = lax.fori_loop(0, SX, spread_out, zero)
    square = square[:, :LANES] + square[:, LANES:]
    lane = lax.broadcasted_iota(jnp.int32, (1, LANES), 1)
    row = jnp.concatenate([jnp.where(lane == LANES - 1, count, mean), square], axis=1)
    stats[...] = jnp.broadcast_to(row, stats.shape)


def convolution(act, x_low, x_high, y_low, y_high, weight, devices):
    return pl.pallas_call(
        conv_kernel,
        out_shape=(
            jax.ShapeDtypeStruct((SX, PAIRS * SZ, 2 * LANES), f32),
            jax.ShapeDtypeStruct((devices, 2 * LANES), f32),
        ),
        in_specs=[VMEM] * 6,
        out_specs=(VMEM, VMEM),
        scratch_shapes=[
            pltpu.VMEM((3, SX + 2, PAIRS + 1, 2, SZ, LANES), bf16),
            pltpu.VMEM((9 * 512, 2 * LANES), bf16),
            pltpu.VMEM((SX, PAIRS * SZ, 2 * LANES), bf16),
        ],
        compiler_params=params(),
        name="conv",
    )(act, x_low, x_high, y_low, y_high, weight)


def padded_row(values):
    return jnp.pad(values, (0, LANES - values.shape[0]))[None]


def section_kernel(conv, act, table, gain, shift, weight, owners, sent, stats, taps, down, cover):
    means, squares = table[:, :LANES], table[:, LANES:]
    counts = table[:, LANES - 1 : LANES]
    whole = jnp.sum(counts, axis=0, keepdims=True)
    mean = jnp.sum(means * counts, axis=0, keepdims=True) / whole
    var = jnp.sum(squares + counts * (means - mean) ** 2, axis=0, keepdims=True) / whole
    lane = lax.broadcasted_iota(jnp.int32, (1, LANES), 1)
    scale = jnp.where(lane < C, gain[...] / jnp.sqrt(var + epsilon), 0.0)
    mean = jnp.where(lane < C, mean, 0.0)
    mean = jnp.concatenate([mean, mean], axis=1)
    scale = jnp.concatenate([scale, scale], axis=1)
    moved = jnp.concatenate([shift[...], shift[...]], axis=1)
    taps[...] = jnp.zeros(taps.shape, bf16)
    for a in range(2):
        for b in range(2):
            for c in range(2):
                first = ((a * 2 + c) * 2 + b) * LANES
                taps[:C2, first : first + C] = weight[(a * 2 + b) * 2 + c]

    def reduce_plane(X, carry):
        total, count = carry
        pieces, covers = [], []
        spread = lane_spread()
        for a in range(2):
            x = 2 * X + a
            even = act[x, 0:PAIRS, 1].reshape(PAIRS * SZ, LANES)
            odd = act[x, 1 : PAIRS + 1, 0].reshape(PAIRS * SZ, LANES)
            even_mask, odd_mask = plain_dot(even, spread), plain_dot(odd, spread)
            mask = jnp.concatenate([even_mask, odd_mask], axis=1)
            active = jnp.concatenate([even, odd], axis=1).astype(f32)
            normed = (conv[x] - mean) * scale + moved
            section = active + mask * jnp.maximum(normed, 0.0)
            section = section.reshape(PAIRS, 2, 8, 2 * LANES)
            for c in range(2):
                pieces.append(section[:, c].reshape(PAIRS * 8, 2 * LANES).astype(bf16))
            both = jnp.maximum(even_mask, odd_mask).reshape(PAIRS, 2, 8, LANES)
            covers.append(jnp.maximum(both[:, 0], both[:, 1]).reshape(PAIRS * 8, LANES))
        value = rows_dot(jnp.concatenate(pieces, axis=1), taps[...])
        value = value.astype(bf16).astype(f32)
        covered = jnp.maximum(covers[0], covers[1])
        covered = jnp.concatenate([covered, covered], axis=1)
        down[X] = value
        cover[X] = covered
        total = total + jnp.sum(value * covered, axis=0, keepdims=True)
        return total, count + jnp.sum(covered, axis=0, keepdims=True)

    zero = jnp.zeros((1, 2 * LANES), f32)
    total, count = lax.fori_loop(0, SX // 2, reduce_plane, (zero, zero))
    mean2 = total / jnp.maximum(count, 1.0)

    def spread_out(X, carry):
        gap = (down[X] - mean2) * cover[X]
        return carry + jnp.sum(gap * gap, axis=0, keepdims=True)

    square = lax.fori_loop(0, SX // 2, spread_out, zero)
    wide_lane = lax.broadcasted_iota(jnp.int32, (1, 2 * LANES), 1)
    row = jnp.concatenate([jnp.where(wide_lane == 2 * LANES - 1, count, mean2), square], axis=1)
    stats[...] = jnp.broadcast_to(row, stats.shape)

    level = lax.axis_index("level")
    groups = lax.axis_size("level")
    unit = (
        lax.broadcasted_iota(jnp.int32, (C2, 2 * LANES), 0)
        == lax.broadcasted_iota(jnp.int32, (C2, 2 * LANES), 1)
    )
    unit = jnp.where(unit, 1.0, 0.0).astype(bf16)
    half = PAIRS // 2 * 8
    rows = []
    for q in range(2):
        value = down[:, q * half : (q + 1) * half].reshape(SX // 2 * half, 2 * LANES)
        covered = cover[:, q * half : (q + 1) * half].reshape(SX // 2 * half, 2 * LANES)
        coded = jnp.where(covered > 0, value, EMPTY).astype(bf16)
        rows.append(rows_dot(unit, coded).astype(bf16))
    first, second = owners[0, 0], owners[1, 0]
    for distance in range(4):
        target = (level + distance) % groups
        for k in range(CAPC):
            takes_first = (first == target) & (k == 0)
            takes_second = (second == target) & (jnp.where(first == second, 1, 0) == k)
            chosen = jnp.where(takes_first, rows[0], jnp.where(takes_second, rows[1], EMPTY))
            sent[distance, k] = chosen.astype(bf16)


def section(conv, act, table, gain, shift, weight, owners):
    return pl.pallas_call(
        section_kernel,
        out_shape=(
            jax.ShapeDtypeStruct((4, CAPC, C2, 512), bf16),
            jax.ShapeDtypeStruct((table.shape[0], 4 * LANES), f32),
        ),
        in_specs=[VMEM] * 6 + [SMEM],
        out_specs=(VMEM, VMEM),
        scratch_shapes=[
            pltpu.VMEM((2 * LANES, 8 * LANES), bf16),
            pltpu.VMEM((SX // 2, PAIRS * 8, 2 * LANES), f32),
            pltpu.VMEM((SX // 2, PAIRS * 8, 2 * LANES), f32),
        ],
        compiler_params=params(),
        name="section",
    )(conv, act, table, gain, shift, weight, owners)


def settle_kernel(own, near, far, back, table, gain, shift, out):
    turned = table[...].T
    means, squares = turned[:C2], turned[2 * LANES : 2 * LANES + C2]
    counts = turned[2 * LANES - 1 : 2 * LANES]
    whole = jnp.sum(counts, axis=1, keepdims=True)
    mean = jnp.sum(means * counts, axis=1, keepdims=True) / whole
    var = jnp.sum(squares + counts * (means - mean) ** 2, axis=1, keepdims=True) / whole
    scale = gain[...] / jnp.sqrt(var + epsilon)
    moved = shift[...]
    level = lax.axis_index("level")
    groups = lax.axis_size("level")
    for distance, source in enumerate((own, near, far, back)):
        origin = (level + groups - distance) % groups
        for k in range(CAPC):
            value = source[k].astype(f32)
            normed = (value - mean) * scale + moved
            out[origin * CAPC + k] = jnp.maximum(normed, 0.0).astype(bf16)


def settle(own, near, far, back, table, gain, shift):
    return pl.pallas_call(
        settle_kernel,
        out_shape=jax.ShapeDtypeStruct((8, C2, 512), bf16),
        in_specs=[VMEM] * 7,
        out_specs=VMEM,
        compiler_params=params(),
        name="settle",
    )(own, near, far, back, table, gain, shift)


def to_all(rows):
    return lax.all_to_all(rows, ("level", "space"), 0, 0, tiled=True)


def shards(
    features,
    occupancy,
    brick_coords,
    coarse_owner,
    conv_weight,
    conv_gain,
    conv_shift,
    reduce_weight,
    down_gain,
    down_shift,
):
    space_count = lax.axis_size("space")
    level_count = lax.axis_size("level")
    grid_x = space_count // GRID_Y

    def from_tile(block, step_x, step_y):
        route = []
        for s in range(space_count):
            x, y = s // GRID_Y, s % GRID_Y
            route.append(((x + step_x) % grid_x * GRID_Y + (y + step_y) % GRID_Y, s))
        return lax.ppermute(block, "space", route)

    act, x_low, x_high, y_low, y_high = pack(brick_coords, features, occupancy)
    y_before = from_tile(y_high, 0, -1)
    y_after = from_tile(y_low, 0, 1)
    tile_y = lax.axis_index("space") % GRID_Y
    for_low = (y_before * (tile_y > 0).astype(bf16), y_after * (tile_y < GRID_Y - 1).astype(bf16))

    def with_corners(face, x):
        face = face.at[0, 0].set(for_low[0][x])
        return face.at[PAIRS, 1].set(for_low[1][x])

    x_before = from_tile(with_corners(x_high, SX - 1), -1, 0)
    x_after = from_tile(with_corners(x_low, 0), 1, 0)
    conv, stats = convolution(
        act, x_before, x_after, y_before, y_after, conv_weight, space_count * level_count
    )
    sent, stats2 = section(
        conv,
        act,
        to_all(stats),
        padded_row(conv_gain),
        padded_row(conv_shift),
        reduce_weight,
        coarse_owner,
    )
    arrived = [
        lax.ppermute(sent[d], "level", [(g, (g + d) % level_count) for g in range(level_count)])
        for d in range(1, level_count)
    ]
    return settle(
        sent[0], *arrived, to_all(stats2), down_gain[:, None], down_shift[:, None]
    )


def solution(mesh):
    in_specs = (
        P(("level", "space"), None, None),
        P(("level", "space"), None),
        P(None, ("level", "space")),
        P(("level", "space"), None),
        P(),
        P(),
        P(),
        P(),
        P(),
        P(),
    )
    out_specs = P(("level", "space"), None, None)
    return jax.shard_map(shards, mesh=mesh, in_specs=in_specs, out_specs=out_specs, check_vma=False)
```

time: 516 us -> 106 us (0.21); the launches traced: 508 us -> 105 us
  blocking collectives: 257 us -> 0 us
  local copies, waits for them, and re-layouts: 80.7 us -> 12.1 us
  matrix products: 49.5 us -> 0 us
  Pallas kernels: 0 us -> 36.4 us
  waiting for transfers between devices: 58.6 us -> 30.1 us
  other arithmetic: 23 us -> 0.02 us
  starting transfers between devices: 37.7 us -> 25.8 us
    psum x4 -> x0, blocking collectives: 257 us -> none  [the longest x2 130 us: moments(): lax.psum((jnp.sum(weights), jnp.sum(values * weights, axis=1)), ('level',...]
    dot_general x19 -> x0, matrix products: 49.5 us -> none  [the longest x9 45.8 us: shards(): total = total + jnp.dot(joined, stacked, preferred_element_type=jnp.float32)]
    slice x7 -> x0, local copies, waits for them, and re-layouts: 37.2 us -> none  [the longest x2 29 us: shards(): column[:, :, :, shift_c:shift_c + size_z].reshape(depth, -1)]
    pallas_call x0 -> x4, Pallas kernels: none -> 36.4 us  [the longest x1 19.9 us: convolution(): pl.pallas_call(conv_kernel, out_shape=(jax.ShapeDtypeStruct((SX, PAIRS *...]
    ppermute x8 -> x7, waiting for transfers between devices: 38.7 us -> 9.88 us  [the longest x4 9.87 us: from_tile(): return lax.ppermute(block, 'space', route)]
    ppermute x8 -> x7, starting transfers between devices: 28.6 us -> 11.4 us  [the longest x4 7.39 us: from_tile(): return lax.ppermute(block, 'space', route)]
    convert_element_type x9 -> x0, local copies, waits for them, and re-layouts: 15.1 us -> none  [the longest x2 9.42 us: shards(): active.reshape(depth, -1).astype(jnp.float32)]
    scatter x8 -> x2, local copies, waits for them, and re-layouts: 11.8 us -> 1.22 us  [the longest x1 0.62 us: with_corners(): return face.at[PAIRS, 1].set(for_low[1][x])]
  transfers between devices with their start and end apart: 10 -> 9, of which waited for: 2 -> 5; matrix products, arithmetic and copies ran while one was open for 28% -> 5% of each run, Pallas kernels for 0% -> 0%
where the time goes in v2:
time: 106 us; the launch traced here: 105 us
  Pallas kernels  36.4 us (34%)
  waiting for transfers between devices  30.1 us (28%)
  starting transfers between devices  25.8 us (24%)
  local copies, waits for them, and re-layouts  12.1 us (11%)
    all_to_all x2, waiting for transfers between devices, to_all(): return lax.all_to_all(rows, ('level', 'space'), 0, 0, tiled=True)  20.2 us
    pallas_call x1, Pallas kernels, convolution(): pl.pallas_call(conv_kernel, out_shape=(jax.ShapeDtypeStruct((SX, PAIRS *...  19.9 us
    all_to_all x2, starting transfers between devices, to_all(): return lax.all_to_all(rows, ('level', 'space'), 0, 0, tiled=True)  14.4 us
    ppermute x4, waiting for transfers between devices, from_tile(): return lax.ppermute(block, 'space', route)  9.87 us
    pallas_call x1, Pallas kernels, section(): pl.pallas_call(section_kernel, out_shape=(jax.ShapeDtypeStruct((4, CAPC,...  8.59 us
    ppermute x4, starting transfers between devices, from_tile(): return lax.ppermute(block, 'space', route)  7.39 us
    pallas_call x1, Pallas kernels, pack(): pl.pallas_call(pack_kernel, out_shape=(jax.ShapeDtypeStruct((SX, PAIRS +...  4.36 us
    ppermute x3, starting transfers between devices, shards(): lax.ppermute(sent[d], 'level', [(g, (g + d) % level_count) for g in range...  4.05 us
  transfers between devices with their start and end apart: 9, of which 5 were waited for; matrix products, arithmetic and copies ran while one was open for 5% of the time, Pallas kernels for 0%

profile of v2, /device:TPU:0, one launch (start us, length us, event | category | flops | bytes accessed | tf_op | source)
XLA Modules:
  0.0 104.5 jit_solution(16150572133940930594)
XLA Ops:
  0.0 4.4 %pack.1 = (bf16[16,17,2,16,128]{4,3,2,1,0:T(8,128)(2,1)}, bf16[17,2,16,128]{3,2,1,0:T(8,128)(2,1)}, bf16[17,2,16,128]{3,2,1,0:T(8,128)(2,1)}, bf16[16,16,128]{2,1,0:T(8,128)(2,1)}, bf16[16,16,128]{2,1,0:T(8,128)(2,1)}) custom-call(s32[3,16]{1,0:T(4,128)} %coords.1, bf16[16,96,512]{2,1,0:T(8,128)(2,1)} %features.1, s32[16,512]{1,0:T(8,128)} %occupancy.1, ...), custom_call_target="tpu_custom_call" | custom-call | tf_op jit(solution)/shard_map/pack/pallas_call | solution.py:84
  4.4 0.0 collective-permute-start
  4.4 1.7 %collective-permute-start.1 = (bf16[16,16,128]{2,1,0:T(8,128)(2,1)}, bf16[16,16,128]{2,1,0:T(8,128)(2,1)S(1)}, u32[]{:S(2)}, u32[]{:S(2)}) collective-permute-start(bf16[16,16,128]{2,1,0:T(8,128)(2,1)} %get-tuple-element.65), channel_id=1, source_target_pairs={{1,0},{2,1},{3,2},{0,3},{5,4},{6,5},{7,6},{4,7},{9,8},{10,9},{11,1... | collective-permute-start | bytes 196616 | tf_op jit(solution)/shard_map/ppermute | solution.py:368
  6.1 2.2 %collective-permute-done.y_low = bf16[16,16,128]{2,1,0:T(8,128)(2,1)S(1)} collective-permute-done((bf16[16,16,128]{2,1,0:T(8,128)(2,1)}, bf16[16,16,128]{2,1,0:T(8,128)(2,1)S(1)}, u32[]{:S(2)}, u32[]{:S(2)}) %collective-permute-start) | collective-permute-done | bytes 65568 | tf_op jit(solution)/shard_map/ppermute | solution.py:368
  8.3 0.6 fusion.1
  8.9 0.0 collective-permute-done.1.y_high
  8.9 0.6 fusion
  9.5 3.3 %collective-permute-start.2 = (bf16[17,2,16,128]{3,2,1,0:T(8,128)(2,1)}, bf16[17,2,16,128]{3,2,1,0:T(8,128)(2,1)S(1)}, u32[]{:S(2)}, u32[]{:S(2)}) collective-permute-start(bf16[17,2,16,128]{3,2,1,0:T(8,128)(2,1)} %get-tuple-element.76), channel_id=1, source_target_pairs={{28,0},{29,1},{30,2},{31,3},{0,4},{1,5},{2,6},{3,7},{4,8},{5,9},{6... | collective-permute-start | bytes 417800 | tf_op jit(solution)/shard_map/ppermute | solution.py:368
  12.8 2.4 %collective-permute-start.3 = (bf16[17,2,16,128]{3,2,1,0:T(8,128)(2,1)}, bf16[17,2,16,128]{3,2,1,0:T(8,128)(2,1)S(1)}, u32[]{:S(2)}, u32[]{:S(2)}) collective-permute-start(bf16[17,2,16,128]{3,2,1,0:T(8,128)(2,1)} %get-tuple-element.75), channel_id=1, source_target_pairs={{4,0},{5,1},{6,2},{7,3},{8,4},{9,5},{10,6},{11,7},{12,8},{13,9},{1... | collective-permute-start | bytes 417800 | tf_op jit(solution)/shard_map/ppermute | solution.py:368
  15.2 4.8 %collective-permute-done.2.x_low = bf16[17,2,16,128]{3,2,1,0:T(8,128)(2,1)S(1)} collective-permute-done((bf16[17,2,16,128]{3,2,1,0:T(8,128)(2,1)}, bf16[17,2,16,128]{3,2,1,0:T(8,128)(2,1)S(1)}, u32[]{:S(2)}, u32[]{:S(2)}) %collective-permute-start.2) | collective-permute-done | bytes 139296 | tf_op jit(solution)/shard_map/ppermute | solution.py:368
  20.0 2.9 %collective-permute-done.3.x_high = bf16[17,2,16,128]{3,2,1,0:T(8,128)(2,1)S(1)} collective-permute-done((bf16[17,2,16,128]{3,2,1,0:T(8,128)(2,1)}, bf16[17,2,16,128]{3,2,1,0:T(8,128)(2,1)S(1)}, u32[]{:S(2)}, u32[]{:S(2)}) %collective-permute-start.3) | collective-permute-done | bytes 139296 | tf_op jit(solution)/shard_map/ppermute | solution.py:368
  22.9 0.0 copy-done.3
  22.9 0.0 copy-done.4
  22.9 0.0 copy-done.6
  22.9 0.6 copy-done.7
  23.5 19.9 %conv.1 = (f32[16,256,256]{2,1,0:T(8,128)}, f32[128,256]{1,0:T(8,128)}) custom-call(bf16[16,17,2,16,128]{4,3,2,1,0:T(8,128)(2,1)} %get-tuple-element.62.act, bf16[17,2,16,128]{3,2,1,0:T(8,128)(2,1)} %copy-done.6, bf16[17,2,16,128]{3,2,1,0:T(8,128)(2,1)} %copy-done.7, bf16[16,16,128]{2,1,0:T(8,128)(2,1)} %copy-done.3, bf16[16,16,128]{2,1,0:T(8,128)(2,1)} %copy-done.4, ...), custom_call_target="tpu_custom_call" | custom-call | tf_op jit(solution)/shard_map/conv/pallas_call | solution.py:189
  43.5 1.7 %copy.16 = f32[128,1,256]{2,1,0:T(1,128)} copy(f32[128,1,256]{2,0,1:T(8,128)} %bitcast.41) | data formatting | bytes 262144 | tf_op jit(solution)/shard_map/all_to_all | solution.py:344
  45.2 8.9 %all-to-all-start = ((f32[128,1,256]{2,1,0:T(1,128)}), f32[128,1,256]{2,1,0:T(1,128)S(1)}, u32[]{:S(2)}, u32[]{:S(2)}) async-start(f32[128,1,256]{2,1,0:T(1,128)} %copy.16), calls=%async_computation | async-start | bytes 262144 | tf_op jit(solution)/shard_map/all_to_all | solution.py:344
  54.1 0.0 copy-done.12
  54.1 0.6 copy.17.owners
  54.7 0.0 copy-done.10
  54.7 0.0 copy-done.11
  54.7 0.6 pad_bitcast_fusion
  55.3 8.2 %all-to-all-done = f32[128,1,256]{2,1,0:T(1,128)S(1)} async-done(((f32[128,1,256]{2,1,0:T(1,128)}), f32[128,1,256]{2,1,0:T(1,128)S(1)}, u32[]{:S(2)}, u32[]{:S(2)}) %all-to-all-start) | async-done | bytes 131104 | tf_op jit(solution)/shard_map/all_to_all | solution.py:344
  63.5 0.7 copy.26
  64.2 8.6 %section.1 = (bf16[4,2,192,512]{3,2,1,0:T(8,128)(2,1)}, f32[128,512]{1,0:T(8,128)}) custom-call(f32[16,256,256]{2,1,0:T(8,128)} %get-tuple-element.67.conv, bf16[16,17,2,16,128]{4,3,2,1,0:T(8,128)(2,1)} %get-tuple-element.62.act, f32[128,256]{1,0:T(8,128)} %bitcast.39, f32[1,128]{1,0:T(1,128)} %get-tuple-element.80.gain, f32[1,128]{1,0:T(1,128)} %get-tuple-element.79.shift, ...), custom_call_target="tpu_custom_call" | custom-call | tf_op jit(solution)/shard_map/section/pallas_call | solution.py:295
  72.8 2.3 %slice_bitcast_fusion = (bf16[2,192,512]{2,1,0:T(8,128)(2,1)S(1)}, bf16[2,192,512]{2,1,0:T(8,128)(2,1)S(1)}, bf16[2,192,512]{2,1,0:T(8,128)(2,1)S(1)}, bf16[2,192,512]{2,1,0:T(8,128)(2,1)}) fusion(bf16[4,2,192,512]{3,2,1,0:T(8,128)(2,1)} %get-tuple-element.69), kind=kLoop, calls=%fused_computation | loop fusion | bytes 3145728 | tf_op jit(solution)/shard_map/squeeze | solution.py:395
  75.1 0.8 collective-permute-start.4
  75.9 1.5 %collective-permute-start.5 = (bf16[2,192,512]{2,1,0:T(8,128)(2,1)S(1)}, bf16[2,192,512]{2,1,0:T(8,128)(2,1)S(1)}, u32[]{:S(2)}, u32[]{:S(2)}) collective-permute-start(bf16[2,192,512]{2,1,0:T(8,128)(2,1)S(1)} %get-tuple-element.72), channel_id=1, source_target_pairs={{0,64},{32,96},{64,0},{96,32},{1,65},{33,97},{65,1},{97,33},{2,66}... | collective-permute-start | bytes 1179656 | tf_op jit(solution)/shard_map/ppermute | solution.py:395
  77.5 1.7 %collective-permute-start.6 = (bf16[2,192,512]{2,1,0:T(8,128)(2,1)S(1)}, bf16[2,192,512]{2,1,0:T(8,128)(2,1)S(1)}, u32[]{:S(2)}, u32[]{:S(2)}) collective-permute-start(bf16[2,192,512]{2,1,0:T(8,128)(2,1)S(1)} %get-tuple-element.71), channel_id=1, source_target_pairs={{0,96},{32,0},{64,32},{96,64},{1,97},{33,1},{65,33},{97,65},{2,98}... | collective-permute-start | bytes 1179656 | tf_op jit(solution)/shard_map/ppermute | solution.py:395
  79.2 0.0 copy-done.5
  79.2 1.0 copy.18
  80.1 5.5 %all-to-all-start.1 = ((f32[128,1,512]{2,1,0:T(1,128)}), f32[128,1,512]{2,1,0:T(1,128)S(1)}, u32[]{:S(2)}, u32[]{:S(2)}) async-start(f32[128,1,512]{2,1,0:T(1,128)} %copy.18), calls=%async_computation.1 | async-start | bytes 524288 | tf_op jit(solution)/shard_map/all_to_all | solution.py:344
  85.6 0.0 copy-done.8
  85.6 0.8 copy.19.gain
  86.4 0.0 copy-done.9
  86.4 0.8 copy.20.shift
  87.2 12.0 %all-to-all-done.1 = f32[128,1,512]{2,1,0:T(1,128)S(1)} async-done(((f32[128,1,512]{2,1,0:T(1,128)}), f32[128,1,512]{2,1,0:T(1,128)S(1)}, u32[]{:S(2)}, u32[]{:S(2)}) %all-to-all-start.1) | async-done | bytes 262176 | tf_op jit(solution)/shard_map/all_to_all | solution.py:344
  99.2 0.7 copy.25
  99.9 0.0 collective-permute-done.4.near
  99.9 0.0 collective-permute-done.5.far
  99.9 0.0 copy-start.1
  99.9 0.0 collective-permute-done.6.back
  99.9 0.0 copy-start.2
  99.9 0.7 copy-done
  100.7 0.1 copy-done.1
  100.8 0.2 copy-done.2
  101.0 3.5 %settle.1 = bf16[8,192,512]{2,1,0:T(8,128)(2,1)} custom-call(bf16[2,192,512]{2,1,0:T(8,128)(2,1)} %get-tuple-element.74.own, bf16[2,192,512]{2,1,0:T(8,128)(2,1)} %copy-done, bf16[2,192,512]{2,1,0:T(8,128)(2,1)} %copy-done.1, bf16[2,192,512]{2,1,0:T(8,128)(2,1)} %copy-done.2, f32[128,512]{1,0:T(8,128)} %bitcast.38, f32[192,1]{1,0:T(8,128)} %copy.19.gain, ...), custom_call_target="tpu_custom_call" | custom-call | tf_op jit(solution)/shard_map/settle/pallas_call | solution.py:333
  (13 shorter events, 0.0 us)
Async XLA Ops:
  4.4 3.9 %collective-permute-start = (bf16[16,16,128]{2,1,0:T(8,128)(2,1)}, bf16[16,16,128]{2,1,0:T(8,128)(2,1)S(1)}, u32[]{:S(2)}, u32[]{:S(2)}) collective-permute-start(bf16[16,16,128]{2,1,0:T(8,128)(2,1)} %get-tuple-element.64), channel_id=1, source_target_pairs={{3,0},{0,1},{1,2},{2,3},{7,4},{4,5},{5,6},{6,7},{11,8},{8,9},{9,10... | collective-permute-start | bytes 196616 | tf_op jit(solution)/shard_map/ppermute | solution.py:368
  4.4 4.5 %collective-permute-start.1 = (bf16[16,16,128]{2,1,0:T(8,128)(2,1)}, bf16[16,16,128]{2,1,0:T(8,128)(2,1)S(1)}, u32[]{:S(2)}, u32[]{:S(2)}) collective-permute-start(bf16[16,16,128]{2,1,0:T(8,128)(2,1)} %get-tuple-element.65), channel_id=1, source_target_pairs={{1,0},{2,1},{3,2},{0,3},{5,4},{6,5},{7,6},{4,7},{9,8},{10,9},{11,1... | collective-permute-start | bytes 196616 | tf_op jit(solution)/shard_map/ppermute | solution.py:368
  8.3 14.6 %copy-start.3 = (bf16[16,16,128]{2,1,0:T(8,128)(2,1)}, bf16[16,16,128]{2,1,0:T(8,128)(2,1)S(1)}, u32[]{:S(2)}) copy-start(bf16[16,16,128]{2,1,0:T(8,128)(2,1)S(1)} %collective-permute-done.y_low) | copy-start | bytes 196612
  8.9 14.0 %copy-start.4 = (bf16[16,16,128]{2,1,0:T(8,128)(2,1)}, bf16[16,16,128]{2,1,0:T(8,128)(2,1)S(1)}, u32[]{:S(2)}) copy-start(bf16[16,16,128]{2,1,0:T(8,128)(2,1)S(1)} %collective-permute-done.1.y_high) | copy-start | bytes 196612
  9.5 10.4 %collective-permute-start.2 = (bf16[17,2,16,128]{3,2,1,0:T(8,128)(2,1)}, bf16[17,2,16,128]{3,2,1,0:T(8,128)(2,1)S(1)}, u32[]{:S(2)}, u32[]{:S(2)}) collective-permute-start(bf16[17,2,16,128]{3,2,1,0:T(8,128)(2,1)} %get-tuple-element.76), channel_id=1, source_target_pairs={{28,0},{29,1},{30,2},{31,3},{0,4},{1,5},{2,6},{3,7},{4,8},{5,9},{6... | collective-permute-start | bytes 417800 | tf_op jit(solution)/shard_map/ppermute | solution.py:368
  12.8 10.1 %collective-permute-start.3 = (bf16[17,2,16,128]{3,2,1,0:T(8,128)(2,1)}, bf16[17,2,16,128]{3,2,1,0:T(8,128)(2,1)S(1)}, u32[]{:S(2)}, u32[]{:S(2)}) collective-permute-start(bf16[17,2,16,128]{3,2,1,0:T(8,128)(2,1)} %get-tuple-element.75), channel_id=1, source_target_pairs={{4,0},{5,1},{6,2},{7,3},{8,4},{9,5},{10,6},{11,7},{12,8},{13,9},{1... | collective-permute-start | bytes 417800 | tf_op jit(solution)/shard_map/ppermute | solution.py:368
  20.0 2.9 %copy-start.6 = (bf16[17,2,16,128]{3,2,1,0:T(8,128)(2,1)}, bf16[17,2,16,128]{3,2,1,0:T(8,128)(2,1)S(1)}, u32[]{:S(2)}) copy-start(bf16[17,2,16,128]{3,2,1,0:T(8,128)(2,1)S(1)} %collective-permute-done.2.x_low) | copy-start | bytes 417796
  22.9 0.7 copy-start.7
  23.5 30.5 %copy-start.12 = (s32[2,1]{0,1:T(1,128)S(1)}, s32[2,1]{0,1:T(1,128)}, u32[]{:S(2)}) copy-start(s32[2,1]{0,1:T(1,128)} %param.22) | copy-start | bytes 28
  23.5 31.2 %copy-start.10 = (f32[96]{0:T(128)S(1)}, f32[96]{0:T(128)}, u32[]{:S(2)}) copy-start(f32[96]{0:T(128)} %param.25) | copy-start | bytes 1156
  23.5 31.2 %copy-start.11 = (f32[96]{0:T(128)S(1)}, f32[96]{0:T(128)}, u32[]{:S(2)}) copy-start(f32[96]{0:T(128)} %param.24) | copy-start | bytes 1156
  45.2 18.3 %all-to-all-start = ((f32[128,1,256]{2,1,0:T(1,128)}), f32[128,1,256]{2,1,0:T(1,128)S(1)}, u32[]{:S(2)}, u32[]{:S(2)}) async-start(f32[128,1,256]{2,1,0:T(1,128)} %copy.16), calls=%async_computation | async-start | bytes 262144 | tf_op jit(solution)/shard_map/all_to_all | solution.py:344
  72.8 6.4 %copy-start.5 = (f32[128,512]{1,0:T(8,128)S(1)}, f32[128,512]{1,0:T(8,128)}, u32[]{:S(2)}) copy-start(f32[128,512]{1,0:T(8,128)} %get-tuple-element.70) | copy-start | bytes 786436
  72.8 12.8 %copy-start.8 = (f32[192]{0:T(256)S(1)}, f32[192]{0:T(256)}, u32[]{:S(2)}) copy-start(f32[192]{0:T(256)} %param.27) | copy-start | bytes 2308
  72.8 13.6 %copy-start.9 = (f32[192]{0:T(256)S(1)}, f32[192]{0:T(256)}, u32[]{:S(2)}) copy-start(f32[192]{0:T(256)} %param.28) | copy-start | bytes 2308
  75.1 24.8 %collective-permute-start.4 = (bf16[2,192,512]{2,1,0:T(8,128)(2,1)S(1)}, bf16[2,192,512]{2,1,0:T(8,128)(2,1)S(1)}, u32[]{:S(2)}, u32[]{:S(2)}) collective-permute-start(bf16[2,192,512]{2,1,0:T(8,128)(2,1)S(1)} %get-tuple-element.73), channel_id=1, source_target_pairs={{0,32},{32,64},{64,96},{96,0},{1,33},{33,65},{65,97},{97,1},{2,34}... | collective-permute-start | bytes 1179656 | tf_op jit(solution)/shard_map/ppermute | solution.py:395
  75.9 24.0 %collective-permute-start.5 = (bf16[2,192,512]{2,1,0:T(8,128)(2,1)S(1)}, bf16[2,192,512]{2,1,0:T(8,128)(2,1)S(1)}, u32[]{:S(2)}, u32[]{:S(2)}) collective-permute-start(bf16[2,192,512]{2,1,0:T(8,128)(2,1)S(1)} %get-tuple-element.72), channel_id=1, source_target_pairs={{0,64},{32,96},{64,0},{96,32},{1,65},{33,97},{65,1},{97,33},{2,66}... | collective-permute-start | bytes 1179656 | tf_op jit(solution)/shard_map/ppermute | solution.py:395
  77.5 22.5 %collective-permute-start.6 = (bf16[2,192,512]{2,1,0:T(8,128)(2,1)S(1)}, bf16[2,192,512]{2,1,0:T(8,128)(2,1)S(1)}, u32[]{:S(2)}, u32[]{:S(2)}) collective-permute-start(bf16[2,192,512]{2,1,0:T(8,128)(2,1)S(1)} %get-tuple-element.71), channel_id=1, source_target_pairs={{0,96},{32,0},{64,32},{96,64},{1,97},{33,1},{65,33},{97,65},{2,98}... | collective-permute-start | bytes 1179656 | tf_op jit(solution)/shard_map/ppermute | solution.py:395
  80.1 19.0 %all-to-all-start.1 = ((f32[128,1,512]{2,1,0:T(1,128)}), f32[128,1,512]{2,1,0:T(1,128)S(1)}, u32[]{:S(2)}, u32[]{:S(2)}) async-start(f32[128,1,512]{2,1,0:T(1,128)} %copy.18), calls=%async_computation.1 | async-start | bytes 524288 | tf_op jit(solution)/shard_map/all_to_all | solution.py:344
  99.9 0.8 copy-start
  99.9 0.9 copy-start.1
  99.9 1.1 %copy-start.2 = (bf16[2,192,512]{2,1,0:T(8,128)(2,1)}, bf16[2,192,512]{2,1,0:T(8,128)(2,1)S(1)}, u32[]{:S(2)}) copy-start(bf16[2,192,512]{2,1,0:T(8,128)(2,1)S(1)} %collective-permute-done.6.back) | copy-start | bytes 1179652

commit v3 on v2

v3 whole, which is shorter than its diff:
```python
import functools

import jax
import jax.numpy as jnp
import numpy as np
from jax import lax
from jax.experimental import pallas as pl
from jax.experimental.pallas import tpu as pltpu
from jax.sharding import PartitionSpec as P

BRICK = 8
TX = 2
TY = 4
TZ = 2
CAPC = 2
C = 96
C2 = 192
LANES = 128
SX = TX * BRICK
SY = TY * BRICK
SZ = TZ * BRICK
PAIRS = SY // 2
GRID_Y = 4
EMPTY = -3e38
epsilon = 1e-05

bf16 = jnp.bfloat16
f32 = jnp.float32
VMEM = pl.BlockSpec(memory_space=pltpu.VMEM)
SMEM = pl.BlockSpec(memory_space=pltpu.SMEM)


def params(mib=56):
    return pltpu.CompilerParams(vmem_limit_bytes=mib << 20)


def cell_chooser():
    chosen = np.zeros((256, 256), np.float32)
    for row in range(256):
        i2, j, c, half = row >> 7, (row >> 4) & 7, (row >> 3) & 1, row & 7
        z = 2 * half + c
        chosen[row, (z // 8) * 128 + i2 * 64 + j * 8 + z % 8] = 1
    return jnp.asarray(chosen, bf16)


def rows_dot(left, right):
    return lax.dot_general(left, right, (((1,), (1,)), ((), ())), preferred_element_type=f32)


def plain_dot(left, right):
    return lax.dot_general(left, right, (((1,), (0,)), ((), ())), preferred_element_type=f32)


def pack_kernel(parts, coords, features, occupancy, chooser, act, *rest):
    faces, order = rest[:-1], rest[-1]
    for n in range(16):
        place = ((coords[0, n] % TX) * TY + coords[1, n] % TY) * TZ + coords[2, n]
        order[place] = n
    picks = chooser[...]
    for tx in range(TX):
        for part, ty in enumerate(parts):
            halves = []
            for tz in range(TZ):
                n = order[(tx * TY + ty) * TZ + tz]
                gate = occupancy[pl.ds(n, 1), :].astype(f32)
                gate = jnp.broadcast_to(gate, (LANES, 512)).astype(bf16)
                halves.append(jnp.concatenate([features[n] * gate[:C], gate[C:]], axis=0))
            for h in range(4):
                lanes = slice(128 * h, 128 * h + 128)
                source = jnp.concatenate([half[:, lanes] for half in halves], axis=1)
                cells = rows_dot(picks, source).reshape(2, 4, 2, SZ, LANES).astype(bf16)
                x = 8 * tx + 2 * h
                act[x : x + 2, part] = cells
                if faces and ty == 0:
                    faces[0][x : x + 2] = cells[:, 0, 0]
                if faces and ty == TY - 1:
                    faces[1][x : x + 2] = cells[:, 3, 1]


def pack(coords, features, occupancy, chooser, parts, with_faces):
    side = jax.ShapeDtypeStruct((SX, SZ, LANES), bf16)
    faces = (side, side) if with_faces else ()
    return pl.pallas_call(
        functools.partial(pack_kernel, parts),
        out_shape=(jax.ShapeDtypeStruct((SX, len(parts), 4, 2, SZ, LANES), bf16),) + faces,
        in_specs=[SMEM, VMEM, VMEM, VMEM],
        out_specs=(VMEM,) * (1 + len(faces)),
        scratch_shapes=[pltpu.SMEM((16,), jnp.int32)],
        compiler_params=params(12),
        name="pack",
    )(coords, features, occupancy, chooser)


def z_shifted(cells):
    shape = cells.shape[:-2]
    wide = cells.astype(f32).reshape(-1, 2, 8, LANES)
    even, odd = wide[:, 0], wide[:, 1]
    place = lax.broadcasted_iota(jnp.int32, odd.shape, 1)
    before = jnp.where(place == 0, 0.0, pltpu.roll(odd, 1, 1))
    after = jnp.where(place == 7, 0.0, pltpu.roll(even, 7, 1))
    low = jnp.stack([before, even], axis=1).reshape(*shape, SZ, LANES).astype(bf16)
    high = jnp.stack([odd, after], axis=1).reshape(*shape, SZ, LANES).astype(bf16)
    return low, high


def lane_spread():
    row = lax.broadcasted_iota(jnp.int32, (LANES, LANES), 0)
    return jnp.where(row == LANES - 1, 1.0, 0.0).astype(bf16)


def plane_of(outer, inner, x):
    return jnp.concatenate([outer[x, 0], inner[x, 0], inner[x, 1], outer[x, 1]], axis=0)


def put_columns(grid, slot, before, plane, after):
    for c, (first, middle, last) in enumerate(
        zip(z_triple(before), z_triple(plane), z_triple(after))
    ):
        grid[c, slot, 0, 0] = first
        grid[c, slot, 0:PAIRS, 1] = middle[:, 0]
        grid[c, slot, 1 : PAIRS + 1, 0] = middle[:, 1]
        grid[c, slot, PAIRS, 1] = last


def z_triple(cells):
    low, high = z_shifted(cells)
    return low, cells, high


def kept(value, inside):
    return value * jnp.where(inside, 1.0, 0.0).astype(bf16)


def planes_dot(grid, slot, count, taps):
    rows = count * PAIRS * SZ
    pieces = []
    for a in range(3):
        for c in range(3):
            for d in range(4):
                block = grid[c, pl.ds(slot + a, count), d // 2 : d // 2 + PAIRS, d % 2]
                pieces.append(block.reshape(rows, LANES))
    return plain_dot(jnp.concatenate(pieces, axis=1), taps[...])


def planes_mask(grid, slot, count):
    rows = count * PAIRS * SZ
    spread = lane_spread()
    even = grid[1, pl.ds(slot + 1, count), 0:PAIRS, 1].reshape(rows, LANES)
    odd = grid[1, pl.ds(slot + 1, count), 1 : PAIRS + 1, 0].reshape(rows, LANES)
    return jnp.concatenate([plain_dot(even, spread), plain_dot(odd, spread)], axis=1)


def folded(row):
    return row[:, :LANES] + row[:, LANES:]


MID = SX - 2
STEP = 2


def middle_kernel(outer, inner, y_before, y_after, weight, out, stats, taps, grid, masks):
    tile_y = lax.axis_index("space") % GRID_Y

    def fill(x, carry):
        before = kept(y_before[x], tile_y > 0)
        after = kept(y_after[x], tile_y < GRID_Y - 1)
        put_columns(grid, x, before, plane_of(outer, inner, x), after)
        return carry

    lax.fori_loop(0, SX, fill, 0)
    taps[...] = jnp.zeros(taps.shape, bf16)
    for a in range(3):
        for b in range(3):
            for c in range(3):
                for parity in range(2):
                    first = (a * 3 + c) * 512 + (b + parity) * LANES
                    taps[first : first + C, parity * LANES : parity * LANES + C] = weight[(a * 3 + b) * 3 + c].T

    def convolve(step, carry):
        total, count = carry
        x = step * STEP
        value = planes_dot(grid, x, STEP, taps)
        mask = planes_mask(grid, x, STEP)
        out[pl.ds(x, STEP)] = value.reshape(STEP, PAIRS * SZ, 2 * LANES)
        masks[pl.ds(x, STEP)] = mask.astype(bf16).reshape(STEP, PAIRS * SZ, 2 * LANES)
        total = total + jnp.sum(value * mask, axis=0, keepdims=True)
        return total, count + jnp.sum(mask, axis=0, keepdims=True)

    zero = jnp.zeros((1, 2 * LANES), f32)
    total, count = lax.fori_loop(0, MID // STEP, convolve, (zero, zero))
    count = folded(count)
    mean = folded(total) / jnp.maximum(count, 1.0)
    both = jnp.concatenate([mean, mean], axis=1)

    def spread_out(x, carry):
        gap = (out[x] - both) * masks[x].astype(f32)
        return carry + jnp.sum(gap * gap, axis=0, keepdims=True)

    square = folded(lax.fori_loop(0, MID, spread_out, zero))
    stats[...] = jnp.concatenate([mean, square, count, jnp.zeros((5, LANES), f32)], axis=0)


def middle(outer, inner, y_before, y_after, weight):
    return pl.pallas_call(
        middle_kernel,
        out_shape=(
            jax.ShapeDtypeStruct((MID, PAIRS * SZ, 2 * LANES), f32),
            jax.ShapeDtypeStruct((8, LANES), f32),
            jax.ShapeDtypeStruct((9 * 512, 2 * LANES), bf16),
        ),
        in_specs=[VMEM] * 5,
        out_specs=(VMEM,) * 3,
        scratch_shapes=[
            pltpu.VMEM((3, SX, PAIRS + 1, 2, SZ, LANES), bf16),
            pltpu.VMEM((MID, PAIRS * SZ, 2 * LANES), bf16),
        ],
        compiler_params=params(26),
        name="middle",
    )(outer, inner, y_before, y_after, weight)


def edge_kernel(outer, inner, y_before, y_after, x_before, x_after, taps, part, out, stats, grid):
    space = lax.axis_index("space")
    tile_x, tile_y = space // GRID_Y, space % GRID_Y
    last_x = lax.axis_size("space") // GRID_Y - 1
    for slot, x in zip((1, 2, 3, 4), (0, 1, SX - 2, SX - 1)):
        before = kept(y_before[x], tile_y > 0)
        after = kept(y_after[x], tile_y < GRID_Y - 1)
        put_columns(grid, slot, before, plane_of(outer, inner, x), after)
    for slot, halo, inside in ((0, x_before, tile_x > 0), (5, x_after, tile_x < last_x)):
        for c, cells in enumerate(z_triple(kept(halo[...], inside))):
            grid[c, slot] = cells.reshape(PAIRS + 1, 2, SZ, LANES)
    values, masks = [], []
    for index, slot in enumerate((0, 3)):
        value = planes_dot(grid, slot, 1, taps)
        out[index] = value
        values.append(value)
        masks.append(planes_mask(grid, slot, 1))
    value, mask = jnp.concatenate(values, axis=0), jnp.concatenate(masks, axis=0)
    count = folded(jnp.sum(mask, axis=0, keepdims=True))
    mean = folded(jnp.sum(value * mask, axis=0, keepdims=True)) / jnp.maximum(count, 1.0)
    gap = (value - jnp.concatenate([mean, mean], axis=1)) * mask
    square = folded(jnp.sum(gap * gap, axis=0, keepdims=True))
    mean0, square0, count0 = part[0:1], part[1:2], part[2:3]
    both = count + count0
    joint = (mean * count + mean0 * count0) / jnp.maximum(both, 1.0)
    square = square + square0 + count * (mean - joint) ** 2 + count0 * (mean0 - joint) ** 2
    lane = lax.broadcasted_iota(jnp.int32, (1, LANES), 1)
    row = jnp.concatenate([jnp.where(lane == LANES - 1, both, joint), square], axis=1)
    stats[...] = jnp.broadcast_to(row[None], stats.shape)


def edges(outer, inner, y_before, y_after, x_before, x_after, taps, part, devices):
    return pl.pallas_call(
        edge_kernel,
        out_shape=(
            jax.ShapeDtypeStruct((2, PAIRS * SZ, 2 * LANES), f32),
            jax.ShapeDtypeStruct((devices, 1, 2 * LANES), f32),
        ),
        in_specs=[VMEM] * 8,
        out_specs=(VMEM, VMEM),
        scratch_shapes=[pltpu.VMEM((3, 6, PAIRS + 1, 2, SZ, LANES), bf16)],
        compiler_params=params(20),
        name="edges",
    )(outer, inner, y_before, y_after, x_before, x_after, taps, part)


def joined(table, width):
    means, squares = table[:, :, :width], table[:, :, width:]
    counts = table[:, :, width - 1 : width]
    whole = jnp.sum(counts, axis=0)
    mean = jnp.sum(means * counts, axis=0) / whole
    gap = means - mean[None]
    return mean, jnp.sum(squares + counts * gap * gap, axis=0) / whole


def section_kernel(mid, edge, outer, inner, table, gain, shift, weight, owners, *rest):
    sent, (stats, taps, down, cover, lines) = rest[:4], rest[4:]
    mean, var = joined(table, LANES)
    lines[...] = jnp.zeros(lines.shape, f32)
    lines[0:1, :C] = gain[...]
    lines[1:2, :C] = shift[...]
    real = lax.broadcasted_iota(jnp.int32, (1, LANES), 1) < C
    scale = jnp.where(real, lines[0:1] / jnp.sqrt(var + epsilon), 0.0)
    mean = jnp.where(real, mean, 0.0)
    moved = lines[1:2]
    mean = jnp.concatenate([mean, mean], axis=1)
    scale = jnp.concatenate([scale, scale], axis=1)
    moved = jnp.concatenate([moved, moved], axis=1)
    taps[...] = jnp.zeros(taps.shape, bf16)
    for a in range(2):
        for b in range(2):
            for c in range(2):
                first = ((a * 2 + c) * 2 + b) * LANES
                taps[:C2, first : first + C] = weight[(a * 2 + b) * 2 + c]

    spread = lane_spread()
    total = count = jnp.zeros((1, 2 * LANES), f32)
    for X in range(SX // 2):
        pieces, covers = [], []
        for a in range(2):
            x = 2 * X + a
            conv = edge[0] if x == 0 else edge[1] if x == SX - 1 else mid[x - 1]
            plane = plane_of(outer, inner, x)
            even = plane[:, 0].reshape(PAIRS * SZ, LANES)
            odd = plane[:, 1].reshape(PAIRS * SZ, LANES)
            even_mask, odd_mask = plain_dot(even, spread), plain_dot(odd, spread)
            mask = jnp.concatenate([even_mask, odd_mask], axis=1)
            active = jnp.concatenate([even, odd], axis=1).astype(f32)
            normed = (conv - mean) * scale + moved
            section = active + mask * jnp.maximum(normed, 0.0)
            section = section.reshape(PAIRS, 2, 8, 2 * LANES)
            for c in range(2):
                pieces.append(section[:, c].reshape(PAIRS * 8, 2 * LANES).astype(bf16))
            both = jnp.maximum(even_mask, odd_mask).reshape(PAIRS, 2, 8, LANES)
            covers.append(jnp.maximum(both[:, 0], both[:, 1]).reshape(PAIRS * 8, LANES))
        value = rows_dot(jnp.concatenate(pieces, axis=1), taps[...])
        value = value.astype(bf16).astype(f32)
        covered = jnp.maximum(covers[0], covers[1])
        covered = jnp.concatenate([covered, covered], axis=1)
        down[X] = value
        cover[X] = covered
        total = total + jnp.sum(value * covered, axis=0, keepdims=True)
        count = count + jnp.sum(covered, axis=0, keepdims=True)

    zero = jnp.zeros((1, 2 * LANES), f32)
    mean2 = total / jnp.maximum(count, 1.0)

    def spread_out(X, carry):
        gap = (down[X] - mean2) * cover[X]
        return carry + jnp.sum(gap * gap, axis=0, keepdims=True)

    square = lax.fori_loop(0, SX // 2, spread_out, zero)
    wide_lane = lax.broadcasted_iota(jnp.int32, (1, 2 * LANES), 1)
    row = jnp.concatenate([jnp.where(wide_lane == 2 * LANES - 1, count, mean2), square], axis=1)
    stats[...] = jnp.broadcast_to(row[None], stats.shape)

    level = lax.axis_index("level")
    groups = lax.axis_size("level")
    unit = (
        lax.broadcasted_iota(jnp.int32, (C2, 2 * LANES), 0)
        == lax.broadcasted_iota(jnp.int32, (C2, 2 * LANES), 1)
    )
    unit = jnp.where(unit, 1.0, 0.0).astype(bf16)
    half = PAIRS // 2 * 8
    rows = []
    for q in range(2):
        value = down[:, q * half : (q + 1) * half].reshape(SX // 2 * half, 2 * LANES)
        covered = cover[:, q * half : (q + 1) * half].reshape(SX // 2 * half, 2 * LANES)
        coded = jnp.where(covered > 0, value, EMPTY).astype(bf16)
        rows.append(rows_dot(unit, coded).astype(bf16))
    first, second = owners[0, 0], owners[1, 0]
    for distance in range(4):
        target = (level + distance) % groups
        for k in range(CAPC):
            takes_first = (first == target) & (k == 0)
            takes_second = (second == target) & (jnp.where(first == second, 1, 0) == k)
            chosen = jnp.where(takes_first, rows[0], jnp.where(takes_second, rows[1], EMPTY))
            sent[distance][k] = chosen.astype(bf16)


def section(mid, edge, outer, inner, table, gain, shift, weight, owners):
    return pl.pallas_call(
        section_kernel,
        out_shape=(jax.ShapeDtypeStruct((CAPC, C2, 512), bf16),) * 4
        + (jax.ShapeDtypeStruct((table.shape[0], 1, 4 * LANES), f32),),
        in_specs=[VMEM] * 8 + [SMEM],
        out_specs=(VMEM,) * 5,
        scratch_shapes=[
            pltpu.VMEM((2 * LANES, 8 * LANES), bf16),
            pltpu.VMEM((SX // 2, PAIRS * 8, 2 * LANES), f32),
            pltpu.VMEM((SX // 2, PAIRS * 8, 2 * LANES), f32),
            pltpu.VMEM((8, LANES), f32),
        ],
        compiler_params=params(20),
        name="section",
    )(mid, edge, outer, inner, table, gain, shift, weight, owners)


def settle_kernel(own, near, far, back, table, gain, shift, out, lines):
    lines[...] = jnp.zeros(lines.shape, f32)
    mean, var = joined(table, 2 * LANES)
    lines[0:1] = mean
    lines[1:2] = var
    lines[2:3, :C2] = gain[...]
    lines[3:4, :C2] = shift[...]
    turned = lines[...].T[:C2]
    mean, moved = turned[:, 0:1], turned[:, 3:4]
    scale = turned[:, 2:3] / jnp.sqrt(turned[:, 1:2] + epsilon)
    level = lax.axis_index("level")
    groups = lax.axis_size("level")
    for distance, source in enumerate((own, near, far, back)):
        origin = (level + groups - distance) % groups
        for k in range(CAPC):
            value = source[k].astype(f32)
            normed = (value - mean) * scale + moved
            out[origin * CAPC + k] = jnp.maximum(normed, 0.0).astype(bf16)


def settle(own, near, far, back, table, gain, shift):
    return pl.pallas_call(
        settle_kernel,
        out_shape=jax.ShapeDtypeStruct((8, C2, 512), bf16),
        in_specs=[VMEM] * 7,
        out_specs=VMEM,
        scratch_shapes=[pltpu.VMEM((8, 2 * LANES), f32)],
        compiler_params=params(12),
        name="settle",
    )(own, near, far, back, table, gain, shift)


def to_all(rows):
    return lax.all_to_all(rows, ("level", "space"), 0, 0, tiled=True)


def shards(
    features,
    occupancy,
    brick_coords,
    coarse_owner,
    conv_weight,
    conv_gain,
    conv_shift,
    reduce_weight,
    down_gain,
    down_shift,
):
    space_count = lax.axis_size("space")
    level_count = lax.axis_size("level")
    grid_x = space_count // GRID_Y

    def from_tile(block, step_x, step_y):
        route = []
        for s in range(space_count):
            x, y = s // GRID_Y, s % GRID_Y
            route.append(((x + step_x) % grid_x * GRID_Y + (y + step_y) % GRID_Y, s))
        return lax.ppermute(block, "space", route)

    chooser = cell_chooser()
    outer, y_low, y_high = pack(brick_coords, features, occupancy, chooser, (0, TY - 1), True)
    y_before = from_tile(y_high, 0, -1)
    y_after = from_tile(y_low, 0, 1)
    (inner,) = pack(brick_coords, features, occupancy, chooser, (1, 2), False)
    tile_y = lax.axis_index("space") % GRID_Y
    from_below = (tile_y > 0).astype(bf16)
    from_above = (tile_y < GRID_Y - 1).astype(bf16)

    def face(x):
        return jnp.concatenate(
            [
                (y_before[x] * from_below)[None],
                outer[x, 0].reshape(8, SZ, LANES),
                inner[x].reshape(16, SZ, LANES),
                outer[x, 1].reshape(8, SZ, LANES),
                (y_after[x] * from_above)[None],
            ]
        )

    x_before = from_tile(face(SX - 1), -1, 0)
    x_after = from_tile(face(0), 1, 0)
    mid, part, taps = middle(outer, inner, y_before, y_after, conv_weight)
    edge, stats = edges(
        outer,
        inner,
        y_before,
        y_after,
        x_before,
        x_after,
        taps,
        part,
        space_count * level_count,
    )
    *sent, stats2 = section(
        mid,
        edge,
        outer,
        inner,
        to_all(stats),
        conv_gain[None],
        conv_shift[None],
        reduce_weight,
        coarse_owner,
    )
    arrived = [
        lax.ppermute(sent[d], "level", [(g, (g + d) % level_count) for g in range(level_count)])
        for d in range(1, level_count)
    ]
    return settle(sent[0], *arrived, to_all(stats2), down_gain[None], down_shift[None])


def solution(mesh):
    in_specs = (
        P(("level", "space"), None, None),
        P(("level", "space"), None),
        P(None, ("level", "space")),
        P(("level", "space"), None),
        P(),
        P(),
        P(),
        P(),
        P(),
        P(),
    )
    out_specs = P(("level", "space"), None, None)
    return jax.shard_map(shards, mesh=mesh, in_specs=in_specs, out_specs=out_specs, check_vma=False)
```

time: 106 us -> 83 us (0.78)
  waiting for transfers between devices: 30.1 us -> 9.82 us
  blocking collectives: 0 us -> 20.1 us
  Pallas kernels: 36.4 us -> 24.6 us
  local copies, waits for them, and re-layouts: 12.1 us -> 6 us
  starting transfers between devices: 25.8 us -> 20.9 us
    all_to_all x0 -> x1, blocking collectives: none -> 20.1 us  [to_all(): return lax.all_to_all(rows, ('level', 'space'), 0, 0, tiled=True)]
    all_to_all x2 -> x1, waiting for transfers between devices: 20.2 us -> 9.33 us  [to_all(): return lax.all_to_all(rows, ('level', 'space'), 0, 0, tiled=True)]
    pallas_call x3 -> x5, Pallas kernels: 32.9 us -> 22.1 us  [the longest x1 12.8 us: middle(): pl.pallas_call(middle_kernel, out_shape=(jax.ShapeDtypeStruct((MID, PAIRS...]
    ppermute x4, waiting for transfers between devices: 9.87 us -> 0.48 us  [from_tile(): return lax.ppermute(block, 'space', route)]
    all_to_all x2 -> x1, starting transfers between devices: 14.4 us -> 9.3 us  [to_all(): return lax.all_to_all(rows, ('level', 'space'), 0, 0, tiled=True)]
    all_to_all x2 -> x0, local copies, waits for them, and re-layouts: 2.67 us -> none  [to_all(): return lax.all_to_all(rows, ('level', 'space'), 0, 0, tiled=True)]
    squeeze x1 -> x0, local copies, waits for them, and re-layouts: 2.31 us -> none  [shards(): sent[d]]
    unnamed x29 -> x32, local copies, waits for them, and re-layouts: 3.76 us -> 5.98 us
  transfers between devices with their start and end apart: 9 -> 8, of which waited for: 5 -> 2; matrix products, arithmetic and copies ran while one was open for 5% -> 0% of each run, Pallas kernels for 0% -> 17%
where the time goes in v3:
time: 83 us; the launch traced here: 81.6 us
  Pallas kernels  24.6 us (30%)
  starting transfers between devices  20.9 us (25%)
  blocking collectives  20.1 us (24%)
  waiting for transfers between devices  9.82 us (12%)
  local copies, waits for them, and re-layouts  6 us (7%)
    all_to_all x1, blocking collectives, to_all(): return lax.all_to_all(rows, ('level', 'space'), 0, 0, tiled=True)  20.1 us
    pallas_call x1, Pallas kernels, middle(): pl.pallas_call(middle_kernel, out_shape=(jax.ShapeDtypeStruct((MID, PAIRS...  12.8 us
    all_to_all x1, waiting for transfers between devices, to_all(): return lax.all_to_all(rows, ('level', 'space'), 0, 0, tiled=True)  9.33 us
    all_to_all x1, starting transfers between devices, to_all(): return lax.all_to_all(rows, ('level', 'space'), 0, 0, tiled=True)  9.3 us
    ppermute x4, starting transfers between devices, from_tile(): return lax.ppermute(block, 'space', route)  7.52 us
    unnamed x32, local copies, waits for them, and re-layouts  5.98 us
    ppermute x3, starting transfers between devices, shards(): lax.ppermute(sent[d], 'level', [(g, (g + d) % level_count) for g in range...  4.12 us
    pallas_call x1, Pallas kernels, section(): pl.pallas_call(section_kernel, out_shape=(jax.ShapeDtypeStruct((CAPC, C2,...  4.11 us
  transfers between devices with their start and end apart: 8, of which 2 were waited for; matrix products, arithmetic and copies ran while one was open for 0% of the time, Pallas kernels for 17%

profile of v3, /device:TPU:0, one launch (start us, length us, event | category | flops | bytes accessed | tf_op | source)
XLA Modules:
  0.0 81.6 jit_solution(3783757124890624132)
XLA Ops:
  0.0 0.0 copy-start
  0.0 1.4 %copy-done = bf16[16,96,512]{2,1,0:T(8,128)(2,1)S(1)} copy-done((bf16[16,96,512]{2,1,0:T(8,128)(2,1)S(1)}, bf16[16,96,512]{2,1,0:T(8,128)(2,1)}, u32[]{:S(2)}) %copy-start) | copy-done | bytes 1572888
  1.4 0.0 copy-start.4
  1.4 0.9 %copy-done.4 = bf16[256,256]{1,0:T(8,128)(2,1)S(1)} copy-done((bf16[256,256]{1,0:T(8,128)(2,1)S(1)}, bf16[256,256]{1,0:T(8,128)(2,1)}, u32[]{:S(2)}) %copy-start.4) | copy-done | bytes 131096
  2.3 0.0 copy-start.6
  2.3 0.8 copy-done.6
  3.1 0.0 copy-start.7
  3.1 0.7 copy-done.7
  3.8 1.4 %pack.2 = (bf16[16,2,4,2,16,128]{5,4,3,2,1,0:T(8,128)(2,1)S(1)}, bf16[16,16,128]{2,1,0:T(8,128)(2,1)S(1)}, bf16[16,16,128]{2,1,0:T(8,128)(2,1)S(1)}) custom-call(s32[3,16]{1,0:T(4,128)S(1)} %copy-done.7, bf16[16,96,512]{2,1,0:T(8,128)(2,1)S(1)} %copy-done, s32[16,512]{1,0:T(8,128)S(1)} %copy-done.6, bf16[256,256]{1,0:T(8,128)(2,1)S(1)} %copy-done.4), custom_call_target="tpu_custom_call" | custom-call | tf_op jit(solution)/shard_map/pack/pallas_call | solution.py:83
  5.2 0.0 copy-start.3
  5.2 0.1 collective-permute-start
  5.3 1.7 %collective-permute-start.1 = (bf16[16,16,128]{2,1,0:T(8,128)(2,1)S(1)}, bf16[16,16,128]{2,1,0:T(8,128)(2,1)S(1)}, u32[]{:S(2)}, u32[]{:S(2)}) collective-permute-start(bf16[16,16,128]{2,1,0:T(8,128)(2,1)S(1)} %get-tuple-element.20), channel_id=1, source_target_pairs={{1,0},{2,1},{3,2},{0,3},{5,4},{6,5},{7,6},{4,7},{9,8},{10,9},{11,1... | collective-permute-start | bytes 196616 | tf_op jit(solution)/shard_map/ppermute | solution.py:437
  7.0 1.4 %pack.3.inner = bf16[16,2,4,2,16,128]{5,4,3,2,1,0:T(8,128)(2,1)S(1)} custom-call(s32[3,16]{1,0:T(4,128)S(1)} %copy-done.7, bf16[16,96,512]{2,1,0:T(8,128)(2,1)S(1)} %copy-done, s32[16,512]{1,0:T(8,128)S(1)} %copy-done.6, bf16[256,256]{1,0:T(8,128)(2,1)S(1)} %copy-done.4), custom_call_target="tpu_custom_call" | custom-call | tf_op jit(solution)/shard_map/pack/pallas_call | solution.py:83
  8.5 0.5 collective-permute-done.y_before
  9.0 0.0 collective-permute-done.1.y_after
  9.0 3.3 %collective-permute-start.2 = (bf16[34,16,128]{2,1,0:T(8,128)(2,1)S(1)}, bf16[34,16,128]{2,1,0:T(8,128)(2,1)S(1)}, u32[]{:S(2)}, u32[]{:S(2)}) collective-permute-start(bf16[34,16,128]{2,1,0:T(8,128)(2,1)S(1)} %get-tuple-element.38), channel_id=1, source_target_pairs={{28,0},{29,1},{30,2},{31,3},{0,4},{1,5},{2,6},{3,7},{4,8},{5,9},{6... | collective-permute-start | bytes 417800 | tf_op jit(solution)/shard_map/ppermute | solution.py:437
  12.4 2.4 %collective-permute-start.3 = (bf16[34,16,128]{2,1,0:T(8,128)(2,1)S(1)}, bf16[34,16,128]{2,1,0:T(8,128)(2,1)S(1)}, u32[]{:S(2)}, u32[]{:S(2)}) collective-permute-start(bf16[34,16,128]{2,1,0:T(8,128)(2,1)S(1)} %get-tuple-element.37), channel_id=1, source_target_pairs={{4,0},{5,1},{6,2},{7,3},{8,4},{9,5},{10,6},{11,7},{12,8},{13,9},{1... | collective-permute-start | bytes 417800 | tf_op jit(solution)/shard_map/ppermute | solution.py:437
  14.8 0.0 copy-done.3
  14.8 12.8 %middle.1 = (f32[14,256,256]{2,1,0:T(8,128)S(1)}, f32[8,128]{1,0:T(8,128)S(1)}, bf16[4608,256]{1,0:T(8,128)(2,1)S(1)}) custom-call(bf16[16,2,4,2,16,128]{5,4,3,2,1,0:T(8,128)(2,1)S(1)} %get-tuple-element.18.outer, bf16[16,2,4,2,16,128]{5,4,3,2,1,0:T(8,128)(2,1)S(1)} %pack.3.inner, bf16[16,16,128]{2,1,0:T(8,128)(2,1)S(1)} %collective-permute-done.y_before, ...), custom_call_target="tpu_custom_call" | custom-call | tf_op jit(solution)/shard_map/middle/pallas_call | solution.py:204
  27.6 0.0 copy-start.1
  27.6 0.0 collective-permute-done.2.x_before
  27.6 0.0 collective-permute-done.3.x_after
  27.6 0.0 copy-start.12
  27.6 0.0 copy-start.5
  27.6 0.0 copy-start.10
  27.6 0.0 copy-start.11
  27.6 2.4 %edges.1 = (f32[2,256,256]{2,1,0:T(8,128)S(1)}, f32[128,1,256]{2,1,0:T(1,128)}) custom-call(bf16[16,2,4,2,16,128]{5,4,3,2,1,0:T(8,128)(2,1)S(1)} %get-tuple-element.18.outer, bf16[16,2,4,2,16,128]{5,4,3,2,1,0:T(8,128)(2,1)S(1)} %pack.3.inner, bf16[16,16,128]{2,1,0:T(8,128)(2,1)S(1)} %collective-permute-done.y_before, ...), custom_call_target="tpu_custom_call" | custom-call | tf_op jit(solution)/shard_map/edges/pallas_call | solution.py:254
  30.0 0.0 copy-done.1
  30.1 9.3 %all-to-all-start = ((f32[128,1,256]{2,1,0:T(1,128)}), f32[128,1,256]{2,1,0:T(1,128)S(1)}, u32[]{:S(2)}, u32[]{:S(2)}) async-start(f32[128,1,256]{2,1,0:T(1,128)} %get-tuple-element.25), calls=%async_computation | async-start | bytes 262144 | tf_op jit(solution)/shard_map/all_to_all | solution.py:413
  39.4 0.0 copy-done.12
  39.4 0.1 copy.12.owners
  39.5 9.3 %all-to-all-done.table = f32[128,1,256]{2,1,0:T(1,128)S(1)} async-done(((f32[128,1,256]{2,1,0:T(1,128)}), f32[128,1,256]{2,1,0:T(1,128)S(1)}, u32[]{:S(2)}, u32[]{:S(2)}) %all-to-all-start) | async-done | bytes 131104 | tf_op jit(solution)/shard_map/all_to_all | solution.py:413
  48.8 0.0 copy-done.5
  48.8 0.0 copy-done.10
  48.8 0.0 copy-done.11
  48.8 0.0 copy-start.2
  48.8 2.0 %copy-done.2 = f32[14,256,256]{2,1,0:T(8,128)S(1)} copy-done((f32[14,256,256]{2,1,0:T(8,128)S(1)}, f32[14,256,256]{2,1,0:T(8,128)}, u32[]{:S(2)}) %copy-start.2) | copy-done | bytes 3670040
  50.8 4.1 %section.1 = (bf16[2,192,512]{2,1,0:T(8,128)(2,1)S(1)}, bf16[2,192,512]{2,1,0:T(8,128)(2,1)S(1)}, bf16[2,192,512]{2,1,0:T(8,128)(2,1)S(1)}, bf16[2,192,512]{2,1,0:T(8,128)(2,1)S(1)}, f32[128,1,512]{2,1,0:T(1,128)S(1)}) custom-call(f32[14,256,256]{2,1,0:T(8,128)S(1)} %copy-done.2, f32[2,256,256]{2,1,0:T(8,128)S(1)} %get-tuple-element.24.edge, ...), custom_call_target="tpu_custom_call" | custom-call | tf_op jit(solution)/shard_map/section/pallas_call | solution.py:363
  55.0 0.9 %collective-permute-start.4 = (bf16[2,192,512]{2,1,0:T(8,128)(2,1)S(1)}, bf16[2,192,512]{2,1,0:T(8,128)(2,1)S(1)}, u32[]{:S(2)}, u32[]{:S(2)}) collective-permute-start(bf16[2,192,512]{2,1,0:T(8,128)(2,1)S(1)} %get-tuple-element.27), channel_id=1, source_target_pairs={{0,32},{32,64},{64,96},{96,0},{1,33},{33,65},{65,97},{97,1},{2,34}... | collective-permute-start | bytes 1179656 | tf_op jit(solution)/shard_map/ppermute | solution.py:485
  55.9 1.5 %collective-permute-start.5 = (bf16[2,192,512]{2,1,0:T(8,128)(2,1)S(1)}, bf16[2,192,512]{2,1,0:T(8,128)(2,1)S(1)}, u32[]{:S(2)}, u32[]{:S(2)}) collective-permute-start(bf16[2,192,512]{2,1,0:T(8,128)(2,1)S(1)} %get-tuple-element.28), channel_id=1, source_target_pairs={{0,64},{32,96},{64,0},{96,32},{1,65},{33,97},{65,1},{97,33},{2,66}... | collective-permute-start | bytes 1179656 | tf_op jit(solution)/shard_map/ppermute | solution.py:485
  57.4 1.7 %collective-permute-start.6 = (bf16[2,192,512]{2,1,0:T(8,128)(2,1)S(1)}, bf16[2,192,512]{2,1,0:T(8,128)(2,1)S(1)}, u32[]{:S(2)}, u32[]{:S(2)}) collective-permute-start(bf16[2,192,512]{2,1,0:T(8,128)(2,1)S(1)} %get-tuple-element.29), channel_id=1, source_target_pairs={{0,96},{32,0},{64,32},{96,64},{1,97},{33,1},{65,33},{97,65},{2,98}... | collective-permute-start | bytes 1179656 | tf_op jit(solution)/shard_map/ppermute | solution.py:485
  59.1 20.1 %all_to_all.10.table = f32[128,1,512]{2,1,0:T(1,128)S(1)} all-to-all(f32[128,1,512]{2,1,0:T(1,128)S(1)} %get-tuple-element.30), channel_id=1, replica_groups=mesh['level'=4,'space'=32] {'level','space'}, dimensions={0} | all-to-all | bytes 524288 | tf_op jit(solution)/shard_map/all_to_all | solution.py:413
  79.1 0.0 collective-permute-done.4.near
  79.1 0.0 collective-permute-done.5.far
  79.1 0.0 collective-permute-done.6.back
  79.1 0.0 copy-done.8
  79.2 0.0 copy-done.9
  79.2 2.5 %settle.1 = bf16[8,192,512]{2,1,0:T(8,128)(2,1)} custom-call(bf16[2,192,512]{2,1,0:T(8,128)(2,1)S(1)} %get-tuple-element.26.own, bf16[2,192,512]{2,1,0:T(8,128)(2,1)S(1)} %collective-permute-done.4.near, bf16[2,192,512]{2,1,0:T(8,128)(2,1)S(1)} %collective-permute-done.5.far, bf16[2,192,512]{2,1,0:T(8,128)(2,1)S(1)} %collective-permute-done.6.back, ...), custom_call_target="tpu_custom_call" | custom-call | tf_op jit(solution)/shard_map/settle/pallas_call | solution.py:401
  (11 shorter events, 0.1 us)
Async XLA Ops:
  0.0 1.4 %copy-start = (bf16[16,96,512]{2,1,0:T(8,128)(2,1)S(1)}, bf16[16,96,512]{2,1,0:T(8,128)(2,1)}, u32[]{:S(2)}) copy-start(bf16[16,96,512]{2,1,0:T(8,128)(2,1)} %features.3) | copy-start | bytes 4718596
  1.4 0.9 %copy-start.4 = (bf16[256,256]{1,0:T(8,128)(2,1)S(1)}, bf16[256,256]{1,0:T(8,128)(2,1)}, u32[]{:S(2)}) copy-start(bf16[256,256]{1,0:T(8,128)(2,1)} %constant.21.clone.chooser) | copy-start | bytes 393220
  2.3 0.8 copy-start.6
  3.1 0.7 copy-start.7
  5.2 9.6 %copy-start.3 = (bf16[27,96,96]{2,1,0:T(8,128)(2,1)S(1)}, bf16[27,96,96]{2,1,0:T(8,128)(2,1)}, u32[]{:S(2)}) copy-start(bf16[27,96,96]{2,1,0:T(8,128)(2,1)} %weight.2) | copy-start | bytes 1492996
  5.2 3.8 %collective-permute-start = (bf16[16,16,128]{2,1,0:T(8,128)(2,1)S(1)}, bf16[16,16,128]{2,1,0:T(8,128)(2,1)S(1)}, u32[]{:S(2)}, u32[]{:S(2)}) collective-permute-start(bf16[16,16,128]{2,1,0:T(8,128)(2,1)S(1)} %get-tuple-element.19), channel_id=1, source_target_pairs={{3,0},{0,1},{1,2},{2,3},{7,4},{4,5},{5,6},{6,7},{11,8},{8,9},{9,10... | collective-permute-start | bytes 196616 | tf_op jit(solution)/shard_map/ppermute | solution.py:437
  5.3 3.8 %collective-permute-start.1 = (bf16[16,16,128]{2,1,0:T(8,128)(2,1)S(1)}, bf16[16,16,128]{2,1,0:T(8,128)(2,1)S(1)}, u32[]{:S(2)}, u32[]{:S(2)}) collective-permute-start(bf16[16,16,128]{2,1,0:T(8,128)(2,1)S(1)} %get-tuple-element.20), channel_id=1, source_target_pairs={{1,0},{2,1},{3,2},{0,3},{5,4},{6,5},{7,6},{4,7},{9,8},{10,9},{11,1... | collective-permute-start | bytes 196616 | tf_op jit(solution)/shard_map/ppermute | solution.py:437
  9.0 18.5 %collective-permute-start.2 = (bf16[34,16,128]{2,1,0:T(8,128)(2,1)S(1)}, bf16[34,16,128]{2,1,0:T(8,128)(2,1)S(1)}, u32[]{:S(2)}, u32[]{:S(2)}) collective-permute-start(bf16[34,16,128]{2,1,0:T(8,128)(2,1)S(1)} %get-tuple-element.38), channel_id=1, source_target_pairs={{28,0},{29,1},{30,2},{31,3},{0,4},{1,5},{2,6},{3,7},{4,8},{5,9},{6... | collective-permute-start | bytes 417800 | tf_op jit(solution)/shard_map/ppermute | solution.py:437
  12.4 15.2 %collective-permute-start.3 = (bf16[34,16,128]{2,1,0:T(8,128)(2,1)S(1)}, bf16[34,16,128]{2,1,0:T(8,128)(2,1)S(1)}, u32[]{:S(2)}, u32[]{:S(2)}) collective-permute-start(bf16[34,16,128]{2,1,0:T(8,128)(2,1)S(1)} %get-tuple-element.37), channel_id=1, source_target_pairs={{4,0},{5,1},{6,2},{7,3},{8,4},{9,5},{10,6},{11,7},{12,8},{13,9},{1... | collective-permute-start | bytes 417800 | tf_op jit(solution)/shard_map/ppermute | solution.py:437
  27.6 2.5 %copy-start.1 = (f32[14,256,256]{2,1,0:T(8,128)}, f32[14,256,256]{2,1,0:T(8,128)S(1)}, u32[]{:S(2)}) copy-start(f32[14,256,256]{2,1,0:T(8,128)S(1)} %get-tuple-element.21.mid) | copy-start | bytes 11010052
  27.6 11.8 %copy-start.12 = (s32[2,1]{0,1:T(1,128)S(1)}, s32[2,1]{0,1:T(1,128)}, u32[]{:S(2)}) copy-start(s32[2,1]{0,1:T(1,128)} %param.14) | copy-start | bytes 28
  27.6 21.2 %copy-start.5 = (bf16[8,192,96]{2,1,0:T(8,128)(2,1)S(1)}, bf16[8,192,96]{2,1,0:T(8,128)(2,1)}, u32[]{:S(2)}) copy-start(bf16[8,192,96]{2,1,0:T(8,128)(2,1)} %weight.3) | copy-start | bytes 884740
  27.6 21.2 %copy-start.10 = (f32[96]{0:T(128)S(1)}, f32[96]{0:T(128)}, u32[]{:S(2)}) copy-start(f32[96]{0:T(128)} %param.16) | copy-start | bytes 1156
  27.6 21.2 %copy-start.11 = (f32[96]{0:T(128)S(1)}, f32[96]{0:T(128)}, u32[]{:S(2)}) copy-start(f32[96]{0:T(128)} %param.17) | copy-start | bytes 1156
  30.1 18.7 %all-to-all-start = ((f32[128,1,256]{2,1,0:T(1,128)}), f32[128,1,256]{2,1,0:T(1,128)S(1)}, u32[]{:S(2)}, u32[]{:S(2)}) async-start(f32[128,1,256]{2,1,0:T(1,128)} %get-tuple-element.25), calls=%async_computation | async-start | bytes 262144 | tf_op jit(solution)/shard_map/all_to_all | solution.py:413
  48.8 2.0 %copy-start.2 = (f32[14,256,256]{2,1,0:T(8,128)S(1)}, f32[14,256,256]{2,1,0:T(8,128)}, u32[]{:S(2)}) copy-start(f32[14,256,256]{2,1,0:T(8,128)} %copy-done.1) | copy-start | bytes 11010052
  50.8 28.3 %copy-start.8 = (f32[192]{0:T(256)S(1)}, f32[192]{0:T(256)}, u32[]{:S(2)}) copy-start(f32[192]{0:T(256)} %param.19) | copy-start | bytes 2308
  50.8 28.3 %copy-start.9 = (f32[192]{0:T(256)S(1)}, f32[192]{0:T(256)}, u32[]{:S(2)}) copy-start(f32[192]{0:T(256)} %param.20) | copy-start | bytes 2308
  55.0 24.2 %collective-permute-start.4 = (bf16[2,192,512]{2,1,0:T(8,128)(2,1)S(1)}, bf16[2,192,512]{2,1,0:T(8,128)(2,1)S(1)}, u32[]{:S(2)}, u32[]{:S(2)}) collective-permute-start(bf16[2,192,512]{2,1,0:T(8,128)(2,1)S(1)} %get-tuple-element.27), channel_id=1, source_target_pairs={{0,32},{32,64},{64,96},{96,0},{1,33},{33,65},{65,97},{97,1},{2,34}... | collective-permute-start | bytes 1179656 | tf_op jit(solution)/shard_map/ppermute | solution.py:485
  55.9 23.3 %collective-permute-start.5 = (bf16[2,192,512]{2,1,0:T(8,128)(2,1)S(1)}, bf16[2,192,512]{2,1,0:T(8,128)(2,1)S(1)}, u32[]{:S(2)}, u32[]{:S(2)}) collective-permute-start(bf16[2,192,512]{2,1,0:T(8,128)(2,1)S(1)} %get-tuple-element.28), channel_id=1, source_target_pairs={{0,64},{32,96},{64,0},{96,32},{1,65},{33,97},{65,1},{97,33},{2,66}... | collective-permute-start | bytes 1179656 | tf_op jit(solution)/shard_map/ppermute | solution.py:485
  57.4 21.7 %collective-permute-start.6 = (bf16[2,192,512]{2,1,0:T(8,128)(2,1)S(1)}, bf16[2,192,512]{2,1,0:T(8,128)(2,1)S(1)}, u32[]{:S(2)}, u32[]{:S(2)}) collective-permute-start(bf16[2,192,512]{2,1,0:T(8,128)(2,1)S(1)} %get-tuple-element.29), channel_id=1, source_target_pairs={{0,96},{32,0},{64,32},{96,64},{1,97},{33,1},{65,33},{97,65},{2,98}... | collective-permute-start | bytes 1179656 | tf_op jit(solution)/shard_map/ppermute | solution.py:485

commit v4 on v3

--- a/solution.py
+++ b/solution.py
@@ -2,7 +2,6 @@
 
 import jax
 import jax.numpy as jnp
-import numpy as np
 from jax import lax
 from jax.experimental import pallas as pl
 from jax.experimental.pallas import tpu as pltpu
@@ -28,6 +27,7 @@
 f32 = jnp.float32
 VMEM = pl.BlockSpec(memory_space=pltpu.VMEM)
 SMEM = pl.BlockSpec(memory_space=pltpu.SMEM)
+HBM = pl.BlockSpec(memory_space=pltpu.HBM)
 
 
 def params(mib=56):
@@ -35,12 +35,11 @@
 
 
 def cell_chooser():
-    chosen = np.zeros((256, 256), np.float32)
-    for row in range(256):
-        i2, j, c, half = row >> 7, (row >> 4) & 7, (row >> 3) & 1, row & 7
-        z = 2 * half + c
-        chosen[row, (z // 8) * 128 + i2 * 64 + j * 8 + z % 8] = 1
-    return jnp.asarray(chosen, bf16)
+    row = lax.broadcasted_iota(jnp.int32, (256, 256), 0)
+    lane = lax.broadcasted_iota(jnp.int32, (256, 256), 1)
+    z = 2 * (row & 7) + ((row >> 3) & 1)
+    source = ((z >> 3) << 7) + ((row >> 4) << 3) + (z & 7)
+    return jnp.where(source == lane, 1.0, 0.0).astype(bf16)
 
 
 def rows_dot(left, right):
@@ -51,12 +50,11 @@
     return lax.dot_general(left, right, (((1,), (0,)), ((), ())), preferred_element_type=f32)
 
 
-def pack_kernel(parts, coords, features, occupancy, chooser, act, *rest):
-    faces, order = rest[:-1], rest[-1]
+def pack_bricks(parts, coords, features, occupancy, act, faces, order):
     for n in range(16):
         place = ((coords[0, n] % TX) * TY + coords[1, n] % TY) * TZ + coords[2, n]
         order[place] = n
-    picks = chooser[...]
+    picks = cell_chooser()
     for tx in range(TX):
         for part, ty in enumerate(parts):
             halves = []
@@ -77,18 +75,76 @@
                     faces[1][x : x + 2] = cells[:, 3, 1]
 
 
-def pack(coords, features, occupancy, chooser, parts, with_faces):
+def outer_kernel(coords, features, occupancy, act, y_low, y_high, order, places, bricks, gates, sems):
+    copies = [
+        pltpu.make_async_copy(coords, places, sems.at[0]),
+        pltpu.make_async_copy(occupancy, gates, sems.at[1]),
+        pltpu.make_async_copy(features, bricks, sems.at[2]),
+    ]
+    for copy in copies:
+        copy.start()
+    for copy in copies:
+        copy.wait()
+    pack_bricks((0, TY - 1), places, bricks, gates, act, (y_low, y_high), order)
+
+
+def inner_kernel(coords, features, occupancy, act, order):
+    pack_bricks((1, 2), coords, features, occupancy, act, (), order)
+
+
+ACT = jax.ShapeDtypeStruct((SX, 2, 4, 2, SZ, LANES), bf16)
+
+
+def pack_outer(coords, features, occupancy):
     side = jax.ShapeDtypeStruct((SX, SZ, LANES), bf16)
-    faces = (side, side) if with_faces else ()
-    return pl.pallas_call(
-        functools.partial(pack_kernel, parts),
-        out_shape=(jax.ShapeDtypeStruct((SX, len(parts), 4, 2, SZ, LANES), bf16),) + faces,
-        in_specs=[SMEM, VMEM, VMEM, VMEM],
-        out_specs=(VMEM,) * (1 + len(faces)),
+    arrays = [pltpu.with_memory_space_constraint(a, pltpu.HBM) for a in (coords, features, occupancy)]
+    return pl.pallas_call(
+        outer_kernel,
+        out_shape=(ACT, side, side),
+        in_specs=[HBM] * 3,
+        out_specs=(VMEM,) * 3,
+        scratch_shapes=[
+            pltpu.SMEM((16,), jnp.int32),
+            pltpu.SMEM((3, 16), jnp.int32),
+            pltpu.VMEM((16, C, 512), bf16),
+            pltpu.VMEM((16, 512), jnp.int32),
+            pltpu.SemaphoreType.DMA((3,)),
+        ],
+        compiler_params=params(12),
+        name="pack_outer",
+    )(*arrays)
+
+
+def pack_inner(coords, features, occupancy):
+    return pl.pallas_call(
+        inner_kernel,
+        out_shape=ACT,
+        in_specs=[SMEM, VMEM, VMEM],
+        out_specs=VMEM,
         scratch_shapes=[pltpu.SMEM((16,), jnp.int32)],
         compiler_params=params(12),
-        name="pack",
-    )(coords, features, occupancy, chooser)
+        name="pack_inner",
+    )(coords, features, occupancy)
+
+
+def face_kernel(outer, inner, y_before, y_after, low, high):
+    tile_y = lax.axis_index("space") % GRID_Y
+    for face, x in ((low, 0), (high, SX - 1)):
+        face[0] = kept(y_before[x], tile_y > 0)
+        face[1 : SY + 1] = plane_of(outer, inner, x).reshape(SY, SZ, LANES)
+        face[SY + 1] = kept(y_after[x], tile_y < GRID_Y - 1)
+
+
+def faces(outer, inner, y_before, y_after):
+    face = jax.ShapeDtypeStruct((SY + 2, SZ, LANES), bf16)
+    return pl.pallas_call(
+        face_kernel,
+        out_shape=(face, face),
+        in_specs=[VMEM] * 4,
+        out_specs=(VMEM, VMEM),
+        compiler_params=params(8),
+        name="faces",
+    )(outer, inner, y_before, y_after)
 
 
 def z_shifted(cells):
@@ -158,16 +214,29 @@
 STEP = 2
 
 
-def middle_kernel(outer, inner, y_before, y_after, weight, out, stats, taps, grid, masks):
+def merged(first, second):
+    (mean0, square0, count0), (mean1, square1, count1) = first, second
+    count = count0 + count1
+    mean = (mean0 * count0 + mean1 * count1) / jnp.maximum(count, 1.0)
+    square = square0 + square1 + count0 * (mean0 - mean) ** 2 + count1 * (mean1 - mean) ** 2
+    return mean, square, count
+
+
+def moments_of(value, mask):
+    count = folded(jnp.sum(mask, axis=0, keepdims=True))
+    mean = folded(jnp.sum(value * mask, axis=0, keepdims=True)) / jnp.maximum(count, 1.0)
+    gap = (value - jnp.concatenate([mean, mean], axis=1)) * mask
+    return mean, folded(jnp.sum(gap * gap, axis=0, keepdims=True)), count
+
+
+def middle_kernel(outer, inner, y_before, y_after, weight, out, stats, taps, grid):
     tile_y = lax.axis_index("space") % GRID_Y
 
-    def fill(x, carry):
+    def fill(x):
         before = kept(y_before[x], tile_y > 0)
         after = kept(y_after[x], tile_y < GRID_Y - 1)
         put_columns(grid, x, before, plane_of(outer, inner, x), after)
-        return carry
-
-    lax.fori_loop(0, SX, fill, 0)
+
     taps[...] = jnp.zeros(taps.shape, bf16)
     for a in range(3):
         for b in range(3):
@@ -175,51 +244,36 @@
                 for parity in range(2):
                     first = (a * 3 + c) * 512 + (b + parity) * LANES
                     taps[first : first + C, parity * LANES : parity * LANES + C] = weight[(a * 3 + b) * 3 + c].T
-
-    def convolve(step, carry):
-        total, count = carry
-        x = step * STEP
+    for x in range(STEP + 2):
+        fill(x)
+    zero = jnp.zeros((1, LANES), f32)
+    carry = (zero, zero, zero)
+    for x in range(0, MID, STEP):
+        for later in range(x + STEP + 2, min(x + 2 * STEP + 2, SX)):
+            fill(later)
         value = planes_dot(grid, x, STEP, taps)
-        mask = planes_mask(grid, x, STEP)
-        out[pl.ds(x, STEP)] = value.reshape(STEP, PAIRS * SZ, 2 * LANES)
-        masks[pl.ds(x, STEP)] = mask.astype(bf16).reshape(STEP, PAIRS * SZ, 2 * LANES)
-        total = total + jnp.sum(value * mask, axis=0, keepdims=True)
-        return total, count + jnp.sum(mask, axis=0, keepdims=True)
-
-    zero = jnp.zeros((1, 2 * LANES), f32)
-    total, count = lax.fori_loop(0, MID // STEP, convolve, (zero, zero))
-    count = folded(count)
-    mean = folded(total) / jnp.maximum(count, 1.0)
-    both = jnp.concatenate([mean, mean], axis=1)
-
-    def spread_out(x, carry):
-        gap = (out[x] - both) * masks[x].astype(f32)
-        return carry + jnp.sum(gap * gap, axis=0, keepdims=True)
-
-    square = folded(lax.fori_loop(0, MID, spread_out, zero))
-    stats[...] = jnp.concatenate([mean, square, count, jnp.zeros((5, LANES), f32)], axis=0)
+        out[x : x + STEP] = value.reshape(STEP, PAIRS * SZ, 2 * LANES)
+        carry = merged(carry, moments_of(value, planes_mask(grid, x, STEP)))
+    stats[...] = jnp.concatenate(list(carry) + [jnp.zeros((5, LANES), f32)], axis=0)
 
 
 def middle(outer, inner, y_before, y_after, weight):
     return pl.pallas_call(
         middle_kernel,
         out_shape=(
-            jax.ShapeDtypeStruct((MID, PAIRS * SZ, 2 * LANES), f32),
+            pltpu.VMEM((MID, PAIRS * SZ, 2 * LANES), f32),
             jax.ShapeDtypeStruct((8, LANES), f32),
             jax.ShapeDtypeStruct((9 * 512, 2 * LANES), bf16),
         ),
         in_specs=[VMEM] * 5,
         out_specs=(VMEM,) * 3,
-        scratch_shapes=[
-            pltpu.VMEM((3, SX, PAIRS + 1, 2, SZ, LANES), bf16),
-            pltpu.VMEM((MID, PAIRS * SZ, 2 * LANES), bf16),
-        ],
-        compiler_params=params(26),
+        scratch_shapes=[pltpu.VMEM((3, SX, PAIRS + 1, 2, SZ, LANES), bf16)],
+        compiler_params=params(24),
         name="middle",
     )(outer, inner, y_before, y_after, weight)
 
 
-def edge_kernel(outer, inner, y_before, y_after, x_before, x_after, taps, part, out, stats, grid):
+def edge_kernel(outer, inner, y_before, y_after, x_before, x_after, taps, part, owners, out, stats, grid):
     space = lax.axis_index("space")
     tile_x, tile_y = space // GRID_Y, space % GRID_Y
     last_x = lax.axis_size("space") // GRID_Y - 1
@@ -230,39 +284,33 @@
     for slot, halo, inside in ((0, x_before, tile_x > 0), (5, x_after, tile_x < last_x)):
         for c, cells in enumerate(z_triple(kept(halo[...], inside))):
             grid[c, slot] = cells.reshape(PAIRS + 1, 2, SZ, LANES)
-    values, masks = [], []
+    carry = (part[0:1], part[1:2], part[2:3])
     for index, slot in enumerate((0, 3)):
         value = planes_dot(grid, slot, 1, taps)
         out[index] = value
-        values.append(value)
-        masks.append(planes_mask(grid, slot, 1))
-    value, mask = jnp.concatenate(values, axis=0), jnp.concatenate(masks, axis=0)
-    count = folded(jnp.sum(mask, axis=0, keepdims=True))
-    mean = folded(jnp.sum(value * mask, axis=0, keepdims=True)) / jnp.maximum(count, 1.0)
-    gap = (value - jnp.concatenate([mean, mean], axis=1)) * mask
-    square = folded(jnp.sum(gap * gap, axis=0, keepdims=True))
-    mean0, square0, count0 = part[0:1], part[1:2], part[2:3]
-    both = count + count0
-    joint = (mean * count + mean0 * count0) / jnp.maximum(both, 1.0)
-    square = square + square0 + count * (mean - joint) ** 2 + count0 * (mean0 - joint) ** 2
+        carry = merged(carry, moments_of(value, planes_mask(grid, slot, 1)))
+    joint, square, both = carry
     lane = lax.broadcasted_iota(jnp.int32, (1, LANES), 1)
-    row = jnp.concatenate([jnp.where(lane == LANES - 1, both, joint), square], axis=1)
+    joint = jnp.where(lane == LANES - 1, both, joint)
+    for q in range(2):
+        joint = jnp.where(lane == C + q, owners[q, 0].astype(f32), joint)
+    row = jnp.concatenate([joint, square], axis=1)
     stats[...] = jnp.broadcast_to(row[None], stats.shape)
 
 
-def edges(outer, inner, y_before, y_after, x_before, x_after, taps, part, devices):
+def edges(outer, inner, y_before, y_after, x_before, x_after, taps, part, owners, devices):
     return pl.pallas_call(
         edge_kernel,
         out_shape=(
             jax.ShapeDtypeStruct((2, PAIRS * SZ, 2 * LANES), f32),
             jax.ShapeDtypeStruct((devices, 1, 2 * LANES), f32),
         ),
-        in_specs=[VMEM] * 8,
+        in_specs=[VMEM] * 8 + [SMEM],
         out_specs=(VMEM, VMEM),
         scratch_shapes=[pltpu.VMEM((3, 6, PAIRS + 1, 2, SZ, LANES), bf16)],
         compiler_params=params(20),
         name="edges",
-    )(outer, inner, y_before, y_after, x_before, x_after, taps, part)
+    )(outer, inner, y_before, y_after, x_before, x_after, taps, part, owners)
 
 
 def joined(table, width):
@@ -274,8 +322,14 @@
     return mean, jnp.sum(squares + counts * gap * gap, axis=0) / whole
 
 
-def section_kernel(mid, edge, outer, inner, table, gain, shift, weight, owners, *rest):
-    sent, (stats, taps, down, cover, lines) = rest[:4], rest[4:]
+def section_kernel(
+    mid, edge, outer, inner, table, gain, shift, weight, sent, names, stats, taps, down, cover, lines
+):
+    level, groups = lax.axis_index("level"), lax.axis_size("level")
+    for distance in range(4):
+        origin = (level + groups - distance) % groups
+        device = origin * lax.axis_size("space") + lax.axis_index("space")
+        names[distance] = table[device][:, :LANES]
     mean, var = joined(table, LANES)
     lines[...] = jnp.zeros(lines.shape, f32)
     lines[0:1, :C] = gain[...]
@@ -335,37 +389,29 @@
     row = jnp.concatenate([jnp.where(wide_lane == 2 * LANES - 1, count, mean2), square], axis=1)
     stats[...] = jnp.broadcast_to(row[None], stats.shape)
 
-    level = lax.axis_index("level")
-    groups = lax.axis_size("level")
     unit = (
         lax.broadcasted_iota(jnp.int32, (C2, 2 * LANES), 0)
         == lax.broadcasted_iota(jnp.int32, (C2, 2 * LANES), 1)
     )
     unit = jnp.where(unit, 1.0, 0.0).astype(bf16)
     half = PAIRS // 2 * 8
-    rows = []
     for q in range(2):
         value = down[:, q * half : (q + 1) * half].reshape(SX // 2 * half, 2 * LANES)
         covered = cover[:, q * half : (q + 1) * half].reshape(SX // 2 * half, 2 * LANES)
         coded = jnp.where(covered > 0, value, EMPTY).astype(bf16)
-        rows.append(rows_dot(unit, coded).astype(bf16))
-    first, second = owners[0, 0], owners[1, 0]
-    for distance in range(4):
-        target = (level + distance) % groups
-        for k in range(CAPC):
-            takes_first = (first == target) & (k == 0)
-            takes_second = (second == target) & (jnp.where(first == second, 1, 0) == k)
-            chosen = jnp.where(takes_first, rows[0], jnp.where(takes_second, rows[1], EMPTY))
-            sent[distance][k] = chosen.astype(bf16)
-
-
-def section(mid, edge, outer, inner, table, gain, shift, weight, owners):
+        sent[q] = rows_dot(unit, coded).astype(bf16)
+
+
+def section(mid, edge, outer, inner, table, gain, shift, weight, devices):
     return pl.pallas_call(
         section_kernel,
-        out_shape=(jax.ShapeDtypeStruct((CAPC, C2, 512), bf16),) * 4
-        + (jax.ShapeDtypeStruct((table.shape[0], 1, 4 * LANES), f32),),
-        in_specs=[VMEM] * 8 + [SMEM],
-        out_specs=(VMEM,) * 5,
+        out_shape=(
+            jax.ShapeDtypeStruct((2, C2, 512), bf16),
+            jax.ShapeDtypeStruct((4, 1, LANES), f32),
+            jax.ShapeDtypeStruct((devices, 1, 4 * LANES), f32),
+        ),
+        in_specs=[VMEM] * 8,
+        out_specs=(VMEM,) * 3,
         scratch_shapes=[
             pltpu.VMEM((2 * LANES, 8 * LANES), bf16),
             pltpu.VMEM((SX // 2, PAIRS * 8, 2 * LANES), f32),
@@ -374,11 +420,38 @@
         ],
         compiler_params=params(20),
         name="section",
-    )(mid, edge, outer, inner, table, gain, shift, weight, owners)
-
-
-def settle_kernel(own, near, far, back, table, gain, shift, out, lines):
+    )(mid, edge, outer, inner, table, gain, shift, weight)
+
+
+def merge_kernel(table, out):
+    width = 2 * LANES
+    means, squares = table[:, :, :width], table[:, :, width:]
+    counts = table[:, :, width - 1 : width]
+    whole = jnp.sum(counts, axis=0)
+    mean = jnp.sum(means * counts, axis=0) / jnp.maximum(whole, 1.0)
+    gap = means - mean[None]
+    square = jnp.sum(squares + counts * gap * gap, axis=0)
+    lane = lax.broadcasted_iota(jnp.int32, (1, width), 1)
+    out[:, :, :width] = jnp.where(lane == width - 1, whole, mean)[None]
+    out[:, :, width:] = square[None]
+
+
+def merge(table):
+    return pl.pallas_call(
+        merge_kernel,
+        out_shape=jax.ShapeDtypeStruct((1, 1, 4 * LANES), f32),
+        in_specs=[VMEM],
+        out_specs=VMEM,
+        compiler_params=params(4),
+        name="merge",
+    )(table)
+
+
+def settle_kernel(
+    own, near, far0, far1, back, names, row0, row1, row2, row3, gain, shift, out, lines, ready, sems
+):
     lines[...] = jnp.zeros(lines.shape, f32)
+    table = jnp.concatenate([row0[...], row1[...], row2[...], row3[...]], axis=0)
     mean, var = joined(table, 2 * LANES)
     lines[0:1] = mean
     lines[1:2] = var
@@ -389,28 +462,47 @@
     scale = turned[:, 2:3] / jnp.sqrt(turned[:, 1:2] + epsilon)
     level = lax.axis_index("level")
     groups = lax.axis_size("level")
-    for distance, source in enumerate((own, near, far, back)):
+    copies = []
+    sources = ((own, 0, own, 1), (near, 0, near, 1), (far0, 0, far1, 0), (back, 0, back, 1))
+    for distance, (first, first_at, second, second_at) in enumerate(sources):
         origin = (level + groups - distance) % groups
+        named = jnp.where(names[distance] == level.astype(f32), 1.0, 0.0)
+        takes0, takes1 = named[:, C : C + 1], named[:, C + 1 : C + 2]
+        value0 = jnp.maximum((first[first_at].astype(f32) - mean) * scale + moved, 0.0)
+        value1 = jnp.maximum((second[second_at].astype(f32) - mean) * scale + moved, 0.0)
+        chosen = (
+            jnp.where(takes0 > 0, value0, jnp.where(takes1 > 0, value1, 0.0)),
+            jnp.where(takes0 * takes1 > 0, value1, 0.0),
+        )
         for k in range(CAPC):
-            value = source[k].astype(f32)
-            normed = (value - mean) * scale + moved
-            out[origin * CAPC + k] = jnp.maximum(normed, 0.0).astype(bf16)
-
-
-def settle(own, near, far, back, table, gain, shift):
+            slot = distance * CAPC + k
+            ready[slot] = chosen[k].astype(bf16)
+            copies.append(
+                pltpu.make_async_copy(ready.at[slot], out.at[origin * CAPC + k], sems.at[slot])
+            )
+            copies[-1].start()
+    for copy in copies:
+        copy.wait()
+
+
+def settle(rows, names, tables, gain, shift):
     return pl.pallas_call(
         settle_kernel,
         out_shape=jax.ShapeDtypeStruct((8, C2, 512), bf16),
-        in_specs=[VMEM] * 7,
-        out_specs=VMEM,
-        scratch_shapes=[pltpu.VMEM((8, 2 * LANES), f32)],
+        in_specs=[VMEM] * 12,
+        out_specs=HBM,
+        scratch_shapes=[
+            pltpu.VMEM((8, 2 * LANES), f32),
+            pltpu.VMEM((8, C2, 512), bf16),
+            pltpu.SemaphoreType.DMA((8,)),
+        ],
         compiler_params=params(12),
         name="settle",
-    )(own, near, far, back, table, gain, shift)
-
-
-def to_all(rows):
-    return lax.all_to_all(rows, ("level", "space"), 0, 0, tiled=True)
+    )(*rows, names, *tables, gain, shift)
+
+
+def to_all(rows, axes):
+    return lax.all_to_all(rows, axes, 0, 0, tiled=True)
 
 
 def shards(
@@ -436,28 +528,13 @@
             route.append(((x + step_x) % grid_x * GRID_Y + (y + step_y) % GRID_Y, s))
         return lax.ppermute(block, "space", route)
 
-    chooser = cell_chooser()
-    outer, y_low, y_high = pack(brick_coords, features, occupancy, chooser, (0, TY - 1), True)
+    outer, y_low, y_high = pack_outer(brick_coords, features, occupancy)
     y_before = from_tile(y_high, 0, -1)
     y_after = from_tile(y_low, 0, 1)
-    (inner,) = pack(brick_coords, features, occupancy, chooser, (1, 2), False)
-    tile_y = lax.axis_index("space") % GRID_Y
-    from_below = (tile_y > 0).astype(bf16)
-    from_above = (tile_y < GRID_Y - 1).astype(bf16)
-
-    def face(x):
-        return jnp.concatenate(
-            [
-                (y_before[x] * from_below)[None],
-                outer[x, 0].reshape(8, SZ, LANES),
-                inner[x].reshape(16, SZ, LANES),
-                outer[x, 1].reshape(8, SZ, LANES),
-                (y_after[x] * from_above)[None],
-            ]
-        )
-
-    x_before = from_tile(face(SX - 1), -1, 0)
-    x_after = from_tile(face(0), 1, 0)
+    inner = pack_inner(brick_coords, features, occupancy)
+    x_low, x_high = faces(outer, inner, y_before, y_after)
+    x_before = from_tile(x_high, -1, 0)
+    x_after = from_tile(x_low, 1, 0)
     mid, part, taps = middle(outer, inner, y_before, y_after, conv_weight)
     edge, stats = edges(
         outer,
@@ -468,24 +545,35 @@
         x_after,
         taps,
         part,
+        coarse_owner,
         space_count * level_count,
     )
-    *sent, stats2 = section(
+    sent, names, stats2 = section(
         mid,
         edge,
         outer,
         inner,
-        to_all(stats),
+        to_all(stats, ("level", "space")),
         conv_gain[None],
         conv_shift[None],
         reduce_weight,
-        coarse_owner,
+        space_count,
     )
-    arrived = [
-        lax.ppermute(sent[d], "level", [(g, (g + d) % level_count) for g in range(level_count)])
-        for d in range(1, level_count)
-    ]
-    return settle(sent[0], *arrived, to_all(stats2), down_gain[None], down_shift[None])
+    def up_level(block, distance):
+        route = [(g, (g + distance) % level_count) for g in range(level_count)]
+        return lax.ppermute(block, "level", route)
+
+    near = up_level(sent, 1)
+    back = up_level(sent, -1)
+    table = to_all(stats2, "space")
+    near, back, table = lax.optimization_barrier((near, back, table))
+    here = merge(table)
+    far0 = up_level(near[:1], 1)
+    far1 = up_level(back[1:], -1)
+    tables = [here] + [up_level(here, d) for d in range(1, level_count)]
+    return settle(
+        (sent, near, far0, far1, back), names, tables, down_gain[None], down_shift[None]
+    )
 
 
 def solution(mesh):

time: 83 us -> 74.4 us (0.90); the launches traced: 81.6 us -> 74.2 us
  blocking collectives: 20.1 us -> 29.4 us
  waiting for transfers between devices: 9.82 us -> 4.16 us
  starting transfers between devices: 20.9 us -> 16.1 us
  local copies, waits for them, and re-layouts: 6 us -> 1.6 us
  Pallas kernels: 24.6 us -> 22.5 us
    all_to_all x1 -> x2, blocking collectives: 20.1 us -> 29.4 us  [to_all(): return lax.all_to_all(rows, axes, 0, 0, tiled=True)]
    all_to_all x1 -> x0, waiting for transfers between devices: 9.33 us -> none  [to_all(): return lax.all_to_all(rows, ('level', 'space'), 0, 0, tiled=True)]
    all_to_all x1 -> x0, starting transfers between devices: 9.3 us -> none  [to_all(): return lax.all_to_all(rows, ('level', 'space'), 0, 0, tiled=True)]
    ppermute x3 -> x7, starting transfers between devices: 4.12 us -> 8.53 us  [up_level(): return lax.ppermute(block, 'level', route)]
    unnamed x32 -> x21, local copies, waits for them, and re-layouts: 5.98 us -> 1.58 us
    ppermute x3 -> x7, waiting for transfers between devices: 0.01 us -> 4.15 us  [up_level(): return lax.ppermute(block, 'level', route)]
    pallas_call x4 -> x6, Pallas kernels: 19.7 us -> 18.1 us  [the longest x1 10.5 us: middle(): pl.pallas_call(middle_kernel, out_shape=(pltpu.VMEM((MID, PAIRS * SZ, 2 *...]
  transfers between devices with their start and end apart: 8 -> 11, of which waited for: 2 -> 2; matrix products, arithmetic and copies ran while one was open for 0% -> 0% of each run, Pallas kernels for 17% -> 16%
where the time goes in v4:
time: 74.4 us; the launch traced here: 74.2 us
  blocking collectives  29.4 us (40%)
  Pallas kernels  22.5 us (30%)
  starting transfers between devices  16.1 us (22%)
  waiting for transfers between devices  4.16 us (6%)
  local copies, waits for them, and re-layouts  1.6 us (2%)
    all_to_all x2, blocking collectives, to_all(): return lax.all_to_all(rows, axes, 0, 0, tiled=True)  29.4 us
    pallas_call x1, Pallas kernels, middle(): pl.pallas_call(middle_kernel, out_shape=(pltpu.VMEM((MID, PAIRS * SZ, 2 *...  10.5 us
    ppermute x7, starting transfers between devices, up_level(): return lax.ppermute(block, 'level', route)  8.53 us
    ppermute x4, starting transfers between devices, from_tile(): return lax.ppermute(block, 'space', route)  7.6 us
    ppermute x7, waiting for transfers between devices, up_level(): return lax.ppermute(block, 'level', route)  4.15 us
    pallas_call x1, Pallas kernels, section(): pl.pallas_call(section_kernel, out_shape=(jax.ShapeDtypeStruct((2, C2, 51...  3.62 us
    pallas_call x1, Pallas kernels, pack_outer(): pl.pallas_call(outer_kernel, out_shape=(ACT, side, side), in_specs=[HBM]...  2.31 us
    pallas_call x1, Pallas kernels, edges(): pl.pallas_call(edge_kernel, out_shape=(jax.ShapeDtypeStruct((2, PAIRS * S...  2.26 us
  transfers between devices with their start and end apart: 11, of which 2 were waited for; matrix products, arithmetic and copies ran while one was open for 0% of the time, Pallas kernels for 16%

profile of v4, /device:TPU:0, one launch (start us, length us, event | category | flops | bytes accessed | tf_op | source)
XLA Modules:
  0.0 74.2 jit_solution(7212849165943374648)
XLA Ops:
  0.0 2.3 %pack_outer.1 = (bf16[16,2,4,2,16,128]{5,4,3,2,1,0:T(8,128)(2,1)S(1)}, bf16[16,16,128]{2,1,0:T(8,128)(2,1)S(1)}, bf16[16,16,128]{2,1,0:T(8,128)(2,1)S(1)}) custom-call(s32[3,16]{1,0:T(4,128)} %coords.3, bf16[16,96,512]{2,1,0:T(8,128)(2,1)} %features.3, s32[16,512]{1,0:T(8,128)} %occupancy.3), custom_call_target="tpu_custom_call" | custom-call | tf_op jit(solution)/shard_map/pack_outer/pallas_call | solution.py:101
  2.3 0.1 collective-permute-start
  2.4 0.0 copy-start.1
  2.4 1.7 %collective-permute-start.1 = (bf16[16,16,128]{2,1,0:T(8,128)(2,1)S(1)}, bf16[16,16,128]{2,1,0:T(8,128)(2,1)S(1)}, u32[]{:S(2)}, u32[]{:S(2)}) collective-permute-start(bf16[16,16,128]{2,1,0:T(8,128)(2,1)S(1)} %get-tuple-element.23), channel_id=1, source_target_pairs={{1,0},{2,1},{3,2},{0,3},{5,4},{6,5},{7,6},{4,7},{9,8},{10,9},{11,1... | collective-permute-start | bytes 196616 | tf_op jit(solution)/shard_map/ppermute | solution.py:529
  4.1 0.0 copy-done
  4.1 0.8 %copy-done.3 = s32[16,512]{1,0:T(8,128)S(1)} copy-done((s32[16,512]{1,0:T(8,128)S(1)}, s32[16,512]{1,0:T(8,128)}, u32[]{:S(2)}) %copy-start.3) | copy-done | bytes 32792
  4.9 0.7 copy-done.4
  5.6 1.4 %pack_inner.1.inner = bf16[16,2,4,2,16,128]{5,4,3,2,1,0:T(8,128)(2,1)S(1)} custom-call(s32[3,16]{1,0:T(4,128)S(1)} %copy-done.4, bf16[16,96,512]{2,1,0:T(8,128)(2,1)S(1)} %copy-done, s32[16,512]{1,0:T(8,128)S(1)} %copy-done.3), custom_call_target="tpu_custom_call" | custom-call | tf_op jit(solution)/shard_map/pack_inner/pallas_call | solution.py:119
  7.0 0.0 collective-permute-done.y_before
  7.0 0.0 collective-permute-done.1.y_after
  7.1 3.3 %collective-permute-start.2 = (bf16[34,16,128]{2,1,0:T(8,128)(2,1)S(1)}, bf16[34,16,128]{2,1,0:T(8,128)(2,1)S(1)}, u32[]{:S(2)}, u32[]{:S(2)}) collective-permute-start(bf16[34,16,128]{2,1,0:T(8,128)(2,1)S(1)} %get-tuple-element.25), channel_id=1, source_target_pairs={{28,0},{29,1},{30,2},{31,3},{0,4},{1,5},{2,6},{3,7},{4,8},{5,9},{6... | collective-permute-start | bytes 417800 | tf_op jit(solution)/shard_map/ppermute | solution.py:529
  10.4 2.5 %collective-permute-start.3 = (bf16[34,16,128]{2,1,0:T(8,128)(2,1)S(1)}, bf16[34,16,128]{2,1,0:T(8,128)(2,1)S(1)}, u32[]{:S(2)}, u32[]{:S(2)}) collective-permute-start(bf16[34,16,128]{2,1,0:T(8,128)(2,1)S(1)} %get-tuple-element.26), channel_id=1, source_target_pairs={{4,0},{5,1},{6,2},{7,3},{8,4},{9,5},{10,6},{11,7},{12,8},{13,9},{1... | collective-permute-start | bytes 417800 | tf_op jit(solution)/shard_map/ppermute | solution.py:529
  12.9 0.0 copy-done.9
  12.9 0.1 copy.11.owners
  13.0 0.0 copy-done.1
  13.0 10.5 %middle.1 = (f32[14,256,256]{2,1,0:T(8,128)S(1)}, f32[8,128]{1,0:T(8,128)S(1)}, bf16[4608,256]{1,0:T(8,128)(2,1)S(1)}) custom-call(bf16[16,2,4,2,16,128]{5,4,3,2,1,0:T(8,128)(2,1)S(1)} %get-tuple-element.21.outer, bf16[16,2,4,2,16,128]{5,4,3,2,1,0:T(8,128)(2,1)S(1)} %pack_inner.1.inner, bf16[16,16,128]{2,1,0:T(8,128)(2,1)S(1)} %collective-permute-done.y_before, ...), custom_call_target="tpu_custom_call" | custom-call | tf_op jit(solution)/shard_map/middle/pallas_call | solution.py:261
  23.5 0.0 collective-permute-done.2.x_before
  23.5 0.0 collective-permute-done.3.x_after
  23.5 0.0 copy-start.2
  23.5 0.0 copy-start.7
  23.5 0.0 copy-start.8
  23.5 2.3 %edges.1 = (f32[2,256,256]{2,1,0:T(8,128)S(1)}, f32[128,1,256]{2,1,0:T(1,128)S(1)}) custom-call(bf16[16,2,4,2,16,128]{5,4,3,2,1,0:T(8,128)(2,1)S(1)} %get-tuple-element.21.outer, bf16[16,2,4,2,16,128]{5,4,3,2,1,0:T(8,128)(2,1)S(1)} %pack_inner.1.inner, bf16[16,16,128]{2,1,0:T(8,128)(2,1)S(1)} %collective-permute-done.y_before, ...), custom_call_target="tpu_custom_call" | custom-call | tf_op jit(solution)/shard_map/edges/pallas_call | solution.py:302
  25.8 18.4 %all_to_all.10.table = f32[128,1,256]{2,1,0:T(1,128)S(1)} all-to-all(f32[128,1,256]{2,1,0:T(1,128)S(1)} %get-tuple-element.30), channel_id=1, replica_groups=mesh['level'=4,'space'=32] {'level','space'}, dimensions={0} | all-to-all | bytes 262144 | tf_op jit(solution)/shard_map/all_to_all | solution.py:505
  44.3 0.0 copy-done.2
  44.3 0.0 copy-done.7
  44.3 0.0 copy-done.8
  44.3 0.0 copy-start.5
  44.3 0.0 copy-start.6
  44.3 3.6 %section.1 = (bf16[2,192,512]{2,1,0:T(8,128)(2,1)S(1)}, f32[4,1,128]{2,1,0:T(1,128)S(1)}, f32[32,1,512]{2,1,0:T(1,128)S(1)}) custom-call(f32[14,256,256]{2,1,0:T(8,128)S(1)} %get-tuple-element.24.mid, f32[2,256,256]{2,1,0:T(8,128)S(1)} %get-tuple-element.29.edge, bf16[16,2,4,2,16,128]{5,4,3,2,1,0:T(8,128)(2,1)S(1)} %get-tuple-element.21.outer, ...), custom_call_target="tpu_custom_call" | custom-call | tf_op jit(solution)/shard_map/section/pallas_call | solution.py:406
  47.9 1.0 %collective-permute-start.5 = (bf16[2,192,512]{2,1,0:T(8,128)(2,1)S(1)}, bf16[2,192,512]{2,1,0:T(8,128)(2,1)S(1)}, u32[]{:S(2)}, u32[]{:S(2)}) collective-permute-start(bf16[2,192,512]{2,1,0:T(8,128)(2,1)S(1)} %get-tuple-element.31.own), channel_id=1, source_target_pairs={{0,96},{32,0},{64,32},{96,64},{1,97},{33,1},{65,33},{97,65},{2,98}... | collective-permute-start | bytes 1179656 | tf_op jit(solution)/shard_map/ppermute | solution.py:564
  48.9 1.1 %collective-permute-start.4 = (bf16[2,192,512]{2,1,0:T(8,128)(2,1)S(1)}, bf16[2,192,512]{2,1,0:T(8,128)(2,1)S(1)}, u32[]{:S(2)}, u32[]{:S(2)}) collective-permute-start(bf16[2,192,512]{2,1,0:T(8,128)(2,1)S(1)} %get-tuple-element.31.own), channel_id=1, source_target_pairs={{0,32},{32,64},{64,96},{96,0},{1,33},{33,65},{65,97},{97,1},{2,34}... | collective-permute-start | bytes 1179656 | tf_op jit(solution)/shard_map/ppermute | solution.py:564
  50.0 11.0 %all_to_all.11.table = f32[32,1,512]{2,1,0:T(1,128)S(1)} all-to-all(f32[32,1,512]{2,1,0:T(1,128)S(1)} %get-tuple-element.32), channel_id=1, replica_groups=mesh['level'=4,'space'=32] {'space'}, dimensions={0} | all-to-all | bytes 131072 | tf_op jit(solution)/shard_map/all_to_all | solution.py:505
  61.0 0.0 collective-permute-done.5.back
  61.0 0.0 collective-permute-done.4.near
  61.1 2.2 %collective-permute-start.7 = (bf16[1,192,512]{2,1,0:T(8,128)(2,1)S(1)}, bf16[1,192,512]{2,1,0:T(8,128)(2,1)S(1)}, u32[]{:S(2)}, u32[]{:S(2)}) collective-permute-start(bf16[1,192,512]{2,1,0:T(8,128)(2,1)S(1)} %slice.7), channel_id=1, source_target_pairs={{0,96},{32,0},{64,32},{96,64},{1,97},{33,1},{65,33},{97,65},{2,98}... | collective-permute-start | bytes 589832 | tf_op jit(solution)/shard_map/ppermute | solution.py:564
  63.2 0.0 collective-permute-start.6
  63.2 0.2 merge.1.row0
  63.4 3.3 %collective-permute-start.10 = (f32[1,1,512]{2,1,0:T(1,128)S(1)}, f32[1,1,512]{2,1,0:T(1,128)S(1)}, u32[]{:S(2)}, u32[]{:S(2)}) collective-permute-start(f32[1,1,512]{2,1,0:T(1,128)S(1)} %merge.1.row0), channel_id=1, source_target_pairs={{0,96},{32,0},{64,32},{96,64},{1,97},{33,1},{65,33},{97,65},{2,98}... | collective-permute-start | bytes 6152 | tf_op jit(solution)/shard_map/ppermute | solution.py:564
  66.7 0.0 collective-permute-start.9
  66.7 0.9 %collective-permute-start.8 = (f32[1,1,512]{2,1,0:T(1,128)S(1)}, f32[1,1,512]{2,1,0:T(1,128)S(1)}, u32[]{:S(2)}, u32[]{:S(2)}) collective-permute-start(f32[1,1,512]{2,1,0:T(1,128)S(1)} %merge.1.row0), channel_id=1, source_target_pairs={{0,32},{32,64},{64,96},{96,0},{1,33},{33,65},{65,97},{97,1},{2,34}... | collective-permute-start | bytes 6152 | tf_op jit(solution)/shard_map/ppermute | solution.py:564
  67.7 0.5 collective-permute-done.10.row3
  68.1 3.7 %collective-permute-done.9.row2 = f32[1,1,512]{2,1,0:T(1,128)S(1)} collective-permute-done((f32[1,1,512]{2,1,0:T(1,128)S(1)}, f32[1,1,512]{2,1,0:T(1,128)S(1)}, u32[]{:S(2)}, u32[]{:S(2)}) %collective-permute-start.9) | collective-permute-done | bytes 2080 | tf_op jit(solution)/shard_map/ppermute | solution.py:564
  71.8 0.0 collective-permute-done.8.row1
  71.8 0.0 collective-permute-done.7.far1
  71.8 0.0 collective-permute-done.6.far0
  71.8 0.0 copy-done.5
  71.8 0.0 copy-done.6
  71.8 2.2 %settle.1 = bf16[8,192,512]{2,1,0:T(8,128)(2,1)} custom-call(bf16[2,192,512]{2,1,0:T(8,128)(2,1)S(1)} %get-tuple-element.31.own, bf16[2,192,512]{2,1,0:T(8,128)(2,1)S(1)} %collective-permute-done.4.near, bf16[1,192,512]{2,1,0:T(8,128)(2,1)S(1)} %collective-permute-done.6.far0, bf16[1,192,512]{2,1,0:T(8,128)(2,1)S(1)} %collective-permute-done.7.far1, ...), custom_call_target="tpu_custom_call" | custom-call | tf_op jit(solution)/shard_map/settle/pallas_call | solution.py:489
  (7 shorter events, 0.1 us)
Async XLA Ops:
  0.0 4.1 %copy-start = (bf16[16,96,512]{2,1,0:T(8,128)(2,1)S(1)}, bf16[16,96,512]{2,1,0:T(8,128)(2,1)}, u32[]{:S(2)}) copy-start(bf16[16,96,512]{2,1,0:T(8,128)(2,1)} %features.3) | copy-start | bytes 4718596
  2.3 4.7 %collective-permute-start = (bf16[16,16,128]{2,1,0:T(8,128)(2,1)S(1)}, bf16[16,16,128]{2,1,0:T(8,128)(2,1)S(1)}, u32[]{:S(2)}, u32[]{:S(2)}) collective-permute-start(bf16[16,16,128]{2,1,0:T(8,128)(2,1)S(1)} %get-tuple-element.22), channel_id=1, source_target_pairs={{3,0},{0,1},{1,2},{2,3},{7,4},{4,5},{5,6},{6,7},{11,8},{8,9},{9,10... | collective-permute-start | bytes 196616 | tf_op jit(solution)/shard_map/ppermute | solution.py:529
  2.4 10.6 %copy-start.1 = (bf16[27,96,96]{2,1,0:T(8,128)(2,1)S(1)}, bf16[27,96,96]{2,1,0:T(8,128)(2,1)}, u32[]{:S(2)}) copy-start(bf16[27,96,96]{2,1,0:T(8,128)(2,1)} %weight.2) | copy-start | bytes 1492996
  2.4 4.6 %collective-permute-start.1 = (bf16[16,16,128]{2,1,0:T(8,128)(2,1)S(1)}, bf16[16,16,128]{2,1,0:T(8,128)(2,1)S(1)}, u32[]{:S(2)}, u32[]{:S(2)}) collective-permute-start(bf16[16,16,128]{2,1,0:T(8,128)(2,1)S(1)} %get-tuple-element.23), channel_id=1, source_target_pairs={{1,0},{2,1},{3,2},{0,3},{5,4},{6,5},{7,6},{4,7},{9,8},{10,9},{11,1... | collective-permute-start | bytes 196616 | tf_op jit(solution)/shard_map/ppermute | solution.py:529
  4.1 0.8 %copy-start.3 = (s32[16,512]{1,0:T(8,128)S(1)}, s32[16,512]{1,0:T(8,128)}, u32[]{:S(2)}) copy-start(s32[16,512]{1,0:T(8,128)} %occupancy.3) | copy-start | bytes 98308
  4.9 0.7 copy-start.4
  5.6 7.3 %copy-start.9 = (s32[2,1]{0,1:T(1,128)S(1)}, s32[2,1]{0,1:T(1,128)}, u32[]{:S(2)}) copy-start(s32[2,1]{0,1:T(1,128)} %param.13) | copy-start | bytes 28
  7.1 16.4 %collective-permute-start.2 = (bf16[34,16,128]{2,1,0:T(8,128)(2,1)S(1)}, bf16[34,16,128]{2,1,0:T(8,128)(2,1)S(1)}, u32[]{:S(2)}, u32[]{:S(2)}) collective-permute-start(bf16[34,16,128]{2,1,0:T(8,128)(2,1)S(1)} %get-tuple-element.25), channel_id=1, source_target_pairs={{28,0},{29,1},{30,2},{31,3},{0,4},{1,5},{2,6},{3,7},{4,8},{5,9},{6... | collective-permute-start | bytes 417800 | tf_op jit(solution)/shard_map/ppermute | solution.py:529
  10.4 13.1 %collective-permute-start.3 = (bf16[34,16,128]{2,1,0:T(8,128)(2,1)S(1)}, bf16[34,16,128]{2,1,0:T(8,128)(2,1)S(1)}, u32[]{:S(2)}, u32[]{:S(2)}) collective-permute-start(bf16[34,16,128]{2,1,0:T(8,128)(2,1)S(1)} %get-tuple-element.26), channel_id=1, source_target_pairs={{4,0},{5,1},{6,2},{7,3},{8,4},{9,5},{10,6},{11,7},{12,8},{13,9},{1... | collective-permute-start | bytes 417800 | tf_op jit(solution)/shard_map/ppermute | solution.py:529
  23.5 20.8 %copy-start.2 = (bf16[8,192,96]{2,1,0:T(8,128)(2,1)S(1)}, bf16[8,192,96]{2,1,0:T(8,128)(2,1)}, u32[]{:S(2)}) copy-start(bf16[8,192,96]{2,1,0:T(8,128)(2,1)} %weight.3) | copy-start | bytes 884740
  23.5 20.7 %copy-start.7 = (f32[96]{0:T(128)S(1)}, f32[96]{0:T(128)}, u32[]{:S(2)}) copy-start(f32[96]{0:T(128)} %param.15) | copy-start | bytes 1156
  23.5 20.7 %copy-start.8 = (f32[96]{0:T(128)S(1)}, f32[96]{0:T(128)}, u32[]{:S(2)}) copy-start(f32[96]{0:T(128)} %param.16) | copy-start | bytes 1156
  44.3 27.5 %copy-start.5 = (f32[192]{0:T(256)S(1)}, f32[192]{0:T(256)}, u32[]{:S(2)}) copy-start(f32[192]{0:T(256)} %param.18) | copy-start | bytes 2308
  44.3 27.5 %copy-start.6 = (f32[192]{0:T(256)S(1)}, f32[192]{0:T(256)}, u32[]{:S(2)}) copy-start(f32[192]{0:T(256)} %param.19) | copy-start | bytes 2308
  47.9 13.1 %collective-permute-start.5 = (bf16[2,192,512]{2,1,0:T(8,128)(2,1)S(1)}, bf16[2,192,512]{2,1,0:T(8,128)(2,1)S(1)}, u32[]{:S(2)}, u32[]{:S(2)}) collective-permute-start(bf16[2,192,512]{2,1,0:T(8,128)(2,1)S(1)} %get-tuple-element.31.own), channel_id=1, source_target_pairs={{0,96},{32,0},{64,32},{96,64},{1,97},{33,1},{65,33},{97,65},{2,98}... | collective-permute-start | bytes 1179656 | tf_op jit(solution)/shard_map/ppermute | solution.py:564
  48.9 12.1 %collective-permute-start.4 = (bf16[2,192,512]{2,1,0:T(8,128)(2,1)S(1)}, bf16[2,192,512]{2,1,0:T(8,128)(2,1)S(1)}, u32[]{:S(2)}, u32[]{:S(2)}) collective-permute-start(bf16[2,192,512]{2,1,0:T(8,128)(2,1)S(1)} %get-tuple-element.31.own), channel_id=1, source_target_pairs={{0,32},{32,64},{64,96},{96,0},{1,33},{33,65},{65,97},{97,1},{2,34}... | collective-permute-start | bytes 1179656 | tf_op jit(solution)/shard_map/ppermute | solution.py:564
  61.1 10.7 %collective-permute-start.7 = (bf16[1,192,512]{2,1,0:T(8,128)(2,1)S(1)}, bf16[1,192,512]{2,1,0:T(8,128)(2,1)S(1)}, u32[]{:S(2)}, u32[]{:S(2)}) collective-permute-start(bf16[1,192,512]{2,1,0:T(8,128)(2,1)S(1)} %slice.7), channel_id=1, source_target_pairs={{0,96},{32,0},{64,32},{96,64},{1,97},{33,1},{65,33},{97,65},{2,98}... | collective-permute-start | bytes 589832 | tf_op jit(solution)/shard_map/ppermute | solution.py:564
  63.2 8.6 %collective-permute-start.6 = (bf16[1,192,512]{2,1,0:T(8,128)(2,1)S(1)}, bf16[1,192,512]{2,1,0:T(8,128)(2,1)S(1)}, u32[]{:S(2)}, u32[]{:S(2)}) collective-permute-start(bf16[1,192,512]{2,1,0:T(8,128)(2,1)S(1)} %slice.6), channel_id=1, source_target_pairs={{0,32},{32,64},{64,96},{96,0},{1,33},{33,65},{65,97},{97,1},{2,34}... | collective-permute-start | bytes 589832 | tf_op jit(solution)/shard_map/ppermute | solution.py:564
  63.4 4.7 %collective-permute-start.10 = (f32[1,1,512]{2,1,0:T(1,128)S(1)}, f32[1,1,512]{2,1,0:T(1,128)S(1)}, u32[]{:S(2)}, u32[]{:S(2)}) collective-permute-start(f32[1,1,512]{2,1,0:T(1,128)S(1)} %merge.1.row0), channel_id=1, source_target_pairs={{0,96},{32,0},{64,32},{96,64},{1,97},{33,1},{65,33},{97,65},{2,98}... | collective-permute-start | bytes 6152 | tf_op jit(solution)/shard_map/ppermute | solution.py:564
  66.7 5.1 %collective-permute-start.9 = (f32[1,1,512]{2,1,0:T(1,128)S(1)}, f32[1,1,512]{2,1,0:T(1,128)S(1)}, u32[]{:S(2)}, u32[]{:S(2)}) collective-permute-start(f32[1,1,512]{2,1,0:T(1,128)S(1)} %merge.1.row0), channel_id=1, source_target_pairs={{0,64},{32,96},{64,0},{96,32},{1,65},{33,97},{65,1},{97,33},{2,66}... | collective-permute-start | bytes 6152 | tf_op jit(solution)/shard_map/ppermute | solution.py:564
  66.7 5.1 %collective-permute-start.8 = (f32[1,1,512]{2,1,0:T(1,128)S(1)}, f32[1,1,512]{2,1,0:T(1,128)S(1)}, u32[]{:S(2)}, u32[]{:S(2)}) collective-permute-start(f32[1,1,512]{2,1,0:T(1,128)S(1)} %merge.1.row0), channel_id=1, source_target_pairs={{0,32},{32,64},{64,96},{96,0},{1,33},{33,65},{65,97},{97,1},{2,34}... | collective-permute-start | bytes 6152 | tf_op jit(solution)/shard_map/ppermute | solution.py:564

commit v5 on v4

--- a/solution.py
+++ b/solution.py
@@ -19,6 +19,7 @@
 SY = TY * BRICK
 SZ = TZ * BRICK
 PAIRS = SY // 2
+WIDE = 4 * C
 GRID_Y = 4
 EMPTY = -3e38
 epsilon = 1e-05
@@ -75,11 +76,14 @@
                     faces[1][x : x + 2] = cells[:, 3, 1]
 
 
-def outer_kernel(coords, features, occupancy, act, y_low, y_high, order, places, bricks, gates, sems):
+def outer_kernel(
+    coords, features, occupancy, act, y_low, y_high, coords_out, gates, order, places, bricks, sems
+):
     copies = [
         pltpu.make_async_copy(coords, places, sems.at[0]),
         pltpu.make_async_copy(occupancy, gates, sems.at[1]),
         pltpu.make_async_copy(features, bricks, sems.at[2]),
+        pltpu.make_async_copy(coords, coords_out, sems.at[3]),
     ]
     for copy in copies:
         copy.start()
@@ -100,15 +104,20 @@
     arrays = [pltpu.with_memory_space_constraint(a, pltpu.HBM) for a in (coords, features, occupancy)]
     return pl.pallas_call(
         outer_kernel,
-        out_shape=(ACT, side, side),
+        out_shape=(
+            ACT,
+            side,
+            side,
+            jax.ShapeDtypeStruct(coords.shape, jnp.int32),
+            jax.ShapeDtypeStruct(occupancy.shape, jnp.int32),
+        ),
         in_specs=[HBM] * 3,
-        out_specs=(VMEM,) * 3,
+        out_specs=(VMEM,) * 5,
         scratch_shapes=[
             pltpu.SMEM((16,), jnp.int32),
             pltpu.SMEM((3, 16), jnp.int32),
             pltpu.VMEM((16, C, 512), bf16),
-            pltpu.VMEM((16, 512), jnp.int32),
-            pltpu.SemaphoreType.DMA((3,)),
+            pltpu.SemaphoreType.DMA((4,)),
         ],
         compiler_params=params(12),
         name="pack_outer",
@@ -147,16 +156,19 @@
     )(outer, inner, y_before, y_after)
 
 
-def z_shifted(cells):
-    shape = cells.shape[:-2]
-    wide = cells.astype(f32).reshape(-1, 2, 8, LANES)
+def window_forms(a, b, c, d):
+    a, b, c, d = (cells.astype(f32) for cells in (a, b, c, d))
+    lane = lax.broadcasted_iota(jnp.int32, a.shape, 2)
+    b, c, d = pltpu.roll(b, 96, 2), pltpu.roll(c, 64, 2), pltpu.roll(d, 32, 2)
+    wide = jnp.concatenate(
+        [jnp.where(lane < 96, a, b), jnp.where(lane < 64, b, c), jnp.where(lane < 32, c, d)], axis=2
+    ).reshape(PAIRS, 2, 8, WIDE)
     even, odd = wide[:, 0], wide[:, 1]
     place = lax.broadcasted_iota(jnp.int32, odd.shape, 1)
     before = jnp.where(place == 0, 0.0, pltpu.roll(odd, 1, 1))
     after = jnp.where(place == 7, 0.0, pltpu.roll(even, 7, 1))
-    low = jnp.stack([before, even], axis=1).reshape(*shape, SZ, LANES).astype(bf16)
-    high = jnp.stack([odd, after], axis=1).reshape(*shape, SZ, LANES).astype(bf16)
-    return low, high
+    pairs = ((before, even), (even, odd), (odd, after))
+    return [jnp.stack(pair, axis=1).reshape(PAIRS, SZ, WIDE).astype(bf16) for pair in pairs]
 
 
 def lane_spread():
@@ -168,41 +180,19 @@
     return jnp.concatenate([outer[x, 0], inner[x, 0], inner[x, 1], outer[x, 1]], axis=0)
 
 
-def put_columns(grid, slot, before, plane, after):
-    for c, (first, middle, last) in enumerate(
-        zip(z_triple(before), z_triple(plane), z_triple(after))
-    ):
-        grid[c, slot, 0, 0] = first
-        grid[c, slot, 0:PAIRS, 1] = middle[:, 0]
-        grid[c, slot, 1 : PAIRS + 1, 0] = middle[:, 1]
-        grid[c, slot, PAIRS, 1] = last
-
-
-def z_triple(cells):
-    low, high = z_shifted(cells)
-    return low, cells, high
-
-
 def kept(value, inside):
     return value * jnp.where(inside, 1.0, 0.0).astype(bf16)
 
 
-def planes_dot(grid, slot, count, taps):
-    rows = count * PAIRS * SZ
-    pieces = []
-    for a in range(3):
-        for c in range(3):
-            for d in range(4):
-                block = grid[c, pl.ds(slot + a, count), d // 2 : d // 2 + PAIRS, d % 2]
-                pieces.append(block.reshape(rows, LANES))
-    return plain_dot(jnp.concatenate(pieces, axis=1), taps[...])
-
-
-def planes_mask(grid, slot, count):
-    rows = count * PAIRS * SZ
+def planes_dot(pieces, taps):
+    rows = [piece.reshape(-1, WIDE) for piece in pieces]
+    return plain_dot(jnp.concatenate(rows, axis=1), taps)
+
+
+def planes_mask(planes):
     spread = lane_spread()
-    even = grid[1, pl.ds(slot + 1, count), 0:PAIRS, 1].reshape(rows, LANES)
-    odd = grid[1, pl.ds(slot + 1, count), 1 : PAIRS + 1, 0].reshape(rows, LANES)
+    even = jnp.concatenate([plane[:, 0].reshape(PAIRS * SZ, LANES) for plane in planes], axis=0)
+    odd = jnp.concatenate([plane[:, 1].reshape(PAIRS * SZ, LANES) for plane in planes], axis=0)
     return jnp.concatenate([plain_dot(even, spread), plain_dot(odd, spread)], axis=1)
 
 
@@ -229,31 +219,46 @@
     return mean, folded(jnp.sum(gap * gap, axis=0, keepdims=True)), count
 
 
-def middle_kernel(outer, inner, y_before, y_after, weight, out, stats, taps, grid):
+def middle_kernel(outer, inner, y_before, y_after, weight, out, partial, stats, taps, grid):
     tile_y = lax.axis_index("space") % GRID_Y
 
     def fill(x):
-        before = kept(y_before[x], tile_y > 0)
-        after = kept(y_after[x], tile_y < GRID_Y - 1)
-        put_columns(grid, x, before, plane_of(outer, inner, x), after)
+        before = kept(y_before[x], tile_y > 0)[None]
+        after = kept(y_after[x], tile_y < GRID_Y - 1)[None]
+        plane = plane_of(outer, inner, x)
+        even, odd = plane[:, 0], plane[:, 1]
+        forms = window_forms(
+            jnp.concatenate([before, odd[:-1]], axis=0),
+            even,
+            odd,
+            jnp.concatenate([even[1:], after], axis=0),
+        )
+        for c in range(3):
+            grid[c, x] = forms[c]
 
     taps[...] = jnp.zeros(taps.shape, bf16)
     for a in range(3):
         for b in range(3):
             for c in range(3):
                 for parity in range(2):
-                    first = (a * 3 + c) * 512 + (b + parity) * LANES
+                    first = (a * 3 + c) * WIDE + (b + parity) * C
                     taps[first : first + C, parity * LANES : parity * LANES + C] = weight[(a * 3 + b) * 3 + c].T
     for x in range(STEP + 2):
         fill(x)
+    pieces = [grid[c, a] for a in range(2) for c in range(3)]
+    partial[0] = planes_dot(pieces, taps[3 * WIDE :])
     zero = jnp.zeros((1, LANES), f32)
     carry = (zero, zero, zero)
     for x in range(0, MID, STEP):
         for later in range(x + STEP + 2, min(x + 2 * STEP + 2, SX)):
             fill(later)
-        value = planes_dot(grid, x, STEP, taps)
+        pieces = [grid[c, x + a : x + a + STEP] for a in range(3) for c in range(3)]
+        value = planes_dot(pieces, taps[...])
         out[x : x + STEP] = value.reshape(STEP, PAIRS * SZ, 2 * LANES)
-        carry = merged(carry, moments_of(value, planes_mask(grid, x, STEP)))
+        mask = planes_mask([plane_of(outer, inner, x + 1 + step) for step in range(STEP)])
+        carry = merged(carry, moments_of(value, mask))
+    pieces = [grid[c, SX - 2 + a] for a in range(2) for c in range(3)]
+    partial[1] = planes_dot(pieces, taps[: 6 * WIDE])
     stats[...] = jnp.concatenate(list(carry) + [jnp.zeros((5, LANES), f32)], axis=0)
 
 
@@ -262,33 +267,29 @@
         middle_kernel,
         out_shape=(
             pltpu.VMEM((MID, PAIRS * SZ, 2 * LANES), f32),
+            jax.ShapeDtypeStruct((2, PAIRS * SZ, 2 * LANES), f32),
             jax.ShapeDtypeStruct((8, LANES), f32),
-            jax.ShapeDtypeStruct((9 * 512, 2 * LANES), bf16),
+            jax.ShapeDtypeStruct((9 * WIDE, 2 * LANES), bf16),
         ),
         in_specs=[VMEM] * 5,
-        out_specs=(VMEM,) * 3,
-        scratch_shapes=[pltpu.VMEM((3, SX, PAIRS + 1, 2, SZ, LANES), bf16)],
-        compiler_params=params(24),
+        out_specs=(VMEM,) * 4,
+        scratch_shapes=[pltpu.VMEM((3, SX, PAIRS, SZ, WIDE), bf16)],
+        compiler_params=params(26),
         name="middle",
     )(outer, inner, y_before, y_after, weight)
 
 
-def edge_kernel(outer, inner, y_before, y_after, x_before, x_after, taps, part, owners, out, stats, grid):
-    space = lax.axis_index("space")
-    tile_x, tile_y = space // GRID_Y, space % GRID_Y
+def edge_kernel(outer, inner, x_before, x_after, partial, taps, part, owners, out, stats):
+    tile_x = lax.axis_index("space") // GRID_Y
     last_x = lax.axis_size("space") // GRID_Y - 1
-    for slot, x in zip((1, 2, 3, 4), (0, 1, SX - 2, SX - 1)):
-        before = kept(y_before[x], tile_y > 0)
-        after = kept(y_after[x], tile_y < GRID_Y - 1)
-        put_columns(grid, slot, before, plane_of(outer, inner, x), after)
-    for slot, halo, inside in ((0, x_before, tile_x > 0), (5, x_after, tile_x < last_x)):
-        for c, cells in enumerate(z_triple(kept(halo[...], inside))):
-            grid[c, slot] = cells.reshape(PAIRS + 1, 2, SZ, LANES)
     carry = (part[0:1], part[1:2], part[2:3])
-    for index, slot in enumerate((0, 3)):
-        value = planes_dot(grid, slot, 1, taps)
+    sides = ((x_before, tile_x > 0, 0, 0), (x_after, tile_x < last_x, 6 * WIDE, SX - 1))
+    for index, (halo, inside, first, x) in enumerate(sides):
+        cells = kept(halo[...], inside).reshape(PAIRS + 1, 2, SZ, LANES)
+        forms = window_forms(cells[:-1, 0], cells[:-1, 1], cells[1:, 0], cells[1:, 1])
+        value = partial[index] + planes_dot(forms, taps[first : first + 3 * WIDE])
         out[index] = value
-        carry = merged(carry, moments_of(value, planes_mask(grid, slot, 1)))
+        carry = merged(carry, moments_of(value, planes_mask([plane_of(outer, inner, x)])))
     joint, square, both = carry
     lane = lax.broadcasted_iota(jnp.int32, (1, LANES), 1)
     joint = jnp.where(lane == LANES - 1, both, joint)
@@ -298,19 +299,18 @@
     stats[...] = jnp.broadcast_to(row[None], stats.shape)
 
 
-def edges(outer, inner, y_before, y_after, x_before, x_after, taps, part, owners, devices):
+def edges(outer, inner, x_before, x_after, partial, taps, part, owners, devices):
     return pl.pallas_call(
         edge_kernel,
         out_shape=(
             jax.ShapeDtypeStruct((2, PAIRS * SZ, 2 * LANES), f32),
             jax.ShapeDtypeStruct((devices, 1, 2 * LANES), f32),
         ),
-        in_specs=[VMEM] * 8 + [SMEM],
+        in_specs=[VMEM] * 7 + [SMEM],
         out_specs=(VMEM, VMEM),
-        scratch_shapes=[pltpu.VMEM((3, 6, PAIRS + 1, 2, SZ, LANES), bf16)],
-        compiler_params=params(20),
+        compiler_params=params(16),
         name="edges",
-    )(outer, inner, y_before, y_after, x_before, x_after, taps, part, owners)
+    )(outer, inner, x_before, x_after, partial, taps, part, owners)
 
 
 def joined(table, width):
@@ -423,7 +423,7 @@
     )(mid, edge, outer, inner, table, gain, shift, weight)
 
 
-def merge_kernel(table, out):
+def merge_kernel(table, near, back, out, up, down):
     width = 2 * LANES
     means, squares = table[:, :, :width], table[:, :, width:]
     counts = table[:, :, width - 1 : width]
@@ -432,26 +432,40 @@
     gap = means - mean[None]
     square = jnp.sum(squares + counts * gap * gap, axis=0)
     lane = lax.broadcasted_iota(jnp.int32, (1, width), 1)
-    out[:, :, :width] = jnp.where(lane == width - 1, whole, mean)[None]
-    out[:, :, width:] = square[None]
-
-
-def merge(table):
+    row = jnp.concatenate([jnp.where(lane == width - 1, whole, mean), square], axis=1)
+    out[...] = row[None]
+    high = row.astype(bf16).astype(f32)
+    middle = (row - high).astype(bf16).astype(f32)
+    low = row - high - middle
+    rows = jnp.concatenate([high, middle, low, jnp.zeros((13, 2 * width), f32)], axis=0).astype(bf16)
+    for block, brick in ((up, near[0]), (down, back[1])):
+        block[:C2] = brick
+        block[C2:] = rows
+
+
+def merge(table, near, back):
+    block = jax.ShapeDtypeStruct((C2 + 16, 512), bf16)
     return pl.pallas_call(
         merge_kernel,
-        out_shape=jax.ShapeDtypeStruct((1, 1, 4 * LANES), f32),
-        in_specs=[VMEM],
-        out_specs=VMEM,
-        compiler_params=params(4),
+        out_shape=(jax.ShapeDtypeStruct((1, 1, 4 * LANES), f32), block, block),
+        in_specs=[VMEM] * 3,
+        out_specs=(VMEM,) * 3,
+        compiler_params=params(8),
         name="merge",
-    )(table)
+    )(table, near, back)
+
+
+def row_of(block):
+    rows = block[C2:].astype(f32)
+    return rows[0:1] + rows[1:2] + rows[2:3]
 
 
 def settle_kernel(
-    own, near, far0, far1, back, names, row0, row1, row2, row3, gain, shift, out, lines, ready, sems
+    own, near, far0, far1, back, names, row_here, row_far, gain, shift, out, lines, ready, sems
 ):
     lines[...] = jnp.zeros(lines.shape, f32)
-    table = jnp.concatenate([row0[...], row1[...], row2[...], row3[...]], axis=0)
+    rows = (row_here[0], row_of(far0), row_far[0], row_of(far1))
+    table = jnp.concatenate([row[None] for row in rows], axis=0)
     mean, var = joined(table, 2 * LANES)
     lines[0:1] = mean
     lines[1:2] = var
@@ -463,13 +477,13 @@
     level = lax.axis_index("level")
     groups = lax.axis_size("level")
     copies = []
-    sources = ((own, 0, own, 1), (near, 0, near, 1), (far0, 0, far1, 0), (back, 0, back, 1))
-    for distance, (first, first_at, second, second_at) in enumerate(sources):
+    sources = ((own[0], own[1]), (near[0], near[1]), (far0[:C2], far1[:C2]), (back[0], back[1]))
+    for distance, (first, second) in enumerate(sources):
         origin = (level + groups - distance) % groups
         named = jnp.where(names[distance] == level.astype(f32), 1.0, 0.0)
         takes0, takes1 = named[:, C : C + 1], named[:, C + 1 : C + 2]
-        value0 = jnp.maximum((first[first_at].astype(f32) - mean) * scale + moved, 0.0)
-        value1 = jnp.maximum((second[second_at].astype(f32) - mean) * scale + moved, 0.0)
+        value0 = jnp.maximum((first.astype(f32) - mean) * scale + moved, 0.0)
+        value1 = jnp.maximum((second.astype(f32) - mean) * scale + moved, 0.0)
         chosen = (
             jnp.where(takes0 > 0, value0, jnp.where(takes1 > 0, value1, 0.0)),
             jnp.where(takes0 * takes1 > 0, value1, 0.0),
@@ -489,7 +503,7 @@
     return pl.pallas_call(
         settle_kernel,
         out_shape=jax.ShapeDtypeStruct((8, C2, 512), bf16),
-        in_specs=[VMEM] * 12,
+        in_specs=[VMEM] * 10,
         out_specs=HBM,
         scratch_shapes=[
             pltpu.VMEM((8, 2 * LANES), f32),
@@ -528,21 +542,20 @@
             route.append(((x + step_x) % grid_x * GRID_Y + (y + step_y) % GRID_Y, s))
         return lax.ppermute(block, "space", route)
 
-    outer, y_low, y_high = pack_outer(brick_coords, features, occupancy)
+    outer, y_low, y_high, coords, gates = pack_outer(brick_coords, features, occupancy)
     y_before = from_tile(y_high, 0, -1)
     y_after = from_tile(y_low, 0, 1)
-    inner = pack_inner(brick_coords, features, occupancy)
+    inner = pack_inner(coords, features, gates)
     x_low, x_high = faces(outer, inner, y_before, y_after)
     x_before = from_tile(x_high, -1, 0)
     x_after = from_tile(x_low, 1, 0)
-    mid, part, taps = middle(outer, inner, y_before, y_after, conv_weight)
+    mid, partial, part, taps = middle(outer, inner, y_before, y_after, conv_weight)
     edge, stats = edges(
         outer,
         inner,
-        y_before,
-        y_after,
         x_before,
         x_after,
+        partial,
         taps,
         part,
         coarse_owner,
@@ -565,12 +578,10 @@
 
     near = up_level(sent, 1)
     back = up_level(sent, -1)
-    table = to_all(stats2, "space")
-    near, back, table = lax.optimization_barrier((near, back, table))
-    here = merge(table)
-    far0 = up_level(near[:1], 1)
-    far1 = up_level(back[1:], -1)
-    tables = [here] + [up_level(here, d) for d in range(1, level_count)]
+    here, up, down = merge(to_all(stats2, "space"), near, back)
+    tables = [here, up_level(here, 2)]
+    far0 = up_level(up, 1)
+    far1 = up_level(down, -1)
     return settle(
         (sent, near, far0, far1, back), names, tables, down_gain[None], down_shift[None]
     )

time: 74.4 us -> 69.8 us (0.938)
  starting transfers between devices: 16.1 us -> 13.3 us
  Pallas kernels: 22.5 us -> 20.2 us
  waiting for transfers between devices: 4.16 us -> 5.81 us
  local copies, waits for them, and re-layouts: 1.6 us -> 0.14 us
    ppermute x7 -> x5, starting transfers between devices: 8.53 us -> 5.73 us  [up_level(): return lax.ppermute(block, 'level', route)]
    pallas_call x1, Pallas kernels: 10.5 us -> 8.99 us  [middle(): pl.pallas_call(middle_kernel, out_shape=(pltpu.VMEM((MID, PAIRS * SZ, 2 *...]
    unnamed x21 -> x17, local copies, waits for them, and re-layouts: 1.58 us -> 0.14 us
    ppermute x7 -> x5, waiting for transfers between devices: 4.15 us -> 5.3 us  [up_level(): return lax.ppermute(block, 'level', route)]
    pallas_call x1, Pallas kernels: 2.26 us -> 1.35 us  [edges(): pl.pallas_call(edge_kernel, out_shape=(jax.ShapeDtypeStruct((2, PAIRS * S...]
  transfers between devices with their start and end apart: 11 -> 9, of which waited for: 2 -> 2; matrix products, arithmetic and copies ran while one was open for 0% -> 0% of each run, Pallas kernels for 16% -> 15%
where the time goes in v5:
time: 69.8 us; the launch traced here: 69.6 us
  blocking collectives  29.9 us (43%)
  Pallas kernels  20.2 us (29%)
  starting transfers between devices  13.3 us (19%)
  waiting for transfers between devices  5.81 us (8%)
    all_to_all x2, blocking collectives, to_all(): return lax.all_to_all(rows, axes, 0, 0, tiled=True)  29.9 us
    pallas_call x1, Pallas kernels, middle(): pl.pallas_call(middle_kernel, out_shape=(pltpu.VMEM((MID, PAIRS * SZ, 2 *...  8.99 us
    ppermute x4, starting transfers between devices, from_tile(): return lax.ppermute(block, 'space', route)  7.52 us
    ppermute x5, starting transfers between devices, up_level(): return lax.ppermute(block, 'level', route)  5.73 us
    ppermute x5, waiting for transfers between devices, up_level(): return lax.ppermute(block, 'level', route)  5.3 us
    pallas_call x1, Pallas kernels, section(): pl.pallas_call(section_kernel, out_shape=(jax.ShapeDtypeStruct((2, C2, 51...  3.55 us
    pallas_call x1, Pallas kernels, pack_outer(): pl.pallas_call(outer_kernel, out_shape=(ACT, side, side, jax.ShapeDtypeSt...  2.43 us
    pallas_call x1, Pallas kernels, settle(): pl.pallas_call(settle_kernel, out_shape=jax.ShapeDtypeStruct((8, C2, 512)...  2.22 us
  transfers between devices with their start and end apart: 9, of which 2 were waited for; matrix products, arithmetic and copies ran while one was open for 0% of the time, Pallas kernels for 15%

profile of v5, /device:TPU:0, one launch (start us, length us, event | category | flops | bytes accessed | tf_op | source)
XLA Modules:
  0.0 69.6 jit_solution(13197188723813448216)
XLA Ops:
  0.0 0.0 copy-start
  0.0 2.4 %pack_outer.1 = (bf16[16,2,4,2,16,128]{5,4,3,2,1,0:T(8,128)(2,1)S(1)}, bf16[16,16,128]{2,1,0:T(8,128)(2,1)S(1)}, bf16[16,16,128]{2,1,0:T(8,128)(2,1)S(1)}, s32[3,16]{1,0:T(4,128)S(1)}, s32[16,512]{1,0:T(8,128)S(1)}) custom-call(s32[3,16]{1,0:T(4,128)} %coords.1, bf16[16,96,512]{2,1,0:T(8,128)(2,1)} %features.3, s32[16,512]{1,0:T(8,128)} %occupancy.1), custom_call_target="tpu_custom_call" | custom-call | tf_op jit(solution)/shard_map/pack_outer/pallas_call | solution.py:105
  2.4 0.1 collective-permute-start
  2.5 1.7 %collective-permute-start.1 = (bf16[16,16,128]{2,1,0:T(8,128)(2,1)S(1)}, bf16[16,16,128]{2,1,0:T(8,128)(2,1)S(1)}, u32[]{:S(2)}, u32[]{:S(2)}) collective-permute-start(bf16[16,16,128]{2,1,0:T(8,128)(2,1)S(1)} %get-tuple-element.28), channel_id=1, source_target_pairs={{1,0},{2,1},{3,2},{0,3},{5,4},{6,5},{7,6},{4,7},{9,8},{10,9},{11,1... | collective-permute-start | bytes 196616 | tf_op jit(solution)/shard_map/ppermute | solution.py:543
  4.3 0.0 copy-done
  4.3 1.4 %pack_inner.1.inner = bf16[16,2,4,2,16,128]{5,4,3,2,1,0:T(8,128)(2,1)S(1)} custom-call(s32[3,16]{1,0:T(4,128)S(1)} %get-tuple-element.25.coords, bf16[16,96,512]{2,1,0:T(8,128)(2,1)S(1)} %copy-done, s32[16,512]{1,0:T(8,128)S(1)} %get-tuple-element.26.occupancy), custom_call_target="tpu_custom_call" | custom-call | tf_op jit(solution)/shard_map/pack_inner/pallas_call | solution.py:128
  5.7 0.0 copy-start.7
  5.7 0.0 copy-start.1
  5.7 0.5 collective-permute-done.y_before
  6.2 0.0 collective-permute-done.1.y_after
  6.2 3.3 %collective-permute-start.2 = (bf16[34,16,128]{2,1,0:T(8,128)(2,1)S(1)}, bf16[34,16,128]{2,1,0:T(8,128)(2,1)S(1)}, u32[]{:S(2)}, u32[]{:S(2)}) collective-permute-start(bf16[34,16,128]{2,1,0:T(8,128)(2,1)S(1)} %get-tuple-element.30), channel_id=1, source_target_pairs={{28,0},{29,1},{30,2},{31,3},{0,4},{1,5},{2,6},{3,7},{4,8},{5,9},{6... | collective-permute-start | bytes 417800 | tf_op jit(solution)/shard_map/ppermute | solution.py:543
  9.6 2.4 %collective-permute-start.3 = (bf16[34,16,128]{2,1,0:T(8,128)(2,1)S(1)}, bf16[34,16,128]{2,1,0:T(8,128)(2,1)S(1)}, u32[]{:S(2)}, u32[]{:S(2)}) collective-permute-start(bf16[34,16,128]{2,1,0:T(8,128)(2,1)S(1)} %get-tuple-element.31), channel_id=1, source_target_pairs={{4,0},{5,1},{6,2},{7,3},{8,4},{9,5},{10,6},{11,7},{12,8},{13,9},{1... | collective-permute-start | bytes 417800 | tf_op jit(solution)/shard_map/ppermute | solution.py:543
  11.9 0.0 copy-done.7
  11.9 0.1 copy.11.owners
  12.0 0.0 copy-done.1
  12.0 9.0 %middle.1 = (f32[14,256,256]{2,1,0:T(8,128)S(1)}, f32[2,256,256]{2,1,0:T(8,128)S(1)}, f32[8,128]{1,0:T(8,128)S(1)}, bf16[3456,256]{1,0:T(8,128)(2,1)S(1)}) custom-call(bf16[16,2,4,2,16,128]{5,4,3,2,1,0:T(8,128)(2,1)S(1)} %get-tuple-element.24.outer, bf16[16,2,4,2,16,128]{5,4,3,2,1,0:T(8,128)(2,1)S(1)} %pack_inner.1.inner, ...), custom_call_target="tpu_custom_call" | custom-call | tf_op jit(solution)/shard_map/middle/pallas_call | solution.py:266
  21.0 0.0 collective-permute-done.2.x_before
  21.0 0.0 collective-permute-done.3.x_after
  21.1 0.0 copy-start.2
  21.1 0.0 copy-start.5
  21.1 0.0 copy-start.6
  21.1 1.3 %edges.1 = (f32[2,256,256]{2,1,0:T(8,128)S(1)}, f32[128,1,256]{2,1,0:T(1,128)S(1)}) custom-call(bf16[16,2,4,2,16,128]{5,4,3,2,1,0:T(8,128)(2,1)S(1)} %get-tuple-element.24.outer, bf16[16,2,4,2,16,128]{5,4,3,2,1,0:T(8,128)(2,1)S(1)} %pack_inner.1.inner, bf16[34,16,128]{2,1,0:T(8,128)(2,1)S(1)} %collective-permute-done.2.x_before, ...), custom_call_target="tpu_custom_call" | custom-call | tf_op jit(solution)/shard_map/edges/pallas_call | solution.py:303
  22.4 19.0 %all_to_all.10.table = f32[128,1,256]{2,1,0:T(1,128)S(1)} all-to-all(f32[128,1,256]{2,1,0:T(1,128)S(1)} %get-tuple-element.36), channel_id=1, replica_groups=mesh['level'=4,'space'=32] {'level','space'}, dimensions={0} | all-to-all | bytes 262144 | tf_op jit(solution)/shard_map/all_to_all | solution.py:519
  41.4 0.0 copy-done.2
  41.4 0.0 copy-done.5
  41.4 0.0 copy-done.6
  41.4 0.0 copy-start.3
  41.4 0.0 copy-start.4
  41.4 3.6 %section.1 = (bf16[2,192,512]{2,1,0:T(8,128)(2,1)S(1)}, f32[4,1,128]{2,1,0:T(1,128)S(1)}, f32[32,1,512]{2,1,0:T(1,128)S(1)}) custom-call(f32[14,256,256]{2,1,0:T(8,128)S(1)} %get-tuple-element.29.mid, f32[2,256,256]{2,1,0:T(8,128)S(1)} %get-tuple-element.35.edge, bf16[16,2,4,2,16,128]{5,4,3,2,1,0:T(8,128)(2,1)S(1)} %get-tuple-element.24.outer, ...), custom_call_target="tpu_custom_call" | custom-call | tf_op jit(solution)/shard_map/section/pallas_call | solution.py:406
  45.0 1.0 %collective-permute-start.5 = (bf16[2,192,512]{2,1,0:T(8,128)(2,1)S(1)}, bf16[2,192,512]{2,1,0:T(8,128)(2,1)S(1)}, u32[]{:S(2)}, u32[]{:S(2)}) collective-permute-start(bf16[2,192,512]{2,1,0:T(8,128)(2,1)S(1)} %get-tuple-element.37.own), channel_id=1, source_target_pairs={{0,96},{32,0},{64,32},{96,64},{1,97},{33,1},{65,33},{97,65},{2,98}... | collective-permute-start | bytes 1179656 | tf_op jit(solution)/shard_map/ppermute | solution.py:577
  46.0 1.1 %collective-permute-start.4 = (bf16[2,192,512]{2,1,0:T(8,128)(2,1)S(1)}, bf16[2,192,512]{2,1,0:T(8,128)(2,1)S(1)}, u32[]{:S(2)}, u32[]{:S(2)}) collective-permute-start(bf16[2,192,512]{2,1,0:T(8,128)(2,1)S(1)} %get-tuple-element.37.own), channel_id=1, source_target_pairs={{0,32},{32,64},{64,96},{96,0},{1,33},{33,65},{65,97},{97,1},{2,34}... | collective-permute-start | bytes 1179656 | tf_op jit(solution)/shard_map/ppermute | solution.py:577
  47.1 11.0 %all_to_all.11.table = f32[32,1,512]{2,1,0:T(1,128)S(1)} all-to-all(f32[32,1,512]{2,1,0:T(1,128)S(1)} %get-tuple-element.38), channel_id=1, replica_groups=mesh['level'=4,'space'=32] {'space'}, dimensions={0} | all-to-all | bytes 131072 | tf_op jit(solution)/shard_map/all_to_all | solution.py:519
  58.1 0.0 collective-permute-done.5.back
  58.1 0.0 collective-permute-done.4.near
  58.1 0.2 merge.1
  58.3 0.9 %collective-permute-start.6 = (bf16[208,512]{1,0:T(8,128)(2,1)S(1)}, bf16[208,512]{1,0:T(8,128)(2,1)S(1)}, u32[]{:S(2)}, u32[]{:S(2)}) collective-permute-start(bf16[208,512]{1,0:T(8,128)(2,1)S(1)} %get-tuple-element.39), channel_id=1, source_target_pairs={{0,32},{32,64},{64,96},{96,0},{1,33},{33,65},{65,97},{97,1},{2,34}... | collective-permute-start | bytes 638984 | tf_op jit(solution)/shard_map/ppermute | solution.py:577
  59.2 2.4 %collective-permute-start.7 = (bf16[208,512]{1,0:T(8,128)(2,1)S(1)}, bf16[208,512]{1,0:T(8,128)(2,1)S(1)}, u32[]{:S(2)}, u32[]{:S(2)}) collective-permute-start(bf16[208,512]{1,0:T(8,128)(2,1)S(1)} %get-tuple-element.40), channel_id=1, source_target_pairs={{0,96},{32,0},{64,32},{96,64},{1,97},{33,1},{65,33},{97,65},{2,98}... | collective-permute-start | bytes 638984 | tf_op jit(solution)/shard_map/ppermute | solution.py:577
  61.6 0.3 collective-permute-start.8
  61.9 5.3 %collective-permute-done.8.row_far = f32[1,1,512]{2,1,0:T(1,128)S(1)} collective-permute-done((f32[1,1,512]{2,1,0:T(1,128)S(1)}, f32[1,1,512]{2,1,0:T(1,128)S(1)}, u32[]{:S(2)}, u32[]{:S(2)}) %collective-permute-start.8) | collective-permute-done | bytes 2080 | tf_op jit(solution)/shard_map/ppermute | solution.py:577
  67.2 0.0 collective-permute-done.6.far0
  67.2 0.0 collective-permute-done.7.far1
  67.2 0.0 copy-done.3
  67.2 0.0 copy-done.4
  67.2 2.2 %settle.1 = bf16[8,192,512]{2,1,0:T(8,128)(2,1)} custom-call(bf16[2,192,512]{2,1,0:T(8,128)(2,1)S(1)} %get-tuple-element.37.own, bf16[2,192,512]{2,1,0:T(8,128)(2,1)S(1)} %collective-permute-done.4.near, bf16[208,512]{1,0:T(8,128)(2,1)S(1)} %collective-permute-done.6.far0, bf16[208,512]{1,0:T(8,128)(2,1)S(1)} %collective-permute-done.7.far1, ...), custom_call_target="tpu_custom_call" | custom-call | tf_op jit(solution)/shard_map/settle/pallas_call | solution.py:503
  (1 shorter events, 0.0 us)
Async XLA Ops:
  0.0 4.3 %copy-start = (bf16[16,96,512]{2,1,0:T(8,128)(2,1)S(1)}, bf16[16,96,512]{2,1,0:T(8,128)(2,1)}, u32[]{:S(2)}) copy-start(bf16[16,96,512]{2,1,0:T(8,128)(2,1)} %features.3) | copy-start | bytes 4718596
  2.4 3.8 %collective-permute-start = (bf16[16,16,128]{2,1,0:T(8,128)(2,1)S(1)}, bf16[16,16,128]{2,1,0:T(8,128)(2,1)S(1)}, u32[]{:S(2)}, u32[]{:S(2)}) collective-permute-start(bf16[16,16,128]{2,1,0:T(8,128)(2,1)S(1)} %get-tuple-element.27), channel_id=1, source_target_pairs={{3,0},{0,1},{1,2},{2,3},{7,4},{4,5},{5,6},{6,7},{11,8},{8,9},{9,10... | collective-permute-start | bytes 196616 | tf_op jit(solution)/shard_map/ppermute | solution.py:543
  2.5 3.7 %collective-permute-start.1 = (bf16[16,16,128]{2,1,0:T(8,128)(2,1)S(1)}, bf16[16,16,128]{2,1,0:T(8,128)(2,1)S(1)}, u32[]{:S(2)}, u32[]{:S(2)}) collective-permute-start(bf16[16,16,128]{2,1,0:T(8,128)(2,1)S(1)} %get-tuple-element.28), channel_id=1, source_target_pairs={{1,0},{2,1},{3,2},{0,3},{5,4},{6,5},{7,6},{4,7},{9,8},{10,9},{11,1... | collective-permute-start | bytes 196616 | tf_op jit(solution)/shard_map/ppermute | solution.py:543
  5.7 6.3 %copy-start.7 = (s32[2,1]{0,1:T(1,128)S(1)}, s32[2,1]{0,1:T(1,128)}, u32[]{:S(2)}) copy-start(s32[2,1]{0,1:T(1,128)} %param.13) | copy-start | bytes 28
  5.7 6.4 %copy-start.1 = (bf16[27,96,96]{2,1,0:T(8,128)(2,1)S(1)}, bf16[27,96,96]{2,1,0:T(8,128)(2,1)}, u32[]{:S(2)}) copy-start(bf16[27,96,96]{2,1,0:T(8,128)(2,1)} %weight.2) | copy-start | bytes 1492996
  6.2 14.8 %collective-permute-start.2 = (bf16[34,16,128]{2,1,0:T(8,128)(2,1)S(1)}, bf16[34,16,128]{2,1,0:T(8,128)(2,1)S(1)}, u32[]{:S(2)}, u32[]{:S(2)}) collective-permute-start(bf16[34,16,128]{2,1,0:T(8,128)(2,1)S(1)} %get-tuple-element.30), channel_id=1, source_target_pairs={{28,0},{29,1},{30,2},{31,3},{0,4},{1,5},{2,6},{3,7},{4,8},{5,9},{6... | collective-permute-start | bytes 417800 | tf_op jit(solution)/shard_map/ppermute | solution.py:543
  9.6 11.5 %collective-permute-start.3 = (bf16[34,16,128]{2,1,0:T(8,128)(2,1)S(1)}, bf16[34,16,128]{2,1,0:T(8,128)(2,1)S(1)}, u32[]{:S(2)}, u32[]{:S(2)}) collective-permute-start(bf16[34,16,128]{2,1,0:T(8,128)(2,1)S(1)} %get-tuple-element.31), channel_id=1, source_target_pairs={{4,0},{5,1},{6,2},{7,3},{8,4},{9,5},{10,6},{11,7},{12,8},{13,9},{1... | collective-permute-start | bytes 417800 | tf_op jit(solution)/shard_map/ppermute | solution.py:543
  21.1 20.4 %copy-start.2 = (bf16[8,192,96]{2,1,0:T(8,128)(2,1)S(1)}, bf16[8,192,96]{2,1,0:T(8,128)(2,1)}, u32[]{:S(2)}) copy-start(bf16[8,192,96]{2,1,0:T(8,128)(2,1)} %weight.3) | copy-start | bytes 884740
  21.1 20.3 %copy-start.5 = (f32[96]{0:T(128)S(1)}, f32[96]{0:T(128)}, u32[]{:S(2)}) copy-start(f32[96]{0:T(128)} %param.15) | copy-start | bytes 1156
  21.1 20.3 %copy-start.6 = (f32[96]{0:T(128)S(1)}, f32[96]{0:T(128)}, u32[]{:S(2)}) copy-start(f32[96]{0:T(128)} %param.16) | copy-start | bytes 1156
  41.4 25.8 %copy-start.3 = (f32[192]{0:T(256)S(1)}, f32[192]{0:T(256)}, u32[]{:S(2)}) copy-start(f32[192]{0:T(256)} %param.18) | copy-start | bytes 2308
  41.4 25.8 %copy-start.4 = (f32[192]{0:T(256)S(1)}, f32[192]{0:T(256)}, u32[]{:S(2)}) copy-start(f32[192]{0:T(256)} %param.19) | copy-start | bytes 2308
  45.0 13.1 %collective-permute-start.5 = (bf16[2,192,512]{2,1,0:T(8,128)(2,1)S(1)}, bf16[2,192,512]{2,1,0:T(8,128)(2,1)S(1)}, u32[]{:S(2)}, u32[]{:S(2)}) collective-permute-start(bf16[2,192,512]{2,1,0:T(8,128)(2,1)S(1)} %get-tuple-element.37.own), channel_id=1, source_target_pairs={{0,96},{32,0},{64,32},{96,64},{1,97},{33,1},{65,33},{97,65},{2,98}... | collective-permute-start | bytes 1179656 | tf_op jit(solution)/shard_map/ppermute | solution.py:577
  46.0 12.1 %collective-permute-start.4 = (bf16[2,192,512]{2,1,0:T(8,128)(2,1)S(1)}, bf16[2,192,512]{2,1,0:T(8,128)(2,1)S(1)}, u32[]{:S(2)}, u32[]{:S(2)}) collective-permute-start(bf16[2,192,512]{2,1,0:T(8,128)(2,1)S(1)} %get-tuple-element.37.own), channel_id=1, source_target_pairs={{0,32},{32,64},{64,96},{96,0},{1,33},{33,65},{65,97},{97,1},{2,34}... | collective-permute-start | bytes 1179656 | tf_op jit(solution)/shard_map/ppermute | solution.py:577
  58.3 8.9 %collective-permute-start.6 = (bf16[208,512]{1,0:T(8,128)(2,1)S(1)}, bf16[208,512]{1,0:T(8,128)(2,1)S(1)}, u32[]{:S(2)}, u32[]{:S(2)}) collective-permute-start(bf16[208,512]{1,0:T(8,128)(2,1)S(1)} %get-tuple-element.39), channel_id=1, source_target_pairs={{0,32},{32,64},{64,96},{96,0},{1,33},{33,65},{65,97},{97,1},{2,34}... | collective-permute-start | bytes 638984 | tf_op jit(solution)/shard_map/ppermute | solution.py:577
  59.2 8.0 %collective-permute-start.7 = (bf16[208,512]{1,0:T(8,128)(2,1)S(1)}, bf16[208,512]{1,0:T(8,128)(2,1)S(1)}, u32[]{:S(2)}, u32[]{:S(2)}) collective-permute-start(bf16[208,512]{1,0:T(8,128)(2,1)S(1)} %get-tuple-element.40), channel_id=1, source_target_pairs={{0,96},{32,0},{64,32},{96,64},{1,97},{33,1},{65,33},{97,65},{2,98}... | collective-permute-start | bytes 638984 | tf_op jit(solution)/shard_map/ppermute | solution.py:577
  61.6 5.6 %collective-permute-start.8 = (f32[1,1,512]{2,1,0:T(1,128)S(1)}, f32[1,1,512]{2,1,0:T(1,128)S(1)}, u32[]{:S(2)}, u32[]{:S(2)}) collective-permute-start(f32[1,1,512]{2,1,0:T(1,128)S(1)} %get-tuple-element.42.row_here), channel_id=1, source_target_pairs={{0,64},{32,96},{64,0},{96,32},{1,65},{33,97},{65,1},{97,33},{2,66}... | collective-permute-start | bytes 6152 | tf_op jit(solution)/shard_map/ppermute | solution.py:577

commit v6 on v5

--- a/solution.py
+++ b/solution.py
@@ -171,11 +171,6 @@
     return [jnp.stack(pair, axis=1).reshape(PAIRS, SZ, WIDE).astype(bf16) for pair in pairs]
 
 
-def lane_spread():
-    row = lax.broadcasted_iota(jnp.int32, (LANES, LANES), 0)
-    return jnp.where(row == LANES - 1, 1.0, 0.0).astype(bf16)
-
-
 def plane_of(outer, inner, x):
     return jnp.concatenate([outer[x, 0], inner[x, 0], inner[x, 1], outer[x, 1]], axis=0)
 
@@ -189,11 +184,18 @@
     return plain_dot(jnp.concatenate(rows, axis=1), taps)
 
 
+def mask_of(cells):
+    return jnp.broadcast_to(cells[:, LANES - 1 :], cells.shape)
+
+
+def rows_of(planes, parity):
+    return jnp.concatenate(
+        [plane[:, parity].reshape(PAIRS * SZ, LANES) for plane in planes], axis=0
+    ).astype(f32)
+
+
 def planes_mask(planes):
-    spread = lane_spread()
-    even = jnp.concatenate([plane[:, 0].reshape(PAIRS * SZ, LANES) for plane in planes], axis=0)
-    odd = jnp.concatenate([plane[:, 1].reshape(PAIRS * SZ, LANES) for plane in planes], axis=0)
-    return jnp.concatenate([plain_dot(even, spread), plain_dot(odd, spread)], axis=1)
+    return jnp.concatenate([mask_of(rows_of(planes, 0)), mask_of(rows_of(planes, 1))], axis=1)
 
 
 def folded(row):
@@ -202,6 +204,7 @@
 
 MID = SX - 2
 STEP = 2
+GROUP = 2
 
 
 def merged(first, second):
@@ -337,8 +340,7 @@
     real = lax.broadcasted_iota(jnp.int32, (1, LANES), 1) < C
     scale = jnp.where(real, lines[0:1] / jnp.sqrt(var + epsilon), 0.0)
     mean = jnp.where(real, mean, 0.0)
-    moved = lines[1:2]
-    mean = jnp.concatenate([mean, mean], axis=1)
+    moved = lines[1:2] - mean * scale
     scale = jnp.concatenate([scale, scale], axis=1)
     moved = jnp.concatenate([moved, moved], axis=1)
     taps[...] = jnp.zeros(taps.shape, bf16)
@@ -346,34 +348,35 @@
         for b in range(2):
             for c in range(2):
                 first = ((a * 2 + c) * 2 + b) * LANES
-                taps[:C2, first : first + C] = weight[(a * 2 + b) * 2 + c]
-
-    spread = lane_spread()
+                taps[first : first + C, :C2] = weight[(a * 2 + b) * 2 + c].T
+
     total = count = jnp.zeros((1, 2 * LANES), f32)
-    for X in range(SX // 2):
-        pieces, covers = [], []
-        for a in range(2):
-            x = 2 * X + a
-            conv = edge[0] if x == 0 else edge[1] if x == SX - 1 else mid[x - 1]
-            plane = plane_of(outer, inner, x)
-            even = plane[:, 0].reshape(PAIRS * SZ, LANES)
-            odd = plane[:, 1].reshape(PAIRS * SZ, LANES)
-            even_mask, odd_mask = plain_dot(even, spread), plain_dot(odd, spread)
-            mask = jnp.concatenate([even_mask, odd_mask], axis=1)
-            active = jnp.concatenate([even, odd], axis=1).astype(f32)
-            normed = (conv - mean) * scale + moved
-            section = active + mask * jnp.maximum(normed, 0.0)
-            section = section.reshape(PAIRS, 2, 8, 2 * LANES)
-            for c in range(2):
-                pieces.append(section[:, c].reshape(PAIRS * 8, 2 * LANES).astype(bf16))
-            both = jnp.maximum(even_mask, odd_mask).reshape(PAIRS, 2, 8, LANES)
-            covers.append(jnp.maximum(both[:, 0], both[:, 1]).reshape(PAIRS * 8, LANES))
-        value = rows_dot(jnp.concatenate(pieces, axis=1), taps[...])
+    for group in range(0, SX // 2, GROUP):
+        blocks, coverings = [], []
+        for X in range(group, group + GROUP):
+            pieces, covers = [], []
+            for a in range(2):
+                x = 2 * X + a
+                conv = edge[0] if x == 0 else edge[1] if x == SX - 1 else mid[x - 1]
+                plane = plane_of(outer, inner, x)
+                even, odd = rows_of([plane], 0), rows_of([plane], 1)
+                even_mask, odd_mask = mask_of(even), mask_of(odd)
+                mask = jnp.concatenate([even_mask, odd_mask], axis=1)
+                active = jnp.concatenate([even, odd], axis=1)
+                section = active + mask * jnp.maximum(conv * scale + moved, 0.0)
+                section = section.reshape(PAIRS, 2, 8, 2 * LANES)
+                for c in range(2):
+                    pieces.append(section[:, c].reshape(PAIRS * 8, 2 * LANES).astype(bf16))
+                both = jnp.maximum(even_mask, odd_mask).reshape(PAIRS, 2, 8, LANES)
+                covers.append(jnp.maximum(both[:, 0], both[:, 1]).reshape(PAIRS * 8, LANES))
+            blocks.append(jnp.concatenate(pieces, axis=1))
+            coverings.append(jnp.maximum(covers[0], covers[1]))
+        value = plain_dot(jnp.concatenate(blocks, axis=0), taps[...])
         value = value.astype(bf16).astype(f32)
-        covered = jnp.maximum(covers[0], covers[1])
+        covered = jnp.concatenate(coverings, axis=0)
         covered = jnp.concatenate([covered, covered], axis=1)
-        down[X] = value
-        cover[X] = covered
+        down[group : group + GROUP] = value.reshape(GROUP, PAIRS * 8, 2 * LANES)
+        cover[group : group + GROUP] = covered.reshape(GROUP, PAIRS * 8, 2 * LANES)
         total = total + jnp.sum(value * covered, axis=0, keepdims=True)
         count = count + jnp.sum(covered, axis=0, keepdims=True)
 
@@ -413,7 +416,7 @@
         in_specs=[VMEM] * 8,
         out_specs=(VMEM,) * 3,
         scratch_shapes=[
-            pltpu.VMEM((2 * LANES, 8 * LANES), bf16),
+            pltpu.VMEM((8 * LANES, 2 * LANES), bf16),
             pltpu.VMEM((SX // 2, PAIRS * 8, 2 * LANES), f32),
             pltpu.VMEM((SX // 2, PAIRS * 8, 2 * LANES), f32),
             pltpu.VMEM((8, LANES), f32),
@@ -472,8 +475,8 @@
     lines[2:3, :C2] = gain[...]
     lines[3:4, :C2] = shift[...]
     turned = lines[...].T[:C2]
-    mean, moved = turned[:, 0:1], turned[:, 3:4]
     scale = turned[:, 2:3] / jnp.sqrt(turned[:, 1:2] + epsilon)
+    moved = turned[:, 3:4] - turned[:, 0:1] * scale
     level = lax.axis_index("level")
     groups = lax.axis_size("level")
     copies = []
@@ -482,8 +485,8 @@
         origin = (level + groups - distance) % groups
         named = jnp.where(names[distance] == level.astype(f32), 1.0, 0.0)
         takes0, takes1 = named[:, C : C + 1], named[:, C + 1 : C + 2]
-        value0 = jnp.maximum((first.astype(f32) - mean) * scale + moved, 0.0)
-        value1 = jnp.maximum((second.astype(f32) - mean) * scale + moved, 0.0)
+        value0 = jnp.maximum(first.astype(f32) * scale + moved, 0.0)
+        value1 = jnp.maximum(second.astype(f32) * scale + moved, 0.0)
         chosen = (
             jnp.where(takes0 > 0, value0, jnp.where(takes1 > 0, value1, 0.0)),
             jnp.where(takes0 * takes1 > 0, value1, 0.0),

time: 69.8 us -> 68.6 us (0.983)
  Pallas kernels: 20.2 us -> 19 us
  transfers between devices with their start and end apart: 9 -> 9, of which waited for: 2 -> 2; matrix products, arithmetic and copies ran while one was open for 0% -> 0% of each run, Pallas kernels for 15% -> 14%
where the time goes in v6:
time: 68.6 us; the launch traced here: 68.4 us
  blocking collectives  30 us (44%)
  Pallas kernels  19 us (28%)
  starting transfers between devices  13.2 us (19%)
  waiting for transfers between devices  5.81 us (8%)
    all_to_all x2, blocking collectives, to_all(): return lax.all_to_all(rows, axes, 0, 0, tiled=True)  30 us
    pallas_call x1, Pallas kernels, middle(): pl.pallas_call(middle_kernel, out_shape=(pltpu.VMEM((MID, PAIRS * SZ, 2 *...  8.38 us
    ppermute x4, starting transfers between devices, from_tile(): return lax.ppermute(block, 'space', route)  7.52 us
    ppermute x5, starting transfers between devices, up_level(): return lax.ppermute(block, 'level', route)  5.73 us
    ppermute x5, waiting for transfers between devices, up_level(): return lax.ppermute(block, 'level', route)  5.3 us
    pallas_call x1, Pallas kernels, section(): pl.pallas_call(section_kernel, out_shape=(jax.ShapeDtypeStruct((2, C2, 51...  3.05 us
    pallas_call x1, Pallas kernels, pack_outer(): pl.pallas_call(outer_kernel, out_shape=(ACT, side, side, jax.ShapeDtypeSt...  2.43 us
    pallas_call x1, Pallas kernels, settle(): pl.pallas_call(settle_kernel, out_shape=jax.ShapeDtypeStruct((8, C2, 512)...  2.21 us
  transfers between devices with their start and end apart: 9, of which 2 were waited for; matrix products, arithmetic and copies ran while one was open for 0% of the time, Pallas kernels for 14%

profile of v6, /device:TPU:0, one launch (start us, length us, event | category | flops | bytes accessed | tf_op | source)
XLA Modules:
  0.0 68.4 jit_solution(5032724196443685596)
XLA Ops:
  0.0 0.0 copy-start
  0.0 2.4 %pack_outer.1 = (bf16[16,2,4,2,16,128]{5,4,3,2,1,0:T(8,128)(2,1)S(1)}, bf16[16,16,128]{2,1,0:T(8,128)(2,1)S(1)}, bf16[16,16,128]{2,1,0:T(8,128)(2,1)S(1)}, s32[3,16]{1,0:T(4,128)S(1)}, s32[16,512]{1,0:T(8,128)S(1)}) custom-call(s32[3,16]{1,0:T(4,128)} %coords.1, bf16[16,96,512]{2,1,0:T(8,128)(2,1)} %features.3, s32[16,512]{1,0:T(8,128)} %occupancy.1), custom_call_target="tpu_custom_call" | custom-call | tf_op jit(solution)/shard_map/pack_outer/pallas_call | solution.py:105
  2.4 0.1 collective-permute-start
  2.5 1.7 %collective-permute-start.1 = (bf16[16,16,128]{2,1,0:T(8,128)(2,1)S(1)}, bf16[16,16,128]{2,1,0:T(8,128)(2,1)S(1)}, u32[]{:S(2)}, u32[]{:S(2)}) collective-permute-start(bf16[16,16,128]{2,1,0:T(8,128)(2,1)S(1)} %get-tuple-element.28), channel_id=1, source_target_pairs={{1,0},{2,1},{3,2},{0,3},{5,4},{6,5},{7,6},{4,7},{9,8},{10,9},{11,1... | collective-permute-start | bytes 196616 | tf_op jit(solution)/shard_map/ppermute | solution.py:546
  4.3 0.0 copy-done
  4.3 1.4 %pack_inner.1.inner = bf16[16,2,4,2,16,128]{5,4,3,2,1,0:T(8,128)(2,1)S(1)} custom-call(s32[3,16]{1,0:T(4,128)S(1)} %get-tuple-element.25.coords, bf16[16,96,512]{2,1,0:T(8,128)(2,1)S(1)} %copy-done, s32[16,512]{1,0:T(8,128)S(1)} %get-tuple-element.26.occupancy), custom_call_target="tpu_custom_call" | custom-call | tf_op jit(solution)/shard_map/pack_inner/pallas_call | solution.py:128
  5.7 0.0 copy-start.7
  5.7 0.0 copy-start.1
  5.7 0.5 collective-permute-done.y_before
  6.2 0.0 collective-permute-done.1.y_after
  6.2 3.3 %collective-permute-start.2 = (bf16[34,16,128]{2,1,0:T(8,128)(2,1)S(1)}, bf16[34,16,128]{2,1,0:T(8,128)(2,1)S(1)}, u32[]{:S(2)}, u32[]{:S(2)}) collective-permute-start(bf16[34,16,128]{2,1,0:T(8,128)(2,1)S(1)} %get-tuple-element.30), channel_id=1, source_target_pairs={{28,0},{29,1},{30,2},{31,3},{0,4},{1,5},{2,6},{3,7},{4,8},{5,9},{6... | collective-permute-start | bytes 417800 | tf_op jit(solution)/shard_map/ppermute | solution.py:546
  9.6 2.4 %collective-permute-start.3 = (bf16[34,16,128]{2,1,0:T(8,128)(2,1)S(1)}, bf16[34,16,128]{2,1,0:T(8,128)(2,1)S(1)}, u32[]{:S(2)}, u32[]{:S(2)}) collective-permute-start(bf16[34,16,128]{2,1,0:T(8,128)(2,1)S(1)} %get-tuple-element.31), channel_id=1, source_target_pairs={{4,0},{5,1},{6,2},{7,3},{8,4},{9,5},{10,6},{11,7},{12,8},{13,9},{1... | collective-permute-start | bytes 417800 | tf_op jit(solution)/shard_map/ppermute | solution.py:546
  11.9 0.0 copy-done.7
  11.9 0.1 copy.11.owners
  12.0 0.0 copy-done.1
  12.0 8.4 %middle.1 = (f32[14,256,256]{2,1,0:T(8,128)S(1)}, f32[2,256,256]{2,1,0:T(8,128)S(1)}, f32[8,128]{1,0:T(8,128)S(1)}, bf16[3456,256]{1,0:T(8,128)(2,1)S(1)}) custom-call(bf16[16,2,4,2,16,128]{5,4,3,2,1,0:T(8,128)(2,1)S(1)} %get-tuple-element.24.outer, bf16[16,2,4,2,16,128]{5,4,3,2,1,0:T(8,128)(2,1)S(1)} %pack_inner.1.inner, ...), custom_call_target="tpu_custom_call" | custom-call | tf_op jit(solution)/shard_map/middle/pallas_call | solution.py:269
  20.4 0.0 collective-permute-done.2.x_before
  20.4 0.0 collective-permute-done.3.x_after
  20.4 0.0 copy-start.2
  20.4 0.0 copy-start.5
  20.5 0.0 copy-start.6
  20.5 1.3 %edges.1 = (f32[2,256,256]{2,1,0:T(8,128)S(1)}, f32[128,1,256]{2,1,0:T(1,128)S(1)}) custom-call(bf16[16,2,4,2,16,128]{5,4,3,2,1,0:T(8,128)(2,1)S(1)} %get-tuple-element.24.outer, bf16[16,2,4,2,16,128]{5,4,3,2,1,0:T(8,128)(2,1)S(1)} %pack_inner.1.inner, bf16[34,16,128]{2,1,0:T(8,128)(2,1)S(1)} %collective-permute-done.2.x_before, ...), custom_call_target="tpu_custom_call" | custom-call | tf_op jit(solution)/shard_map/edges/pallas_call | solution.py:306
  21.8 19.0 %all_to_all.10.table = f32[128,1,256]{2,1,0:T(1,128)S(1)} all-to-all(f32[128,1,256]{2,1,0:T(1,128)S(1)} %get-tuple-element.36), channel_id=1, replica_groups=mesh['level'=4,'space'=32] {'level','space'}, dimensions={0} | all-to-all | bytes 262144 | tf_op jit(solution)/shard_map/all_to_all | solution.py:522
  40.8 0.0 copy-done.2
  40.8 0.0 copy-done.5
  40.8 0.0 copy-done.6
  40.8 0.0 copy-start.3
  40.8 0.0 copy-start.4
  40.8 3.1 %section.1 = (bf16[2,192,512]{2,1,0:T(8,128)(2,1)S(1)}, f32[4,1,128]{2,1,0:T(1,128)S(1)}, f32[32,1,512]{2,1,0:T(1,128)S(1)}) custom-call(f32[14,256,256]{2,1,0:T(8,128)S(1)} %get-tuple-element.29.mid, f32[2,256,256]{2,1,0:T(8,128)S(1)} %get-tuple-element.35.edge, bf16[16,2,4,2,16,128]{5,4,3,2,1,0:T(8,128)(2,1)S(1)} %get-tuple-element.24.outer, ...), custom_call_target="tpu_custom_call" | custom-call | tf_op jit(solution)/shard_map/section/pallas_call | solution.py:409
  43.8 1.0 %collective-permute-start.5 = (bf16[2,192,512]{2,1,0:T(8,128)(2,1)S(1)}, bf16[2,192,512]{2,1,0:T(8,128)(2,1)S(1)}, u32[]{:S(2)}, u32[]{:S(2)}) collective-permute-start(bf16[2,192,512]{2,1,0:T(8,128)(2,1)S(1)} %get-tuple-element.37.own), channel_id=1, source_target_pairs={{0,96},{32,0},{64,32},{96,64},{1,97},{33,1},{65,33},{97,65},{2,98}... | collective-permute-start | bytes 1179656 | tf_op jit(solution)/shard_map/ppermute | solution.py:580
  44.8 1.1 %collective-permute-start.4 = (bf16[2,192,512]{2,1,0:T(8,128)(2,1)S(1)}, bf16[2,192,512]{2,1,0:T(8,128)(2,1)S(1)}, u32[]{:S(2)}, u32[]{:S(2)}) collective-permute-start(bf16[2,192,512]{2,1,0:T(8,128)(2,1)S(1)} %get-tuple-element.37.own), channel_id=1, source_target_pairs={{0,32},{32,64},{64,96},{96,0},{1,33},{33,65},{65,97},{97,1},{2,34}... | collective-permute-start | bytes 1179656 | tf_op jit(solution)/shard_map/ppermute | solution.py:580
  45.9 11.0 %all_to_all.11.table = f32[32,1,512]{2,1,0:T(1,128)S(1)} all-to-all(f32[32,1,512]{2,1,0:T(1,128)S(1)} %get-tuple-element.38), channel_id=1, replica_groups=mesh['level'=4,'space'=32] {'space'}, dimensions={0} | all-to-all | bytes 131072 | tf_op jit(solution)/shard_map/all_to_all | solution.py:522
  56.9 0.0 collective-permute-done.5.back
  56.9 0.0 collective-permute-done.4.near
  56.9 0.2 merge.1
  57.1 0.9 %collective-permute-start.6 = (bf16[208,512]{1,0:T(8,128)(2,1)S(1)}, bf16[208,512]{1,0:T(8,128)(2,1)S(1)}, u32[]{:S(2)}, u32[]{:S(2)}) collective-permute-start(bf16[208,512]{1,0:T(8,128)(2,1)S(1)} %get-tuple-element.39), channel_id=1, source_target_pairs={{0,32},{32,64},{64,96},{96,0},{1,33},{33,65},{65,97},{97,1},{2,34}... | collective-permute-start | bytes 638984 | tf_op jit(solution)/shard_map/ppermute | solution.py:580
  58.0 2.4 %collective-permute-start.7 = (bf16[208,512]{1,0:T(8,128)(2,1)S(1)}, bf16[208,512]{1,0:T(8,128)(2,1)S(1)}, u32[]{:S(2)}, u32[]{:S(2)}) collective-permute-start(bf16[208,512]{1,0:T(8,128)(2,1)S(1)} %get-tuple-element.40), channel_id=1, source_target_pairs={{0,96},{32,0},{64,32},{96,64},{1,97},{33,1},{65,33},{97,65},{2,98}... | collective-permute-start | bytes 638984 | tf_op jit(solution)/shard_map/ppermute | solution.py:580
  60.4 0.3 collective-permute-start.8
  60.8 5.3 %collective-permute-done.8.row_far = f32[1,1,512]{2,1,0:T(1,128)S(1)} collective-permute-done((f32[1,1,512]{2,1,0:T(1,128)S(1)}, f32[1,1,512]{2,1,0:T(1,128)S(1)}, u32[]{:S(2)}, u32[]{:S(2)}) %collective-permute-start.8) | collective-permute-done | bytes 2080 | tf_op jit(solution)/shard_map/ppermute | solution.py:580
  66.0 0.0 collective-permute-done.6.far0
  66.0 0.0 collective-permute-done.7.far1
  66.1 0.0 copy-done.3
  66.1 0.0 copy-done.4
  66.1 2.2 %settle.1 = bf16[8,192,512]{2,1,0:T(8,128)(2,1)} custom-call(bf16[2,192,512]{2,1,0:T(8,128)(2,1)S(1)} %get-tuple-element.37.own, bf16[2,192,512]{2,1,0:T(8,128)(2,1)S(1)} %collective-permute-done.4.near, bf16[208,512]{1,0:T(8,128)(2,1)S(1)} %collective-permute-done.6.far0, bf16[208,512]{1,0:T(8,128)(2,1)S(1)} %collective-permute-done.7.far1, ...), custom_call_target="tpu_custom_call" | custom-call | tf_op jit(solution)/shard_map/settle/pallas_call | solution.py:506
  (1 shorter events, 0.0 us)
Async XLA Ops:
  0.0 4.3 %copy-start = (bf16[16,96,512]{2,1,0:T(8,128)(2,1)S(1)}, bf16[16,96,512]{2,1,0:T(8,128)(2,1)}, u32[]{:S(2)}) copy-start(bf16[16,96,512]{2,1,0:T(8,128)(2,1)} %features.3) | copy-start | bytes 4718596
  2.4 3.8 %collective-permute-start = (bf16[16,16,128]{2,1,0:T(8,128)(2,1)S(1)}, bf16[16,16,128]{2,1,0:T(8,128)(2,1)S(1)}, u32[]{:S(2)}, u32[]{:S(2)}) collective-permute-start(bf16[16,16,128]{2,1,0:T(8,128)(2,1)S(1)} %get-tuple-element.27), channel_id=1, source_target_pairs={{3,0},{0,1},{1,2},{2,3},{7,4},{4,5},{5,6},{6,7},{11,8},{8,9},{9,10... | collective-permute-start | bytes 196616 | tf_op jit(solution)/shard_map/ppermute | solution.py:546
  2.5 3.7 %collective-permute-start.1 = (bf16[16,16,128]{2,1,0:T(8,128)(2,1)S(1)}, bf16[16,16,128]{2,1,0:T(8,128)(2,1)S(1)}, u32[]{:S(2)}, u32[]{:S(2)}) collective-permute-start(bf16[16,16,128]{2,1,0:T(8,128)(2,1)S(1)} %get-tuple-element.28), channel_id=1, source_target_pairs={{1,0},{2,1},{3,2},{0,3},{5,4},{6,5},{7,6},{4,7},{9,8},{10,9},{11,1... | collective-permute-start | bytes 196616 | tf_op jit(solution)/shard_map/ppermute | solution.py:546
  5.7 6.3 %copy-start.7 = (s32[2,1]{0,1:T(1,128)S(1)}, s32[2,1]{0,1:T(1,128)}, u32[]{:S(2)}) copy-start(s32[2,1]{0,1:T(1,128)} %param.13) | copy-start | bytes 28
  5.7 6.4 %copy-start.1 = (bf16[27,96,96]{2,1,0:T(8,128)(2,1)S(1)}, bf16[27,96,96]{2,1,0:T(8,128)(2,1)}, u32[]{:S(2)}) copy-start(bf16[27,96,96]{2,1,0:T(8,128)(2,1)} %weight.2) | copy-start | bytes 1492996
  6.2 14.2 %collective-permute-start.2 = (bf16[34,16,128]{2,1,0:T(8,128)(2,1)S(1)}, bf16[34,16,128]{2,1,0:T(8,128)(2,1)S(1)}, u32[]{:S(2)}, u32[]{:S(2)}) collective-permute-start(bf16[34,16,128]{2,1,0:T(8,128)(2,1)S(1)} %get-tuple-element.30), channel_id=1, source_target_pairs={{28,0},{29,1},{30,2},{31,3},{0,4},{1,5},{2,6},{3,7},{4,8},{5,9},{6... | collective-permute-start | bytes 417800 | tf_op jit(solution)/shard_map/ppermute | solution.py:546
  9.6 10.9 %collective-permute-start.3 = (bf16[34,16,128]{2,1,0:T(8,128)(2,1)S(1)}, bf16[34,16,128]{2,1,0:T(8,128)(2,1)S(1)}, u32[]{:S(2)}, u32[]{:S(2)}) collective-permute-start(bf16[34,16,128]{2,1,0:T(8,128)(2,1)S(1)} %get-tuple-element.31), channel_id=1, source_target_pairs={{4,0},{5,1},{6,2},{7,3},{8,4},{9,5},{10,6},{11,7},{12,8},{13,9},{1... | collective-permute-start | bytes 417800 | tf_op jit(solution)/shard_map/ppermute | solution.py:546
  20.4 20.3 %copy-start.2 = (bf16[8,192,96]{2,1,0:T(8,128)(2,1)S(1)}, bf16[8,192,96]{2,1,0:T(8,128)(2,1)}, u32[]{:S(2)}) copy-start(bf16[8,192,96]{2,1,0:T(8,128)(2,1)} %weight.3) | copy-start | bytes 884740
  20.4 20.3 %copy-start.5 = (f32[96]{0:T(128)S(1)}, f32[96]{0:T(128)}, u32[]{:S(2)}) copy-start(f32[96]{0:T(128)} %param.15) | copy-start | bytes 1156
  20.5 20.3 %copy-start.6 = (f32[96]{0:T(128)S(1)}, f32[96]{0:T(128)}, u32[]{:S(2)}) copy-start(f32[96]{0:T(128)} %param.16) | copy-start | bytes 1156
  40.8 25.3 %copy-start.3 = (f32[192]{0:T(256)S(1)}, f32[192]{0:T(256)}, u32[]{:S(2)}) copy-start(f32[192]{0:T(256)} %param.18) | copy-start | bytes 2308
  40.8 25.3 %copy-start.4 = (f32[192]{0:T(256)S(1)}, f32[192]{0:T(256)}, u32[]{:S(2)}) copy-start(f32[192]{0:T(256)} %param.19) | copy-start | bytes 2308
  43.8 13.1 %collective-permute-start.5 = (bf16[2,192,512]{2,1,0:T(8,128)(2,1)S(1)}, bf16[2,192,512]{2,1,0:T(8,128)(2,1)S(1)}, u32[]{:S(2)}, u32[]{:S(2)}) collective-permute-start(bf16[2,192,512]{2,1,0:T(8,128)(2,1)S(1)} %get-tuple-element.37.own), channel_id=1, source_target_pairs={{0,96},{32,0},{64,32},{96,64},{1,97},{33,1},{65,33},{97,65},{2,98}... | collective-permute-start | bytes 1179656 | tf_op jit(solution)/shard_map/ppermute | solution.py:580
  44.8 12.1 %collective-permute-start.4 = (bf16[2,192,512]{2,1,0:T(8,128)(2,1)S(1)}, bf16[2,192,512]{2,1,0:T(8,128)(2,1)S(1)}, u32[]{:S(2)}, u32[]{:S(2)}) collective-permute-start(bf16[2,192,512]{2,1,0:T(8,128)(2,1)S(1)} %get-tuple-element.37.own), channel_id=1, source_target_pairs={{0,32},{32,64},{64,96},{96,0},{1,33},{33,65},{65,97},{97,1},{2,34}... | collective-permute-start | bytes 1179656 | tf_op jit(solution)/shard_map/ppermute | solution.py:580
  57.1 8.9 %collective-permute-start.6 = (bf16[208,512]{1,0:T(8,128)(2,1)S(1)}, bf16[208,512]{1,0:T(8,128)(2,1)S(1)}, u32[]{:S(2)}, u32[]{:S(2)}) collective-permute-start(bf16[208,512]{1,0:T(8,128)(2,1)S(1)} %get-tuple-element.39), channel_id=1, source_target_pairs={{0,32},{32,64},{64,96},{96,0},{1,33},{33,65},{65,97},{97,1},{2,34}... | collective-permute-start | bytes 638984 | tf_op jit(solution)/shard_map/ppermute | solution.py:580
  58.0 8.0 %collective-permute-start.7 = (bf16[208,512]{1,0:T(8,128)(2,1)S(1)}, bf16[208,512]{1,0:T(8,128)(2,1)S(1)}, u32[]{:S(2)}, u32[]{:S(2)}) collective-permute-start(bf16[208,512]{1,0:T(8,128)(2,1)S(1)} %get-tuple-element.40), channel_id=1, source_target_pairs={{0,96},{32,0},{64,32},{96,64},{1,97},{33,1},{65,33},{97,65},{2,98}... | collective-permute-start | bytes 638984 | tf_op jit(solution)/shard_map/ppermute | solution.py:580
  60.4 5.6 %collective-permute-start.8 = (f32[1,1,512]{2,1,0:T(1,128)S(1)}, f32[1,1,512]{2,1,0:T(1,128)S(1)}, u32[]{:S(2)}, u32[]{:S(2)}) collective-permute-start(f32[1,1,512]{2,1,0:T(1,128)S(1)} %get-tuple-element.42.row_here), channel_id=1, source_target_pairs={{0,64},{32,96},{64,0},{96,32},{1,65},{33,97},{65,1},{97,33},{2,66}... | collective-permute-start | bytes 6152 | tf_op jit(solution)/shard_map/ppermute | solution.py:580

commit v7 on v6

--- a/solution.py
+++ b/solution.py
@@ -51,33 +51,28 @@
     return lax.dot_general(left, right, (((1,), (0,)), ((), ())), preferred_element_type=f32)
 
 
-def pack_bricks(parts, coords, features, occupancy, act, faces, order):
+def brick_order(coords, order):
     for n in range(16):
         place = ((coords[0, n] % TX) * TY + coords[1, n] % TY) * TZ + coords[2, n]
         order[place] = n
-    picks = cell_chooser()
-    for tx in range(TX):
-        for part, ty in enumerate(parts):
-            halves = []
-            for tz in range(TZ):
-                n = order[(tx * TY + ty) * TZ + tz]
-                gate = occupancy[pl.ds(n, 1), :].astype(f32)
-                gate = jnp.broadcast_to(gate, (LANES, 512)).astype(bf16)
-                halves.append(jnp.concatenate([features[n] * gate[:C], gate[C:]], axis=0))
-            for h in range(4):
-                lanes = slice(128 * h, 128 * h + 128)
-                source = jnp.concatenate([half[:, lanes] for half in halves], axis=1)
-                cells = rows_dot(picks, source).reshape(2, 4, 2, SZ, LANES).astype(bf16)
-                x = 8 * tx + 2 * h
-                act[x : x + 2, part] = cells
-                if faces and ty == 0:
-                    faces[0][x : x + 2] = cells[:, 0, 0]
-                if faces and ty == TY - 1:
-                    faces[1][x : x + 2] = cells[:, 3, 1]
-
-
-def outer_kernel(
-    coords, features, occupancy, act, y_low, y_high, coords_out, gates, order, places, bricks, sems
+
+
+def gated_brick(n, features, occupancy):
+    gate = occupancy[pl.ds(n, 1), :].astype(f32)
+    gate = jnp.broadcast_to(gate, (LANES, 512)).astype(bf16)
+    return jnp.concatenate([features[n] * gate[:C], gate[C:]], axis=0)
+
+
+def side_chooser(j):
+    row = lax.broadcasted_iota(jnp.int32, (128, 1024), 0)
+    lane = lax.broadcasted_iota(jnp.int32, (128, 1024), 1)
+    z = 2 * (row & 7) + ((row >> 3) & 1)
+    source = ((z >> 3) << 9) + ((row >> 4) << 6) + 8 * j + (z & 7)
+    return jnp.where(source == lane, 1.0, 0.0).astype(bf16)
+
+
+def sides_kernel(
+    coords, features, occupancy, y_low, y_high, coords_out, gates, order, places, bricks, sems
 ):
     copies = [
         pltpu.make_async_copy(coords, places, sems.at[0]),
@@ -87,32 +82,31 @@
     ]
     for copy in copies:
         copy.start()
+    choosers = [side_chooser(j) for j in (0, BRICK - 1)]
     for copy in copies:
         copy.wait()
-    pack_bricks((0, TY - 1), places, bricks, gates, act, (y_low, y_high), order)
-
-
-def inner_kernel(coords, features, occupancy, act, order):
-    pack_bricks((1, 2), coords, features, occupancy, act, (), order)
-
-
-ACT = jax.ShapeDtypeStruct((SX, 2, 4, 2, SZ, LANES), bf16)
-
-
-def pack_outer(coords, features, occupancy):
+    brick_order(places, order)
+    for side, ty, picks in ((y_low, 0, choosers[0]), (y_high, TY - 1, choosers[1])):
+        for tx in range(TX):
+            first = (tx * TY + ty) * TZ
+            source = [gated_brick(order[first + tz], bricks, gates) for tz in range(TZ)]
+            cells = rows_dot(picks, jnp.concatenate(source, axis=1))
+            side[8 * tx : 8 * tx + 8] = cells.reshape(8, SZ, LANES).astype(bf16)
+
+
+def pack_sides(coords, features, occupancy):
     side = jax.ShapeDtypeStruct((SX, SZ, LANES), bf16)
     arrays = [pltpu.with_memory_space_constraint(a, pltpu.HBM) for a in (coords, features, occupancy)]
     return pl.pallas_call(
-        outer_kernel,
+        sides_kernel,
         out_shape=(
-            ACT,
             side,
             side,
             jax.ShapeDtypeStruct(coords.shape, jnp.int32),
             jax.ShapeDtypeStruct(occupancy.shape, jnp.int32),
         ),
         in_specs=[HBM] * 3,
-        out_specs=(VMEM,) * 5,
+        out_specs=(VMEM,) * 4,
         scratch_shapes=[
             pltpu.SMEM((16,), jnp.int32),
             pltpu.SMEM((3, 16), jnp.int32),
@@ -120,40 +114,55 @@
             pltpu.SemaphoreType.DMA((4,)),
         ],
         compiler_params=params(12),
-        name="pack_outer",
+        name="pack_sides",
     )(*arrays)
 
 
-def pack_inner(coords, features, occupancy):
-    return pl.pallas_call(
-        inner_kernel,
-        out_shape=ACT,
+def pack_kernel(coords, features, occupancy, act, order):
+    brick_order(coords, order)
+    picks = cell_chooser()
+    for tx in range(TX):
+        for ty in range(TY):
+            first = (tx * TY + ty) * TZ
+            halves = [gated_brick(order[first + tz], features, occupancy) for tz in range(TZ)]
+            for h in range(4):
+                lanes = slice(128 * h, 128 * h + 128)
+                source = jnp.concatenate([half[:, lanes] for half in halves], axis=1)
+                cells = rows_dot(picks, source).reshape(2, 4, 2, SZ, LANES)
+                x = 8 * tx + 2 * h
+                act[x : x + 2, 4 * ty : 4 * ty + 4] = cells.astype(bf16)
+
+
+def pack(coords, features, occupancy):
+    return pl.pallas_call(
+        pack_kernel,
+        out_shape=jax.ShapeDtypeStruct((SX, PAIRS, 2, SZ, LANES), bf16),
         in_specs=[SMEM, VMEM, VMEM],
         out_specs=VMEM,
         scratch_shapes=[pltpu.SMEM((16,), jnp.int32)],
         compiler_params=params(12),
-        name="pack_inner",
+        name="pack",
     )(coords, features, occupancy)
 
 
-def face_kernel(outer, inner, y_before, y_after, low, high):
+def face_kernel(act, y_before, y_after, low, high):
     tile_y = lax.axis_index("space") % GRID_Y
     for face, x in ((low, 0), (high, SX - 1)):
         face[0] = kept(y_before[x], tile_y > 0)
-        face[1 : SY + 1] = plane_of(outer, inner, x).reshape(SY, SZ, LANES)
+        face[1 : SY + 1] = act[x].reshape(SY, SZ, LANES)
         face[SY + 1] = kept(y_after[x], tile_y < GRID_Y - 1)
 
 
-def faces(outer, inner, y_before, y_after):
+def faces(act, y_before, y_after):
     face = jax.ShapeDtypeStruct((SY + 2, SZ, LANES), bf16)
     return pl.pallas_call(
         face_kernel,
         out_shape=(face, face),
-        in_specs=[VMEM] * 4,
+        in_specs=[VMEM] * 3,
         out_specs=(VMEM, VMEM),
         compiler_params=params(8),
         name="faces",
-    )(outer, inner, y_before, y_after)
+    )(act, y_before, y_after)
 
 
 def window_forms(a, b, c, d):
@@ -171,10 +180,6 @@
     return [jnp.stack(pair, axis=1).reshape(PAIRS, SZ, WIDE).astype(bf16) for pair in pairs]
 
 
-def plane_of(outer, inner, x):
-    return jnp.concatenate([outer[x, 0], inner[x, 0], inner[x, 1], outer[x, 1]], axis=0)
-
-
 def kept(value, inside):
     return value * jnp.where(inside, 1.0, 0.0).astype(bf16)
 
@@ -222,13 +227,13 @@
     return mean, folded(jnp.sum(gap * gap, axis=0, keepdims=True)), count
 
 
-def middle_kernel(outer, inner, y_before, y_after, weight, out, partial, stats, taps, grid):
+def middle_kernel(act, y_before, y_after, weight, out, partial, stats, taps, grid):
     tile_y = lax.axis_index("space") % GRID_Y
 
     def fill(x):
         before = kept(y_before[x], tile_y > 0)[None]
         after = kept(y_after[x], tile_y < GRID_Y - 1)[None]
-        plane = plane_of(outer, inner, x)
+        plane = act[x]
         even, odd = plane[:, 0], plane[:, 1]
         forms = window_forms(
             jnp.concatenate([before, odd[:-1]], axis=0),
@@ -258,14 +263,14 @@
         pieces = [grid[c, x + a : x + a + STEP] for a in range(3) for c in range(3)]
         value = planes_dot(pieces, taps[...])
         out[x : x + STEP] = value.reshape(STEP, PAIRS * SZ, 2 * LANES)
-        mask = planes_mask([plane_of(outer, inner, x + 1 + step) for step in range(STEP)])
+        mask = planes_mask([act[x + 1 + step] for step in range(STEP)])
         carry = merged(carry, moments_of(value, mask))
     pieces = [grid[c, SX - 2 + a] for a in range(2) for c in range(3)]
     partial[1] = planes_dot(pieces, taps[: 6 * WIDE])
     stats[...] = jnp.concatenate(list(carry) + [jnp.zeros((5, LANES), f32)], axis=0)
 
 
-def middle(outer, inner, y_before, y_after, weight):
+def middle(act, y_before, y_after, weight):
     return pl.pallas_call(
         middle_kernel,
         out_shape=(
@@ -274,15 +279,15 @@
             jax.ShapeDtypeStruct((8, LANES), f32),
             jax.ShapeDtypeStruct((9 * WIDE, 2 * LANES), bf16),
         ),
-        in_specs=[VMEM] * 5,
+        in_specs=[VMEM] * 4,
         out_specs=(VMEM,) * 4,
         scratch_shapes=[pltpu.VMEM((3, SX, PAIRS, SZ, WIDE), bf16)],
         compiler_params=params(26),
         name="middle",
-    )(outer, inner, y_before, y_after, weight)
-
-
-def edge_kernel(outer, inner, x_before, x_after, partial, taps, part, owners, out, stats):
+    )(act, y_before, y_after, weight)
+
+
+def edge_kernel(act, x_before, x_after, partial, taps, part, owners, out, stats):
     tile_x = lax.axis_index("space") // GRID_Y
     last_x = lax.axis_size("space") // GRID_Y - 1
     carry = (part[0:1], part[1:2], part[2:3])
@@ -292,7 +297,7 @@
         forms = window_forms(cells[:-1, 0], cells[:-1, 1], cells[1:, 0], cells[1:, 1])
         value = partial[index] + planes_dot(forms, taps[first : first + 3 * WIDE])
         out[index] = value
-        carry = merged(carry, moments_of(value, planes_mask([plane_of(outer, inner, x)])))
+        carry = merged(carry, moments_of(value, planes_mask([act[x]])))
     joint, square, both = carry
     lane = lax.broadcasted_iota(jnp.int32, (1, LANES), 1)
     joint = jnp.where(lane == LANES - 1, both, joint)
@@ -302,18 +307,18 @@
     stats[...] = jnp.broadcast_to(row[None], stats.shape)
 
 
-def edges(outer, inner, x_before, x_after, partial, taps, part, owners, devices):
+def edges(act, x_before, x_after, partial, taps, part, owners, devices):
     return pl.pallas_call(
         edge_kernel,
         out_shape=(
             jax.ShapeDtypeStruct((2, PAIRS * SZ, 2 * LANES), f32),
             jax.ShapeDtypeStruct((devices, 1, 2 * LANES), f32),
         ),
-        in_specs=[VMEM] * 7 + [SMEM],
+        in_specs=[VMEM] * 6 + [SMEM],
         out_specs=(VMEM, VMEM),
         compiler_params=params(16),
         name="edges",
-    )(outer, inner, x_before, x_after, partial, taps, part, owners)
+    )(act, x_before, x_after, partial, taps, part, owners)
 
 
 def joined(table, width):
@@ -326,7 +331,7 @@
 
 
 def section_kernel(
-    mid, edge, outer, inner, table, gain, shift, weight, sent, names, stats, taps, down, cover, lines
+    mid, edge, act, table, gain, shift, weight, sent, names, stats, taps, down, cover, lines
 ):
     level, groups = lax.axis_index("level"), lax.axis_size("level")
     for distance in range(4):
@@ -358,7 +363,7 @@
             for a in range(2):
                 x = 2 * X + a
                 conv = edge[0] if x == 0 else edge[1] if x == SX - 1 else mid[x - 1]
-                plane = plane_of(outer, inner, x)
+                plane = act[x]
                 even, odd = rows_of([plane], 0), rows_of([plane], 1)
                 even_mask, odd_mask = mask_of(even), mask_of(odd)
                 mask = jnp.concatenate([even_mask, odd_mask], axis=1)
@@ -387,25 +392,22 @@
         gap = (down[X] - mean2) * cover[X]
         return carry + jnp.sum(gap * gap, axis=0, keepdims=True)
 
-    square = lax.fori_loop(0, SX // 2, spread_out, zero)
+    square = zero
+    for X in range(SX // 2):
+        square = spread_out(X, square)
     wide_lane = lax.broadcasted_iota(jnp.int32, (1, 2 * LANES), 1)
     row = jnp.concatenate([jnp.where(wide_lane == 2 * LANES - 1, count, mean2), square], axis=1)
     stats[...] = jnp.broadcast_to(row[None], stats.shape)
 
-    unit = (
-        lax.broadcasted_iota(jnp.int32, (C2, 2 * LANES), 0)
-        == lax.broadcasted_iota(jnp.int32, (C2, 2 * LANES), 1)
-    )
-    unit = jnp.where(unit, 1.0, 0.0).astype(bf16)
     half = PAIRS // 2 * 8
     for q in range(2):
         value = down[:, q * half : (q + 1) * half].reshape(SX // 2 * half, 2 * LANES)
         covered = cover[:, q * half : (q + 1) * half].reshape(SX // 2 * half, 2 * LANES)
         coded = jnp.where(covered > 0, value, EMPTY).astype(bf16)
-        sent[q] = rows_dot(unit, coded).astype(bf16)
-
-
-def section(mid, edge, outer, inner, table, gain, shift, weight, devices):
+        sent[q] = coded.T[:C2]
+
+
+def section(mid, edge, act, table, gain, shift, weight, devices):
     return pl.pallas_call(
         section_kernel,
         out_shape=(
@@ -413,7 +415,7 @@
             jax.ShapeDtypeStruct((4, 1, LANES), f32),
             jax.ShapeDtypeStruct((devices, 1, 4 * LANES), f32),
         ),
-        in_specs=[VMEM] * 8,
+        in_specs=[VMEM] * 7,
         out_specs=(VMEM,) * 3,
         scratch_shapes=[
             pltpu.VMEM((8 * LANES, 2 * LANES), bf16),
@@ -423,7 +425,7 @@
         ],
         compiler_params=params(20),
         name="section",
-    )(mid, edge, outer, inner, table, gain, shift, weight)
+    )(mid, edge, act, table, gain, shift, weight)
 
 
 def merge_kernel(table, near, back, out, up, down):
@@ -545,17 +547,16 @@
             route.append(((x + step_x) % grid_x * GRID_Y + (y + step_y) % GRID_Y, s))
         return lax.ppermute(block, "space", route)
 
-    outer, y_low, y_high, coords, gates = pack_outer(brick_coords, features, occupancy)
+    y_low, y_high, coords, gates = pack_sides(brick_coords, features, occupancy)
     y_before = from_tile(y_high, 0, -1)
     y_after = from_tile(y_low, 0, 1)
-    inner = pack_inner(coords, features, gates)
-    x_low, x_high = faces(outer, inner, y_before, y_after)
+    act = pack(coords, features, gates)
+    x_low, x_high = faces(act, y_before, y_after)
     x_before = from_tile(x_high, -1, 0)
     x_after = from_tile(x_low, 1, 0)
-    mid, partial, part, taps = middle(outer, inner, y_before, y_after, conv_weight)
+    mid, partial, part, taps = middle(act, y_before, y_after, conv_weight)
     edge, stats = edges(
-        outer,
-        inner,
+        act,
         x_before,
         x_after,
         partial,
@@ -567,8 +568,7 @@
     sent, names, stats2 = section(
         mid,
         edge,
-        outer,
-        inner,
+        act,
         to_all(stats, ("level", "space")),
         conv_gain[None],
         conv_shift[None],

time: 68.6 us -> 67.8 us (0.988)
  transfers between devices with their start and end apart: 9 -> 9, of which waited for: 2 -> 1; matrix products, arithmetic and copies ran while one was open for 0% -> 0% of each run, Pallas kernels for 14% -> 15%
where the time goes in v7:
time: 67.8 us; the launch traced here: 67.6 us
  blocking collectives  29.9 us (44%)
  Pallas kernels  18.7 us (28%)
  starting transfers between devices  13.3 us (20%)
  waiting for transfers between devices  5.31 us (8%)
    all_to_all x2, blocking collectives, to_all(): return lax.all_to_all(rows, axes, 0, 0, tiled=True)  29.9 us
    pallas_call x1, Pallas kernels, middle(): pl.pallas_call(middle_kernel, out_shape=(pltpu.VMEM((MID, PAIRS * SZ, 2 *...  8.37 us
    ppermute x4, starting transfers between devices, from_tile(): return lax.ppermute(block, 'space', route)  7.52 us
    ppermute x5, starting transfers between devices, up_level(): return lax.ppermute(block, 'level', route)  5.74 us
    ppermute x5, waiting for transfers between devices, up_level(): return lax.ppermute(block, 'level', route)  5.3 us
    pallas_call x1, Pallas kernels, section(): pl.pallas_call(section_kernel, out_shape=(jax.ShapeDtypeStruct((2, C2, 51...  2.64 us
    pallas_call x1, Pallas kernels, settle(): pl.pallas_call(settle_kernel, out_shape=jax.ShapeDtypeStruct((8, C2, 512)...  2.21 us
    pallas_call x1, Pallas kernels, pack_sides(): pl.pallas_call(sides_kernel, out_shape=(side, side, jax.ShapeDtypeStruct(...  2.04 us
  transfers between devices with their start and end apart: 9, of which 1 were waited for; matrix products, arithmetic and copies ran while one was open for 0% of the time, Pallas kernels for 15%

profile of v7, /device:TPU:0, one launch (start us, length us, event | category | flops | bytes accessed | tf_op | source)
XLA Modules:
  0.0 67.6 jit_solution(3381547874936051514)
XLA Ops:
  0.0 0.0 copy-start
  0.0 2.0 %pack_sides.1 = (bf16[16,16,128]{2,1,0:T(8,128)(2,1)S(1)}, bf16[16,16,128]{2,1,0:T(8,128)(2,1)S(1)}, s32[3,16]{1,0:T(4,128)S(1)}, s32[16,512]{1,0:T(8,128)S(1)}) custom-call(s32[3,16]{1,0:T(4,128)} %coords.1, bf16[16,96,512]{2,1,0:T(8,128)(2,1)} %features.3, s32[16,512]{1,0:T(8,128)} %occupancy.1), custom_call_target="tpu_custom_call" | custom-call | tf_op jit(solution)/shard_map/pack_sides/pallas_call | solution.py:100
  2.1 0.1 collective-permute-start
  2.1 1.7 %collective-permute-start.1 = (bf16[16,16,128]{2,1,0:T(8,128)(2,1)S(1)}, bf16[16,16,128]{2,1,0:T(8,128)(2,1)S(1)}, u32[]{:S(2)}, u32[]{:S(2)}) collective-permute-start(bf16[16,16,128]{2,1,0:T(8,128)(2,1)S(1)} %get-tuple-element.26), channel_id=1, source_target_pairs={{1,0},{2,1},{3,2},{0,3},{5,4},{6,5},{7,6},{4,7},{9,8},{10,9},{11,1... | collective-permute-start | bytes 196616 | tf_op jit(solution)/shard_map/ppermute | solution.py:548
  3.9 0.0 copy-done
  3.9 2.0 %pack.1.act = bf16[16,16,2,16,128]{4,3,2,1,0:T(8,128)(2,1)S(1)} custom-call(s32[3,16]{1,0:T(4,128)S(1)} %get-tuple-element.23.coords, bf16[16,96,512]{2,1,0:T(8,128)(2,1)S(1)} %copy-done, s32[16,512]{1,0:T(8,128)S(1)} %get-tuple-element.24.occupancy), custom_call_target="tpu_custom_call" | custom-call | tf_op jit(solution)/shard_map/pack/pallas_call | solution.py:137
  5.8 0.0 copy-start.7
  5.8 0.0 copy-start.1
  5.9 0.0 collective-permute-done.y_before
  5.9 0.0 collective-permute-done.1.y_after
  5.9 3.3 %collective-permute-start.2 = (bf16[34,16,128]{2,1,0:T(8,128)(2,1)S(1)}, bf16[34,16,128]{2,1,0:T(8,128)(2,1)S(1)}, u32[]{:S(2)}, u32[]{:S(2)}) collective-permute-start(bf16[34,16,128]{2,1,0:T(8,128)(2,1)S(1)} %get-tuple-element.28), channel_id=1, source_target_pairs={{28,0},{29,1},{30,2},{31,3},{0,4},{1,5},{2,6},{3,7},{4,8},{5,9},{6... | collective-permute-start | bytes 417800 | tf_op jit(solution)/shard_map/ppermute | solution.py:548
  9.3 2.4 %collective-permute-start.3 = (bf16[34,16,128]{2,1,0:T(8,128)(2,1)S(1)}, bf16[34,16,128]{2,1,0:T(8,128)(2,1)S(1)}, u32[]{:S(2)}, u32[]{:S(2)}) collective-permute-start(bf16[34,16,128]{2,1,0:T(8,128)(2,1)S(1)} %get-tuple-element.29), channel_id=1, source_target_pairs={{4,0},{5,1},{6,2},{7,3},{8,4},{9,5},{10,6},{11,7},{12,8},{13,9},{1... | collective-permute-start | bytes 417800 | tf_op jit(solution)/shard_map/ppermute | solution.py:548
  11.6 0.0 copy-done.7
  11.6 0.1 copy.11.owners
  11.7 0.0 copy-done.1
  11.7 8.4 %middle.1 = (f32[14,256,256]{2,1,0:T(8,128)S(1)}, f32[2,256,256]{2,1,0:T(8,128)S(1)}, f32[8,128]{1,0:T(8,128)S(1)}, bf16[3456,256]{1,0:T(8,128)(2,1)S(1)}) custom-call(bf16[16,16,2,16,128]{4,3,2,1,0:T(8,128)(2,1)S(1)} %pack.1.act, bf16[16,16,128]{2,1,0:T(8,128)(2,1)S(1)} %collective-permute-done.y_before, ...), custom_call_target="tpu_custom_call" | custom-call | tf_op jit(solution)/shard_map/middle/pallas_call | solution.py:274
  20.1 0.0 collective-permute-done.2.x_before
  20.1 0.0 collective-permute-done.3.x_after
  20.1 0.0 copy-start.2
  20.1 0.0 copy-start.5
  20.1 0.0 copy-start.6
  20.2 1.3 %edges.1 = (f32[2,256,256]{2,1,0:T(8,128)S(1)}, f32[128,1,256]{2,1,0:T(1,128)S(1)}) custom-call(bf16[16,16,2,16,128]{4,3,2,1,0:T(8,128)(2,1)S(1)} %pack.1.act, bf16[34,16,128]{2,1,0:T(8,128)(2,1)S(1)} %collective-permute-done.2.x_before, bf16[34,16,128]{2,1,0:T(8,128)(2,1)S(1)} %collective-permute-done.3.x_after, ...), custom_call_target="tpu_custom_call" | custom-call | tf_op jit(solution)/shard_map/edges/pallas_call | solution.py:311
  21.5 18.9 %all_to_all.10.table = f32[128,1,256]{2,1,0:T(1,128)S(1)} all-to-all(f32[128,1,256]{2,1,0:T(1,128)S(1)} %get-tuple-element.34), channel_id=1, replica_groups=mesh['level'=4,'space'=32] {'level','space'}, dimensions={0} | all-to-all | bytes 262144 | tf_op jit(solution)/shard_map/all_to_all | solution.py:524
  40.4 0.0 copy-done.2
  40.4 0.0 copy-done.5
  40.4 0.0 copy-done.6
  40.4 0.0 copy-start.3
  40.4 0.0 copy-start.4
  40.4 2.6 %section.1 = (bf16[2,192,512]{2,1,0:T(8,128)(2,1)S(1)}, f32[4,1,128]{2,1,0:T(1,128)S(1)}, f32[32,1,512]{2,1,0:T(1,128)S(1)}) custom-call(f32[14,256,256]{2,1,0:T(8,128)S(1)} %get-tuple-element.27.mid, f32[2,256,256]{2,1,0:T(8,128)S(1)} %get-tuple-element.33.edge, bf16[16,16,2,16,128]{4,3,2,1,0:T(8,128)(2,1)S(1)} %pack.1.act, ...), custom_call_target="tpu_custom_call" | custom-call | tf_op jit(solution)/shard_map/section/pallas_call | solution.py:411
  43.0 1.0 %collective-permute-start.5 = (bf16[2,192,512]{2,1,0:T(8,128)(2,1)S(1)}, bf16[2,192,512]{2,1,0:T(8,128)(2,1)S(1)}, u32[]{:S(2)}, u32[]{:S(2)}) collective-permute-start(bf16[2,192,512]{2,1,0:T(8,128)(2,1)S(1)} %get-tuple-element.35.own), channel_id=1, source_target_pairs={{0,96},{32,0},{64,32},{96,64},{1,97},{33,1},{65,33},{97,65},{2,98}... | collective-permute-start | bytes 1179656 | tf_op jit(solution)/shard_map/ppermute | solution.py:580
  44.0 1.1 %collective-permute-start.4 = (bf16[2,192,512]{2,1,0:T(8,128)(2,1)S(1)}, bf16[2,192,512]{2,1,0:T(8,128)(2,1)S(1)}, u32[]{:S(2)}, u32[]{:S(2)}) collective-permute-start(bf16[2,192,512]{2,1,0:T(8,128)(2,1)S(1)} %get-tuple-element.35.own), channel_id=1, source_target_pairs={{0,32},{32,64},{64,96},{96,0},{1,33},{33,65},{65,97},{97,1},{2,34}... | collective-permute-start | bytes 1179656 | tf_op jit(solution)/shard_map/ppermute | solution.py:580
  45.1 11.0 %all_to_all.11.table = f32[32,1,512]{2,1,0:T(1,128)S(1)} all-to-all(f32[32,1,512]{2,1,0:T(1,128)S(1)} %get-tuple-element.36), channel_id=1, replica_groups=mesh['level'=4,'space'=32] {'space'}, dimensions={0} | all-to-all | bytes 131072 | tf_op jit(solution)/shard_map/all_to_all | solution.py:524
  56.1 0.0 collective-permute-done.5.back
  56.1 0.0 collective-permute-done.4.near
  56.1 0.2 merge.1
  56.3 0.9 %collective-permute-start.6 = (bf16[208,512]{1,0:T(8,128)(2,1)S(1)}, bf16[208,512]{1,0:T(8,128)(2,1)S(1)}, u32[]{:S(2)}, u32[]{:S(2)}) collective-permute-start(bf16[208,512]{1,0:T(8,128)(2,1)S(1)} %get-tuple-element.37), channel_id=1, source_target_pairs={{0,32},{32,64},{64,96},{96,0},{1,33},{33,65},{65,97},{97,1},{2,34}... | collective-permute-start | bytes 638984 | tf_op jit(solution)/shard_map/ppermute | solution.py:580
  57.2 2.4 %collective-permute-start.7 = (bf16[208,512]{1,0:T(8,128)(2,1)S(1)}, bf16[208,512]{1,0:T(8,128)(2,1)S(1)}, u32[]{:S(2)}, u32[]{:S(2)}) collective-permute-start(bf16[208,512]{1,0:T(8,128)(2,1)S(1)} %get-tuple-element.38), channel_id=1, source_target_pairs={{0,96},{32,0},{64,32},{96,64},{1,97},{33,1},{65,33},{97,65},{2,98}... | collective-permute-start | bytes 638984 | tf_op jit(solution)/shard_map/ppermute | solution.py:580
  59.6 0.3 collective-permute-start.8
  60.0 5.3 %collective-permute-done.8.row_far = f32[1,1,512]{2,1,0:T(1,128)S(1)} collective-permute-done((f32[1,1,512]{2,1,0:T(1,128)S(1)}, f32[1,1,512]{2,1,0:T(1,128)S(1)}, u32[]{:S(2)}, u32[]{:S(2)}) %collective-permute-start.8) | collective-permute-done | bytes 2080 | tf_op jit(solution)/shard_map/ppermute | solution.py:580
  65.2 0.0 collective-permute-done.6.far0
  65.3 0.0 collective-permute-done.7.far1
  65.3 0.0 copy-done.3
  65.3 0.0 copy-done.4
  65.3 2.2 %settle.1 = bf16[8,192,512]{2,1,0:T(8,128)(2,1)} custom-call(bf16[2,192,512]{2,1,0:T(8,128)(2,1)S(1)} %get-tuple-element.35.own, bf16[2,192,512]{2,1,0:T(8,128)(2,1)S(1)} %collective-permute-done.4.near, bf16[208,512]{1,0:T(8,128)(2,1)S(1)} %collective-permute-done.6.far0, bf16[208,512]{1,0:T(8,128)(2,1)S(1)} %collective-permute-done.7.far1, ...), custom_call_target="tpu_custom_call" | custom-call | tf_op jit(solution)/shard_map/settle/pallas_call | solution.py:508
  (1 shorter events, 0.0 us)
Async XLA Ops:
  0.0 3.9 %copy-start = (bf16[16,96,512]{2,1,0:T(8,128)(2,1)S(1)}, bf16[16,96,512]{2,1,0:T(8,128)(2,1)}, u32[]{:S(2)}) copy-start(bf16[16,96,512]{2,1,0:T(8,128)(2,1)} %features.3) | copy-start | bytes 4718596
  2.1 3.8 %collective-permute-start = (bf16[16,16,128]{2,1,0:T(8,128)(2,1)S(1)}, bf16[16,16,128]{2,1,0:T(8,128)(2,1)S(1)}, u32[]{:S(2)}, u32[]{:S(2)}) collective-permute-start(bf16[16,16,128]{2,1,0:T(8,128)(2,1)S(1)} %get-tuple-element.25), channel_id=1, source_target_pairs={{3,0},{0,1},{1,2},{2,3},{7,4},{4,5},{5,6},{6,7},{11,8},{8,9},{9,10... | collective-permute-start | bytes 196616 | tf_op jit(solution)/shard_map/ppermute | solution.py:548
  2.1 3.7 %collective-permute-start.1 = (bf16[16,16,128]{2,1,0:T(8,128)(2,1)S(1)}, bf16[16,16,128]{2,1,0:T(8,128)(2,1)S(1)}, u32[]{:S(2)}, u32[]{:S(2)}) collective-permute-start(bf16[16,16,128]{2,1,0:T(8,128)(2,1)S(1)} %get-tuple-element.26), channel_id=1, source_target_pairs={{1,0},{2,1},{3,2},{0,3},{5,4},{6,5},{7,6},{4,7},{9,8},{10,9},{11,1... | collective-permute-start | bytes 196616 | tf_op jit(solution)/shard_map/ppermute | solution.py:548
  5.8 5.8 %copy-start.7 = (s32[2,1]{0,1:T(1,128)S(1)}, s32[2,1]{0,1:T(1,128)}, u32[]{:S(2)}) copy-start(s32[2,1]{0,1:T(1,128)} %param.13) | copy-start | bytes 28
  5.8 5.9 %copy-start.1 = (bf16[27,96,96]{2,1,0:T(8,128)(2,1)S(1)}, bf16[27,96,96]{2,1,0:T(8,128)(2,1)}, u32[]{:S(2)}) copy-start(bf16[27,96,96]{2,1,0:T(8,128)(2,1)} %weight.2) | copy-start | bytes 1492996
  5.9 14.2 %collective-permute-start.2 = (bf16[34,16,128]{2,1,0:T(8,128)(2,1)S(1)}, bf16[34,16,128]{2,1,0:T(8,128)(2,1)S(1)}, u32[]{:S(2)}, u32[]{:S(2)}) collective-permute-start(bf16[34,16,128]{2,1,0:T(8,128)(2,1)S(1)} %get-tuple-element.28), channel_id=1, source_target_pairs={{28,0},{29,1},{30,2},{31,3},{0,4},{1,5},{2,6},{3,7},{4,8},{5,9},{6... | collective-permute-start | bytes 417800 | tf_op jit(solution)/shard_map/ppermute | solution.py:548
  9.3 10.8 %collective-permute-start.3 = (bf16[34,16,128]{2,1,0:T(8,128)(2,1)S(1)}, bf16[34,16,128]{2,1,0:T(8,128)(2,1)S(1)}, u32[]{:S(2)}, u32[]{:S(2)}) collective-permute-start(bf16[34,16,128]{2,1,0:T(8,128)(2,1)S(1)} %get-tuple-element.29), channel_id=1, source_target_pairs={{4,0},{5,1},{6,2},{7,3},{8,4},{9,5},{10,6},{11,7},{12,8},{13,9},{1... | collective-permute-start | bytes 417800 | tf_op jit(solution)/shard_map/ppermute | solution.py:548
  20.1 20.2 %copy-start.2 = (bf16[8,192,96]{2,1,0:T(8,128)(2,1)S(1)}, bf16[8,192,96]{2,1,0:T(8,128)(2,1)}, u32[]{:S(2)}) copy-start(bf16[8,192,96]{2,1,0:T(8,128)(2,1)} %weight.3) | copy-start | bytes 884740
  20.1 20.2 %copy-start.5 = (f32[96]{0:T(128)S(1)}, f32[96]{0:T(128)}, u32[]{:S(2)}) copy-start(f32[96]{0:T(128)} %param.15) | copy-start | bytes 1156
  20.1 20.2 %copy-start.6 = (f32[96]{0:T(128)S(1)}, f32[96]{0:T(128)}, u32[]{:S(2)}) copy-start(f32[96]{0:T(128)} %param.16) | copy-start | bytes 1156
  40.4 24.9 %copy-start.3 = (f32[192]{0:T(256)S(1)}, f32[192]{0:T(256)}, u32[]{:S(2)}) copy-start(f32[192]{0:T(256)} %param.18) | copy-start | bytes 2308
  40.4 24.9 %copy-start.4 = (f32[192]{0:T(256)S(1)}, f32[192]{0:T(256)}, u32[]{:S(2)}) copy-start(f32[192]{0:T(256)} %param.19) | copy-start | bytes 2308
  43.0 13.1 %collective-permute-start.5 = (bf16[2,192,512]{2,1,0:T(8,128)(2,1)S(1)}, bf16[2,192,512]{2,1,0:T(8,128)(2,1)S(1)}, u32[]{:S(2)}, u32[]{:S(2)}) collective-permute-start(bf16[2,192,512]{2,1,0:T(8,128)(2,1)S(1)} %get-tuple-element.35.own), channel_id=1, source_target_pairs={{0,96},{32,0},{64,32},{96,64},{1,97},{33,1},{65,33},{97,65},{2,98}... | collective-permute-start | bytes 1179656 | tf_op jit(solution)/shard_map/ppermute | solution.py:580
  44.0 12.1 %collective-permute-start.4 = (bf16[2,192,512]{2,1,0:T(8,128)(2,1)S(1)}, bf16[2,192,512]{2,1,0:T(8,128)(2,1)S(1)}, u32[]{:S(2)}, u32[]{:S(2)}) collective-permute-start(bf16[2,192,512]{2,1,0:T(8,128)(2,1)S(1)} %get-tuple-element.35.own), channel_id=1, source_target_pairs={{0,32},{32,64},{64,96},{96,0},{1,33},{33,65},{65,97},{97,1},{2,34}... | collective-permute-start | bytes 1179656 | tf_op jit(solution)/shard_map/ppermute | solution.py:580
  56.3 8.9 %collective-permute-start.6 = (bf16[208,512]{1,0:T(8,128)(2,1)S(1)}, bf16[208,512]{1,0:T(8,128)(2,1)S(1)}, u32[]{:S(2)}, u32[]{:S(2)}) collective-permute-start(bf16[208,512]{1,0:T(8,128)(2,1)S(1)} %get-tuple-element.37), channel_id=1, source_target_pairs={{0,32},{32,64},{64,96},{96,0},{1,33},{33,65},{65,97},{97,1},{2,34}... | collective-permute-start | bytes 638984 | tf_op jit(solution)/shard_map/ppermute | solution.py:580
  57.2 8.0 %collective-permute-start.7 = (bf16[208,512]{1,0:T(8,128)(2,1)S(1)}, bf16[208,512]{1,0:T(8,128)(2,1)S(1)}, u32[]{:S(2)}, u32[]{:S(2)}) collective-permute-start(bf16[208,512]{1,0:T(8,128)(2,1)S(1)} %get-tuple-element.38), channel_id=1, source_target_pairs={{0,96},{32,0},{64,32},{96,64},{1,97},{33,1},{65,33},{97,65},{2,98}... | collective-permute-start | bytes 638984 | tf_op jit(solution)/shard_map/ppermute | solution.py:580
  59.6 5.6 %collective-permute-start.8 = (f32[1,1,512]{2,1,0:T(1,128)S(1)}, f32[1,1,512]{2,1,0:T(1,128)S(1)}, u32[]{:S(2)}, u32[]{:S(2)}) collective-permute-start(f32[1,1,512]{2,1,0:T(1,128)S(1)} %get-tuple-element.40.row_here), channel_id=1, source_target_pairs={{0,64},{32,96},{64,0},{96,32},{1,65},{33,97},{65,1},{97,33},{2,66}... | collective-permute-start | bytes 6152 | tf_op jit(solution)/shard_map/ppermute | solution.py:580

commit v8 on v7

--- a/solution.py
+++ b/solution.py
@@ -118,7 +118,7 @@
     )(*arrays)
 
 
-def pack_kernel(coords, features, occupancy, act, order):
+def pack_kernel(coords, features, occupancy, act, masks, cover, order):
     brick_order(coords, order)
     picks = cell_chooser()
     for tx in range(TX):
@@ -131,14 +131,27 @@
                 cells = rows_dot(picks, source).reshape(2, 4, 2, SZ, LANES)
                 x = 8 * tx + 2 * h
                 act[x : x + 2, 4 * ty : 4 * ty + 4] = cells.astype(bf16)
+    for X in range(SX // 2):
+        covers = []
+        for x in (2 * X, 2 * X + 1):
+            even, odd = mask_of(rows_of([act[x]], 0)), mask_of(rows_of([act[x]], 1))
+            masks[x] = jnp.concatenate([even, odd], axis=1).astype(bf16)
+            both = jnp.maximum(even, odd).reshape(PAIRS, 2, 8, LANES)
+            covers.append(jnp.maximum(both[:, 0], both[:, 1]).reshape(PAIRS * 8, LANES))
+        covered = jnp.maximum(covers[0], covers[1])
+        cover[X] = jnp.concatenate([covered, covered], axis=1)
 
 
 def pack(coords, features, occupancy):
     return pl.pallas_call(
         pack_kernel,
-        out_shape=jax.ShapeDtypeStruct((SX, PAIRS, 2, SZ, LANES), bf16),
+        out_shape=(
+            jax.ShapeDtypeStruct((SX, PAIRS, 2, SZ, LANES), bf16),
+            jax.ShapeDtypeStruct((SX, PAIRS * SZ, 2 * LANES), bf16),
+            jax.ShapeDtypeStruct((SX // 2, PAIRS * 8, 2 * LANES), f32),
+        ),
         in_specs=[SMEM, VMEM, VMEM],
-        out_specs=VMEM,
+        out_specs=(VMEM,) * 3,
         scratch_shapes=[pltpu.SMEM((16,), jnp.int32)],
         compiler_params=params(12),
         name="pack",
@@ -199,10 +212,6 @@
     ).astype(f32)
 
 
-def planes_mask(planes):
-    return jnp.concatenate([mask_of(rows_of(planes, 0)), mask_of(rows_of(planes, 1))], axis=1)
-
-
 def folded(row):
     return row[:, :LANES] + row[:, LANES:]
 
@@ -227,7 +236,7 @@
     return mean, folded(jnp.sum(gap * gap, axis=0, keepdims=True)), count
 
 
-def middle_kernel(act, y_before, y_after, weight, out, partial, stats, taps, grid):
+def middle_kernel(act, masks, y_before, y_after, weight, out, partial, stats, taps, grid):
     tile_y = lax.axis_index("space") % GRID_Y
 
     def fill(x):
@@ -263,14 +272,14 @@
         pieces = [grid[c, x + a : x + a + STEP] for a in range(3) for c in range(3)]
         value = planes_dot(pieces, taps[...])
         out[x : x + STEP] = value.reshape(STEP, PAIRS * SZ, 2 * LANES)
-        mask = planes_mask([act[x + 1 + step] for step in range(STEP)])
+        mask = masks[x + 1 : x + 1 + STEP].reshape(STEP * PAIRS * SZ, 2 * LANES).astype(f32)
         carry = merged(carry, moments_of(value, mask))
     pieces = [grid[c, SX - 2 + a] for a in range(2) for c in range(3)]
     partial[1] = planes_dot(pieces, taps[: 6 * WIDE])
     stats[...] = jnp.concatenate(list(carry) + [jnp.zeros((5, LANES), f32)], axis=0)
 
 
-def middle(act, y_before, y_after, weight):
+def middle(act, masks, y_before, y_after, weight):
     return pl.pallas_call(
         middle_kernel,
         out_shape=(
@@ -279,15 +288,15 @@
             jax.ShapeDtypeStruct((8, LANES), f32),
             jax.ShapeDtypeStruct((9 * WIDE, 2 * LANES), bf16),
         ),
-        in_specs=[VMEM] * 4,
+        in_specs=[VMEM] * 5,
         out_specs=(VMEM,) * 4,
         scratch_shapes=[pltpu.VMEM((3, SX, PAIRS, SZ, WIDE), bf16)],
         compiler_params=params(26),
         name="middle",
-    )(act, y_before, y_after, weight)
-
-
-def edge_kernel(act, x_before, x_after, partial, taps, part, owners, out, stats):
+    )(act, masks, y_before, y_after, weight)
+
+
+def edge_kernel(masks, x_before, x_after, partial, taps, part, owners, out, stats):
     tile_x = lax.axis_index("space") // GRID_Y
     last_x = lax.axis_size("space") // GRID_Y - 1
     carry = (part[0:1], part[1:2], part[2:3])
@@ -297,17 +306,17 @@
         forms = window_forms(cells[:-1, 0], cells[:-1, 1], cells[1:, 0], cells[1:, 1])
         value = partial[index] + planes_dot(forms, taps[first : first + 3 * WIDE])
         out[index] = value
-        carry = merged(carry, moments_of(value, planes_mask([act[x]])))
+        carry = merged(carry, moments_of(value, masks[x].astype(f32)))
     joint, square, both = carry
     lane = lax.broadcasted_iota(jnp.int32, (1, LANES), 1)
     joint = jnp.where(lane == LANES - 1, both, joint)
     for q in range(2):
-        joint = jnp.where(lane == C + q, owners[q, 0].astype(f32), joint)
+        joint = jnp.where(lane == C + q, owners[0, q].astype(f32), joint)
     row = jnp.concatenate([joint, square], axis=1)
     stats[...] = jnp.broadcast_to(row[None], stats.shape)
 
 
-def edges(act, x_before, x_after, partial, taps, part, owners, devices):
+def edges(masks, x_before, x_after, partial, taps, part, owners, devices):
     return pl.pallas_call(
         edge_kernel,
         out_shape=(
@@ -318,7 +327,7 @@
         out_specs=(VMEM, VMEM),
         compiler_params=params(16),
         name="edges",
-    )(act, x_before, x_after, partial, taps, part, owners)
+    )(masks, x_before, x_after, partial, taps, part, owners)
 
 
 def joined(table, width):
@@ -331,7 +340,7 @@
 
 
 def section_kernel(
-    mid, edge, act, table, gain, shift, weight, sent, names, stats, taps, down, cover, lines
+    mid, edge, act, table, gain, shift, weight, masks, cover, sent, names, stats, taps, down, lines
 ):
     level, groups = lax.axis_index("level"), lax.axis_size("level")
     for distance in range(4):
@@ -357,31 +366,21 @@
 
     total = count = jnp.zeros((1, 2 * LANES), f32)
     for group in range(0, SX // 2, GROUP):
-        blocks, coverings = [], []
+        blocks = []
         for X in range(group, group + GROUP):
-            pieces, covers = [], []
-            for a in range(2):
-                x = 2 * X + a
+            pieces = []
+            for x in (2 * X, 2 * X + 1):
                 conv = edge[0] if x == 0 else edge[1] if x == SX - 1 else mid[x - 1]
-                plane = act[x]
-                even, odd = rows_of([plane], 0), rows_of([plane], 1)
-                even_mask, odd_mask = mask_of(even), mask_of(odd)
-                mask = jnp.concatenate([even_mask, odd_mask], axis=1)
-                active = jnp.concatenate([even, odd], axis=1)
-                section = active + mask * jnp.maximum(conv * scale + moved, 0.0)
-                section = section.reshape(PAIRS, 2, 8, 2 * LANES)
+                active = jnp.concatenate([rows_of([act[x]], 0), rows_of([act[x]], 1)], axis=1)
+                gained = masks[x].astype(f32) * jnp.maximum(conv * scale + moved, 0.0)
+                section = (active + gained).reshape(PAIRS, 2, 8, 2 * LANES)
                 for c in range(2):
                     pieces.append(section[:, c].reshape(PAIRS * 8, 2 * LANES).astype(bf16))
-                both = jnp.maximum(even_mask, odd_mask).reshape(PAIRS, 2, 8, LANES)
-                covers.append(jnp.maximum(both[:, 0], both[:, 1]).reshape(PAIRS * 8, LANES))
             blocks.append(jnp.concatenate(pieces, axis=1))
-            coverings.append(jnp.maximum(covers[0], covers[1]))
         value = plain_dot(jnp.concatenate(blocks, axis=0), taps[...])
         value = value.astype(bf16).astype(f32)
-        covered = jnp.concatenate(coverings, axis=0)
-        covered = jnp.concatenate([covered, covered], axis=1)
+        covered = cover[group : group + GROUP].reshape(GROUP * PAIRS * 8, 2 * LANES)
         down[group : group + GROUP] = value.reshape(GROUP, PAIRS * 8, 2 * LANES)
-        cover[group : group + GROUP] = covered.reshape(GROUP, PAIRS * 8, 2 * LANES)
         total = total + jnp.sum(value * covered, axis=0, keepdims=True)
         count = count + jnp.sum(covered, axis=0, keepdims=True)
 
@@ -407,7 +406,7 @@
         sent[q] = coded.T[:C2]
 
 
-def section(mid, edge, act, table, gain, shift, weight, devices):
+def section(mid, edge, act, table, gain, shift, weight, masks, cover, devices):
     return pl.pallas_call(
         section_kernel,
         out_shape=(
@@ -415,17 +414,16 @@
             jax.ShapeDtypeStruct((4, 1, LANES), f32),
             jax.ShapeDtypeStruct((devices, 1, 4 * LANES), f32),
         ),
-        in_specs=[VMEM] * 7,
+        in_specs=[VMEM] * 9,
         out_specs=(VMEM,) * 3,
         scratch_shapes=[
             pltpu.VMEM((8 * LANES, 2 * LANES), bf16),
-            pltpu.VMEM((SX // 2, PAIRS * 8, 2 * LANES), f32),
             pltpu.VMEM((SX // 2, PAIRS * 8, 2 * LANES), f32),
             pltpu.VMEM((8, LANES), f32),
         ],
         compiler_params=params(20),
         name="section",
-    )(mid, edge, act, table, gain, shift, weight)
+    )(mid, edge, act, table, gain, shift, weight, masks, cover)
 
 
 def merge_kernel(table, near, back, out, up, down):
@@ -550,19 +548,19 @@
     y_low, y_high, coords, gates = pack_sides(brick_coords, features, occupancy)
     y_before = from_tile(y_high, 0, -1)
     y_after = from_tile(y_low, 0, 1)
-    act = pack(coords, features, gates)
+    act, masks, cover = pack(coords, features, gates)
     x_low, x_high = faces(act, y_before, y_after)
     x_before = from_tile(x_high, -1, 0)
     x_after = from_tile(x_low, 1, 0)
-    mid, partial, part, taps = middle(act, y_before, y_after, conv_weight)
+    mid, partial, part, taps = middle(act, masks, y_before, y_after, conv_weight)
     edge, stats = edges(
-        act,
+        masks,
         x_before,
         x_after,
         partial,
         taps,
         part,
-        coarse_owner,
+        coarse_owner.reshape(1, 2),
         space_count * level_count,
     )
     sent, names, stats2 = section(
@@ -573,6 +571,8 @@
         conv_gain[None],
         conv_shift[None],
         reduce_weight,
+        masks,
+        cover,
         space_count,
     )
     def up_level(block, distance):

time: 67.8 us -> 67.4 us (level)
  transfers between devices with their start and end apart: 9 -> 9, of which waited for: 1 -> 1; matrix products, arithmetic and copies ran while one was open for 0% -> 0% of each run, Pallas kernels for 15% -> 16%
where the time goes in v8:
time: 67.4 us; the launch traced here: 67.3 us
  blocking collectives  29.8 us (44%)
  Pallas kernels  18.5 us (27%)
  starting transfers between devices  13.3 us (20%)
  waiting for transfers between devices  5.31 us (8%)
    all_to_all x2, blocking collectives, to_all(): return lax.all_to_all(rows, axes, 0, 0, tiled=True)  29.8 us
    pallas_call x1, Pallas kernels, middle(): pl.pallas_call(middle_kernel, out_shape=(pltpu.VMEM((MID, PAIRS * SZ, 2 *...  8.64 us
    ppermute x4, starting transfers between devices, from_tile(): return lax.ppermute(block, 'space', route)  7.52 us
    ppermute x5, starting transfers between devices, up_level(): return lax.ppermute(block, 'level', route)  5.74 us
    ppermute x5, waiting for transfers between devices, up_level(): return lax.ppermute(block, 'level', route)  5.3 us
    pallas_call x1, Pallas kernels, settle(): pl.pallas_call(settle_kernel, out_shape=jax.ShapeDtypeStruct((8, C2, 512)...  2.2 us
    pallas_call x1, Pallas kernels, section(): pl.pallas_call(section_kernel, out_shape=(jax.ShapeDtypeStruct((2, C2, 51...  2.09 us
    pallas_call x1, Pallas kernels, pack_sides(): pl.pallas_call(sides_kernel, out_shape=(side, side, jax.ShapeDtypeStruct(...  2.04 us
  transfers between devices with their start and end apart: 9, of which 1 were waited for; matrix products, arithmetic and copies ran while one was open for 0% of the time, Pallas kernels for 16%

profile of v8, /device:TPU:0, one launch (start us, length us, event | category | flops | bytes accessed | tf_op | source)
XLA Modules:
  0.0 67.3 jit_solution(3948199334718997894)
XLA Ops:
  0.0 0.0 copy-start
  0.0 2.0 %pack_sides.1 = (bf16[16,16,128]{2,1,0:T(8,128)(2,1)S(1)}, bf16[16,16,128]{2,1,0:T(8,128)(2,1)S(1)}, s32[3,16]{1,0:T(4,128)S(1)}, s32[16,512]{1,0:T(8,128)S(1)}) custom-call(s32[3,16]{1,0:T(4,128)} %coords.1, bf16[16,96,512]{2,1,0:T(8,128)(2,1)} %features.3, s32[16,512]{1,0:T(8,128)} %occupancy.1), custom_call_target="tpu_custom_call" | custom-call | tf_op jit(solution)/shard_map/pack_sides/pallas_call | solution.py:100
  2.1 0.0 copy-start.1
  2.1 0.1 collective-permute-start
  2.1 1.7 %collective-permute-start.1 = (bf16[16,16,128]{2,1,0:T(8,128)(2,1)S(1)}, bf16[16,16,128]{2,1,0:T(8,128)(2,1)S(1)}, u32[]{:S(2)}, u32[]{:S(2)}) collective-permute-start(bf16[16,16,128]{2,1,0:T(8,128)(2,1)S(1)} %get-tuple-element.31), channel_id=1, source_target_pairs={{1,0},{2,1},{3,2},{0,3},{5,4},{6,5},{7,6},{4,7},{9,8},{10,9},{11,1... | collective-permute-start | bytes 196616 | tf_op jit(solution)/shard_map/ppermute | solution.py:546
  3.9 0.0 copy-done
  3.9 2.0 %pack.1 = (bf16[16,16,2,16,128]{4,3,2,1,0:T(8,128)(2,1)S(1)}, bf16[16,256,256]{2,1,0:T(8,128)(2,1)S(1)}, f32[8,128,256]{2,1,0:T(8,128)S(1)}) custom-call(s32[3,16]{1,0:T(4,128)S(1)} %get-tuple-element.26.coords, bf16[16,96,512]{2,1,0:T(8,128)(2,1)S(1)} %copy-done, s32[16,512]{1,0:T(8,128)S(1)} %get-tuple-element.27.occupancy), custom_call_target="tpu_custom_call" | custom-call | tf_op jit(solution)/shard_map/pack/pallas_call | solution.py:146
  5.9 0.0 collective-permute-done.y_before
  5.9 0.0 collective-permute-done.1.y_after
  6.0 3.3 %collective-permute-start.2 = (bf16[34,16,128]{2,1,0:T(8,128)(2,1)S(1)}, bf16[34,16,128]{2,1,0:T(8,128)(2,1)S(1)}, u32[]{:S(2)}, u32[]{:S(2)}) collective-permute-start(bf16[34,16,128]{2,1,0:T(8,128)(2,1)S(1)} %get-tuple-element.33), channel_id=1, source_target_pairs={{28,0},{29,1},{30,2},{31,3},{0,4},{1,5},{2,6},{3,7},{4,8},{5,9},{6... | collective-permute-start | bytes 417800 | tf_op jit(solution)/shard_map/ppermute | solution.py:546
  9.3 2.4 %collective-permute-start.3 = (bf16[34,16,128]{2,1,0:T(8,128)(2,1)S(1)}, bf16[34,16,128]{2,1,0:T(8,128)(2,1)S(1)}, u32[]{:S(2)}, u32[]{:S(2)}) collective-permute-start(bf16[34,16,128]{2,1,0:T(8,128)(2,1)S(1)} %get-tuple-element.34), channel_id=1, source_target_pairs={{4,0},{5,1},{6,2},{7,3},{8,4},{9,5},{10,6},{11,7},{12,8},{13,9},{1... | collective-permute-start | bytes 417800 | tf_op jit(solution)/shard_map/ppermute | solution.py:546
  11.7 0.0 copy-done.1
  11.7 0.0 copy-start.5
  11.7 8.6 %middle.1 = (f32[14,256,256]{2,1,0:T(8,128)S(1)}, f32[2,256,256]{2,1,0:T(8,128)S(1)}, f32[8,128]{1,0:T(8,128)S(1)}, bf16[3456,256]{1,0:T(8,128)(2,1)S(1)}) custom-call(bf16[16,16,2,16,128]{4,3,2,1,0:T(8,128)(2,1)S(1)} %get-tuple-element.28.act, bf16[16,256,256]{2,1,0:T(8,128)(2,1)S(1)} %get-tuple-element.29.masks, ...), custom_call_target="tpu_custom_call" | custom-call | tf_op jit(solution)/shard_map/middle/pallas_call | solution.py:283
  20.3 0.0 collective-permute-done.2.x_before
  20.4 0.0 collective-permute-done.3.x_after
  20.4 0.0 copy-done.5
  20.4 0.0 copy-start.2
  20.4 0.0 copy-start.6
  20.4 0.0 copy-start.7
  20.4 1.3 %edges.1 = (f32[2,256,256]{2,1,0:T(8,128)S(1)}, f32[128,1,256]{2,1,0:T(1,128)S(1)}) custom-call(bf16[16,256,256]{2,1,0:T(8,128)(2,1)S(1)} %get-tuple-element.29.masks, bf16[34,16,128]{2,1,0:T(8,128)(2,1)S(1)} %collective-permute-done.2.x_before, bf16[34,16,128]{2,1,0:T(8,128)(2,1)S(1)} %collective-permute-done.3.x_after, ...), custom_call_target="tpu_custom_call" | custom-call | tf_op jit(solution)/shard_map/edges/pallas_call | solution.py:320
  21.7 18.8 %all_to_all.10.table = f32[128,1,256]{2,1,0:T(1,128)S(1)} all-to-all(f32[128,1,256]{2,1,0:T(1,128)S(1)} %get-tuple-element.39), channel_id=1, replica_groups=mesh['level'=4,'space'=32] {'level','space'}, dimensions={0} | all-to-all | bytes 262144 | tf_op jit(solution)/shard_map/all_to_all | solution.py:522
  40.6 0.0 copy-done.2
  40.6 0.0 copy-done.6
  40.6 0.0 copy-done.7
  40.6 0.0 copy-start.3
  40.6 0.0 copy-start.4
  40.6 2.1 %section.1 = (bf16[2,192,512]{2,1,0:T(8,128)(2,1)S(1)}, f32[4,1,128]{2,1,0:T(1,128)S(1)}, f32[32,1,512]{2,1,0:T(1,128)S(1)}) custom-call(f32[14,256,256]{2,1,0:T(8,128)S(1)} %get-tuple-element.32.mid, f32[2,256,256]{2,1,0:T(8,128)S(1)} %get-tuple-element.38.edge, bf16[16,16,2,16,128]{4,3,2,1,0:T(8,128)(2,1)S(1)} %get-tuple-element.28.act, ...), custom_call_target="tpu_custom_call" | custom-call | tf_op jit(solution)/shard_map/section/pallas_call | solution.py:410
  42.7 1.0 %collective-permute-start.5 = (bf16[2,192,512]{2,1,0:T(8,128)(2,1)S(1)}, bf16[2,192,512]{2,1,0:T(8,128)(2,1)S(1)}, u32[]{:S(2)}, u32[]{:S(2)}) collective-permute-start(bf16[2,192,512]{2,1,0:T(8,128)(2,1)S(1)} %get-tuple-element.41.own), channel_id=1, source_target_pairs={{0,96},{32,0},{64,32},{96,64},{1,97},{33,1},{65,33},{97,65},{2,98}... | collective-permute-start | bytes 1179656 | tf_op jit(solution)/shard_map/ppermute | solution.py:580
  43.7 1.1 %collective-permute-start.4 = (bf16[2,192,512]{2,1,0:T(8,128)(2,1)S(1)}, bf16[2,192,512]{2,1,0:T(8,128)(2,1)S(1)}, u32[]{:S(2)}, u32[]{:S(2)}) collective-permute-start(bf16[2,192,512]{2,1,0:T(8,128)(2,1)S(1)} %get-tuple-element.41.own), channel_id=1, source_target_pairs={{0,32},{32,64},{64,96},{96,0},{1,33},{33,65},{65,97},{97,1},{2,34}... | collective-permute-start | bytes 1179656 | tf_op jit(solution)/shard_map/ppermute | solution.py:580
  44.8 11.0 %all_to_all.11.table = f32[32,1,512]{2,1,0:T(1,128)S(1)} all-to-all(f32[32,1,512]{2,1,0:T(1,128)S(1)} %get-tuple-element.42), channel_id=1, replica_groups=mesh['level'=4,'space'=32] {'space'}, dimensions={0} | all-to-all | bytes 131072 | tf_op jit(solution)/shard_map/all_to_all | solution.py:522
  55.8 0.0 collective-permute-done.5.back
  55.8 0.0 collective-permute-done.4.near
  55.8 0.2 merge.1
  56.0 0.9 %collective-permute-start.6 = (bf16[208,512]{1,0:T(8,128)(2,1)S(1)}, bf16[208,512]{1,0:T(8,128)(2,1)S(1)}, u32[]{:S(2)}, u32[]{:S(2)}) collective-permute-start(bf16[208,512]{1,0:T(8,128)(2,1)S(1)} %get-tuple-element.43), channel_id=1, source_target_pairs={{0,32},{32,64},{64,96},{96,0},{1,33},{33,65},{65,97},{97,1},{2,34}... | collective-permute-start | bytes 638984 | tf_op jit(solution)/shard_map/ppermute | solution.py:580
  56.9 2.4 %collective-permute-start.7 = (bf16[208,512]{1,0:T(8,128)(2,1)S(1)}, bf16[208,512]{1,0:T(8,128)(2,1)S(1)}, u32[]{:S(2)}, u32[]{:S(2)}) collective-permute-start(bf16[208,512]{1,0:T(8,128)(2,1)S(1)} %get-tuple-element.44), channel_id=1, source_target_pairs={{0,96},{32,0},{64,32},{96,64},{1,97},{33,1},{65,33},{97,65},{2,98}... | collective-permute-start | bytes 638984 | tf_op jit(solution)/shard_map/ppermute | solution.py:580
  59.3 0.3 collective-permute-start.8
  59.6 5.3 %collective-permute-done.8.row_far = f32[1,1,512]{2,1,0:T(1,128)S(1)} collective-permute-done((f32[1,1,512]{2,1,0:T(1,128)S(1)}, f32[1,1,512]{2,1,0:T(1,128)S(1)}, u32[]{:S(2)}, u32[]{:S(2)}) %collective-permute-start.8) | collective-permute-done | bytes 2080 | tf_op jit(solution)/shard_map/ppermute | solution.py:580
  64.9 0.0 collective-permute-done.6.far0
  64.9 0.0 collective-permute-done.7.far1
  64.9 0.0 copy-done.3
  64.9 0.0 copy-done.4
  64.9 2.2 %settle.1 = bf16[8,192,512]{2,1,0:T(8,128)(2,1)} custom-call(bf16[2,192,512]{2,1,0:T(8,128)(2,1)S(1)} %get-tuple-element.41.own, bf16[2,192,512]{2,1,0:T(8,128)(2,1)S(1)} %collective-permute-done.4.near, bf16[208,512]{1,0:T(8,128)(2,1)S(1)} %collective-permute-done.6.far0, bf16[208,512]{1,0:T(8,128)(2,1)S(1)} %collective-permute-done.7.far1, ...), custom_call_target="tpu_custom_call" | custom-call | tf_op jit(solution)/shard_map/settle/pallas_call | solution.py:506
  (1 shorter events, 0.0 us)
Async XLA Ops:
  0.0 3.9 %copy-start = (bf16[16,96,512]{2,1,0:T(8,128)(2,1)S(1)}, bf16[16,96,512]{2,1,0:T(8,128)(2,1)}, u32[]{:S(2)}) copy-start(bf16[16,96,512]{2,1,0:T(8,128)(2,1)} %features.3) | copy-start | bytes 4718596
  2.1 9.6 %copy-start.1 = (bf16[27,96,96]{2,1,0:T(8,128)(2,1)S(1)}, bf16[27,96,96]{2,1,0:T(8,128)(2,1)}, u32[]{:S(2)}) copy-start(bf16[27,96,96]{2,1,0:T(8,128)(2,1)} %weight.2) | copy-start | bytes 1492996
  2.1 3.9 %collective-permute-start = (bf16[16,16,128]{2,1,0:T(8,128)(2,1)S(1)}, bf16[16,16,128]{2,1,0:T(8,128)(2,1)S(1)}, u32[]{:S(2)}, u32[]{:S(2)}) collective-permute-start(bf16[16,16,128]{2,1,0:T(8,128)(2,1)S(1)} %get-tuple-element.30), channel_id=1, source_target_pairs={{3,0},{0,1},{1,2},{2,3},{7,4},{4,5},{5,6},{6,7},{11,8},{8,9},{9,10... | collective-permute-start | bytes 196616 | tf_op jit(solution)/shard_map/ppermute | solution.py:546
  2.1 3.8 %collective-permute-start.1 = (bf16[16,16,128]{2,1,0:T(8,128)(2,1)S(1)}, bf16[16,16,128]{2,1,0:T(8,128)(2,1)S(1)}, u32[]{:S(2)}, u32[]{:S(2)}) collective-permute-start(bf16[16,16,128]{2,1,0:T(8,128)(2,1)S(1)} %get-tuple-element.31), channel_id=1, source_target_pairs={{1,0},{2,1},{3,2},{0,3},{5,4},{6,5},{7,6},{4,7},{9,8},{10,9},{11,1... | collective-permute-start | bytes 196616 | tf_op jit(solution)/shard_map/ppermute | solution.py:546
  6.0 14.4 %collective-permute-start.2 = (bf16[34,16,128]{2,1,0:T(8,128)(2,1)S(1)}, bf16[34,16,128]{2,1,0:T(8,128)(2,1)S(1)}, u32[]{:S(2)}, u32[]{:S(2)}) collective-permute-start(bf16[34,16,128]{2,1,0:T(8,128)(2,1)S(1)} %get-tuple-element.33), channel_id=1, source_target_pairs={{28,0},{29,1},{30,2},{31,3},{0,4},{1,5},{2,6},{3,7},{4,8},{5,9},{6... | collective-permute-start | bytes 417800 | tf_op jit(solution)/shard_map/ppermute | solution.py:546
  9.3 11.0 %collective-permute-start.3 = (bf16[34,16,128]{2,1,0:T(8,128)(2,1)S(1)}, bf16[34,16,128]{2,1,0:T(8,128)(2,1)S(1)}, u32[]{:S(2)}, u32[]{:S(2)}) collective-permute-start(bf16[34,16,128]{2,1,0:T(8,128)(2,1)S(1)} %get-tuple-element.34), channel_id=1, source_target_pairs={{4,0},{5,1},{6,2},{7,3},{8,4},{9,5},{10,6},{11,7},{12,8},{13,9},{1... | collective-permute-start | bytes 417800 | tf_op jit(solution)/shard_map/ppermute | solution.py:546
  11.7 8.7 %copy-start.5 = (s32[2,1]{0,1:T(1,128)S(1)}, s32[2,1]{0,1:T(1,128)}, u32[]{:S(2)}) copy-start(s32[2,1]{0,1:T(1,128)} %param.13) | copy-start | bytes 28
  20.4 20.2 %copy-start.2 = (bf16[8,192,96]{2,1,0:T(8,128)(2,1)S(1)}, bf16[8,192,96]{2,1,0:T(8,128)(2,1)}, u32[]{:S(2)}) copy-start(bf16[8,192,96]{2,1,0:T(8,128)(2,1)} %weight.3) | copy-start | bytes 884740
  20.4 20.2 %copy-start.6 = (f32[96]{0:T(128)S(1)}, f32[96]{0:T(128)}, u32[]{:S(2)}) copy-start(f32[96]{0:T(128)} %param.15) | copy-start | bytes 1156
  20.4 20.2 %copy-start.7 = (f32[96]{0:T(128)S(1)}, f32[96]{0:T(128)}, u32[]{:S(2)}) copy-start(f32[96]{0:T(128)} %param.16) | copy-start | bytes 1156
  40.6 24.3 %copy-start.3 = (f32[192]{0:T(256)S(1)}, f32[192]{0:T(256)}, u32[]{:S(2)}) copy-start(f32[192]{0:T(256)} %param.18) | copy-start | bytes 2308
  40.6 24.3 %copy-start.4 = (f32[192]{0:T(256)S(1)}, f32[192]{0:T(256)}, u32[]{:S(2)}) copy-start(f32[192]{0:T(256)} %param.19) | copy-start | bytes 2308
  42.7 13.1 %collective-permute-start.5 = (bf16[2,192,512]{2,1,0:T(8,128)(2,1)S(1)}, bf16[2,192,512]{2,1,0:T(8,128)(2,1)S(1)}, u32[]{:S(2)}, u32[]{:S(2)}) collective-permute-start(bf16[2,192,512]{2,1,0:T(8,128)(2,1)S(1)} %get-tuple-element.41.own), channel_id=1, source_target_pairs={{0,96},{32,0},{64,32},{96,64},{1,97},{33,1},{65,33},{97,65},{2,98}... | collective-permute-start | bytes 1179656 | tf_op jit(solution)/shard_map/ppermute | solution.py:580
  43.7 12.1 %collective-permute-start.4 = (bf16[2,192,512]{2,1,0:T(8,128)(2,1)S(1)}, bf16[2,192,512]{2,1,0:T(8,128)(2,1)S(1)}, u32[]{:S(2)}, u32[]{:S(2)}) collective-permute-start(bf16[2,192,512]{2,1,0:T(8,128)(2,1)S(1)} %get-tuple-element.41.own), channel_id=1, source_target_pairs={{0,32},{32,64},{64,96},{96,0},{1,33},{33,65},{65,97},{97,1},{2,34}... | collective-permute-start | bytes 1179656 | tf_op jit(solution)/shard_map/ppermute | solution.py:580
  56.0 8.9 %collective-permute-start.6 = (bf16[208,512]{1,0:T(8,128)(2,1)S(1)}, bf16[208,512]{1,0:T(8,128)(2,1)S(1)}, u32[]{:S(2)}, u32[]{:S(2)}) collective-permute-start(bf16[208,512]{1,0:T(8,128)(2,1)S(1)} %get-tuple-element.43), channel_id=1, source_target_pairs={{0,32},{32,64},{64,96},{96,0},{1,33},{33,65},{65,97},{97,1},{2,34}... | collective-permute-start | bytes 638984 | tf_op jit(solution)/shard_map/ppermute | solution.py:580
  56.9 8.0 %collective-permute-start.7 = (bf16[208,512]{1,0:T(8,128)(2,1)S(1)}, bf16[208,512]{1,0:T(8,128)(2,1)S(1)}, u32[]{:S(2)}, u32[]{:S(2)}) collective-permute-start(bf16[208,512]{1,0:T(8,128)(2,1)S(1)} %get-tuple-element.44), channel_id=1, source_target_pairs={{0,96},{32,0},{64,32},{96,64},{1,97},{33,1},{65,33},{97,65},{2,98}... | collective-permute-start | bytes 638984 | tf_op jit(solution)/shard_map/ppermute | solution.py:580
  59.3 5.6 %collective-permute-start.8 = (f32[1,1,512]{2,1,0:T(1,128)S(1)}, f32[1,1,512]{2,1,0:T(1,128)S(1)}, u32[]{:S(2)}, u32[]{:S(2)}) collective-permute-start(f32[1,1,512]{2,1,0:T(1,128)S(1)} %get-tuple-element.46.row_here), channel_id=1, source_target_pairs={{0,64},{32,96},{64,0},{96,32},{1,65},{33,97},{65,1},{97,33},{2,66}... | collective-permute-start | bytes 6152 | tf_op jit(solution)/shard_map/ppermute | solution.py:580

commit v9 on v8

--- a/solution.py
+++ b/solution.py
@@ -217,7 +217,7 @@
 
 
 MID = SX - 2
-STEP = 2
+STEP = 1
 GROUP = 2
 
 

time: 67.4 us -> 67.5 us (level)
  no operation moved by 1% of the time
where the time goes in v9:
time: 67.5 us; the launch traced here: 67.4 us
  blocking collectives  29.8 us (44%)
  Pallas kernels  18.6 us (28%)
  starting transfers between devices  13.3 us (20%)
  waiting for transfers between devices  5.31 us (8%)
    all_to_all x2, blocking collectives, to_all(): return lax.all_to_all(rows, axes, 0, 0, tiled=True)  29.8 us
    pallas_call x1, Pallas kernels, middle(): pl.pallas_call(middle_kernel, out_shape=(pltpu.VMEM((MID, PAIRS * SZ, 2 *...  8.72 us
    ppermute x4, starting transfers between devices, from_tile(): return lax.ppermute(block, 'space', route)  7.52 us
    ppermute x5, starting transfers between devices, up_level(): return lax.ppermute(block, 'level', route)  5.74 us
    ppermute x5, waiting for transfers between devices, up_level(): return lax.ppermute(block, 'level', route)  5.3 us
    pallas_call x1, Pallas kernels, settle(): pl.pallas_call(settle_kernel, out_shape=jax.ShapeDtypeStruct((8, C2, 512)...  2.2 us
    pallas_call x1, Pallas kernels, section(): pl.pallas_call(section_kernel, out_shape=(jax.ShapeDtypeStruct((2, C2, 51...  2.09 us
    pallas_call x1, Pallas kernels, pack_sides(): pl.pallas_call(sides_kernel, out_shape=(side, side, jax.ShapeDtypeStruct(...  2.04 us
  transfers between devices with their start and end apart: 9, of which 1 were waited for; matrix products, arithmetic and copies ran while one was open for 0% of the time, Pallas kernels for 16%

profile of v9, /device:TPU:0, one launch (start us, length us, event | category | flops | bytes accessed | tf_op | source)
XLA Modules:
  0.0 67.4 jit_solution(6756992806098760969)
XLA Ops:
  0.0 0.0 copy-start
  0.0 2.0 %pack_sides.1 = (bf16[16,16,128]{2,1,0:T(8,128)(2,1)S(1)}, bf16[16,16,128]{2,1,0:T(8,128)(2,1)S(1)}, s32[3,16]{1,0:T(4,128)S(1)}, s32[16,512]{1,0:T(8,128)S(1)}) custom-call(s32[3,16]{1,0:T(4,128)} %coords.1, bf16[16,96,512]{2,1,0:T(8,128)(2,1)} %features.3, s32[16,512]{1,0:T(8,128)} %occupancy.1), custom_call_target="tpu_custom_call" | custom-call | tf_op jit(solution)/shard_map/pack_sides/pallas_call | solution.py:100
  2.1 0.0 copy-start.1
  2.1 0.1 collective-permute-start
  2.1 1.7 %collective-permute-start.1 = (bf16[16,16,128]{2,1,0:T(8,128)(2,1)S(1)}, bf16[16,16,128]{2,1,0:T(8,128)(2,1)S(1)}, u32[]{:S(2)}, u32[]{:S(2)}) collective-permute-start(bf16[16,16,128]{2,1,0:T(8,128)(2,1)S(1)} %get-tuple-element.31), channel_id=1, source_target_pairs={{1,0},{2,1},{3,2},{0,3},{5,4},{6,5},{7,6},{4,7},{9,8},{10,9},{11,1... | collective-permute-start | bytes 196616 | tf_op jit(solution)/shard_map/ppermute | solution.py:546
  3.9 0.0 copy-done
  3.9 2.0 %pack.1 = (bf16[16,16,2,16,128]{4,3,2,1,0:T(8,128)(2,1)S(1)}, bf16[16,256,256]{2,1,0:T(8,128)(2,1)S(1)}, f32[8,128,256]{2,1,0:T(8,128)S(1)}) custom-call(s32[3,16]{1,0:T(4,128)S(1)} %get-tuple-element.26.coords, bf16[16,96,512]{2,1,0:T(8,128)(2,1)S(1)} %copy-done, s32[16,512]{1,0:T(8,128)S(1)} %get-tuple-element.27.occupancy), custom_call_target="tpu_custom_call" | custom-call | tf_op jit(solution)/shard_map/pack/pallas_call | solution.py:146
  5.9 0.0 collective-permute-done.y_before
  5.9 0.0 collective-permute-done.1.y_after
  6.0 3.3 %collective-permute-start.2 = (bf16[34,16,128]{2,1,0:T(8,128)(2,1)S(1)}, bf16[34,16,128]{2,1,0:T(8,128)(2,1)S(1)}, u32[]{:S(2)}, u32[]{:S(2)}) collective-permute-start(bf16[34,16,128]{2,1,0:T(8,128)(2,1)S(1)} %get-tuple-element.33), channel_id=1, source_target_pairs={{28,0},{29,1},{30,2},{31,3},{0,4},{1,5},{2,6},{3,7},{4,8},{5,9},{6... | collective-permute-start | bytes 417800 | tf_op jit(solution)/shard_map/ppermute | solution.py:546
  9.3 2.4 %collective-permute-start.3 = (bf16[34,16,128]{2,1,0:T(8,128)(2,1)S(1)}, bf16[34,16,128]{2,1,0:T(8,128)(2,1)S(1)}, u32[]{:S(2)}, u32[]{:S(2)}) collective-permute-start(bf16[34,16,128]{2,1,0:T(8,128)(2,1)S(1)} %get-tuple-element.34), channel_id=1, source_target_pairs={{4,0},{5,1},{6,2},{7,3},{8,4},{9,5},{10,6},{11,7},{12,8},{13,9},{1... | collective-permute-start | bytes 417800 | tf_op jit(solution)/shard_map/ppermute | solution.py:546
  11.7 0.0 copy-done.1
  11.7 0.0 copy-start.5
  11.7 8.7 %middle.1 = (f32[14,256,256]{2,1,0:T(8,128)S(1)}, f32[2,256,256]{2,1,0:T(8,128)S(1)}, f32[8,128]{1,0:T(8,128)S(1)}, bf16[3456,256]{1,0:T(8,128)(2,1)S(1)}) custom-call(bf16[16,16,2,16,128]{4,3,2,1,0:T(8,128)(2,1)S(1)} %get-tuple-element.28.act, bf16[16,256,256]{2,1,0:T(8,128)(2,1)S(1)} %get-tuple-element.29.masks, ...), custom_call_target="tpu_custom_call" | custom-call | tf_op jit(solution)/shard_map/middle/pallas_call | solution.py:283
  20.4 0.0 collective-permute-done.2.x_before
  20.4 0.0 collective-permute-done.3.x_after
  20.4 0.0 copy-done.5
  20.5 0.0 copy-start.2
  20.5 0.0 copy-start.6
  20.5 0.0 copy-start.7
  20.5 1.3 %edges.1 = (f32[2,256,256]{2,1,0:T(8,128)S(1)}, f32[128,1,256]{2,1,0:T(1,128)S(1)}) custom-call(bf16[16,256,256]{2,1,0:T(8,128)(2,1)S(1)} %get-tuple-element.29.masks, bf16[34,16,128]{2,1,0:T(8,128)(2,1)S(1)} %collective-permute-done.2.x_before, bf16[34,16,128]{2,1,0:T(8,128)(2,1)S(1)} %collective-permute-done.3.x_after, ...), custom_call_target="tpu_custom_call" | custom-call | tf_op jit(solution)/shard_map/edges/pallas_call | solution.py:320
  21.8 18.8 %all_to_all.10.table = f32[128,1,256]{2,1,0:T(1,128)S(1)} all-to-all(f32[128,1,256]{2,1,0:T(1,128)S(1)} %get-tuple-element.39), channel_id=1, replica_groups=mesh['level'=4,'space'=32] {'level','space'}, dimensions={0} | all-to-all | bytes 262144 | tf_op jit(solution)/shard_map/all_to_all | solution.py:522
  40.6 0.0 copy-done.2
  40.6 0.0 copy-done.6
  40.6 0.0 copy-done.7
  40.6 0.0 copy-start.3
  40.7 0.0 copy-start.4
  40.7 2.1 %section.1 = (bf16[2,192,512]{2,1,0:T(8,128)(2,1)S(1)}, f32[4,1,128]{2,1,0:T(1,128)S(1)}, f32[32,1,512]{2,1,0:T(1,128)S(1)}) custom-call(f32[14,256,256]{2,1,0:T(8,128)S(1)} %get-tuple-element.32.mid, f32[2,256,256]{2,1,0:T(8,128)S(1)} %get-tuple-element.38.edge, bf16[16,16,2,16,128]{4,3,2,1,0:T(8,128)(2,1)S(1)} %get-tuple-element.28.act, ...), custom_call_target="tpu_custom_call" | custom-call | tf_op jit(solution)/shard_map/section/pallas_call | solution.py:410
  42.8 1.0 %collective-permute-start.5 = (bf16[2,192,512]{2,1,0:T(8,128)(2,1)S(1)}, bf16[2,192,512]{2,1,0:T(8,128)(2,1)S(1)}, u32[]{:S(2)}, u32[]{:S(2)}) collective-permute-start(bf16[2,192,512]{2,1,0:T(8,128)(2,1)S(1)} %get-tuple-element.41.own), channel_id=1, source_target_pairs={{0,96},{32,0},{64,32},{96,64},{1,97},{33,1},{65,33},{97,65},{2,98}... | collective-permute-start | bytes 1179656 | tf_op jit(solution)/shard_map/ppermute | solution.py:580
  43.7 1.1 %collective-permute-start.4 = (bf16[2,192,512]{2,1,0:T(8,128)(2,1)S(1)}, bf16[2,192,512]{2,1,0:T(8,128)(2,1)S(1)}, u32[]{:S(2)}, u32[]{:S(2)}) collective-permute-start(bf16[2,192,512]{2,1,0:T(8,128)(2,1)S(1)} %get-tuple-element.41.own), channel_id=1, source_target_pairs={{0,32},{32,64},{64,96},{96,0},{1,33},{33,65},{65,97},{97,1},{2,34}... | collective-permute-start | bytes 1179656 | tf_op jit(solution)/shard_map/ppermute | solution.py:580
  44.9 11.0 %all_to_all.11.table = f32[32,1,512]{2,1,0:T(1,128)S(1)} all-to-all(f32[32,1,512]{2,1,0:T(1,128)S(1)} %get-tuple-element.42), channel_id=1, replica_groups=mesh['level'=4,'space'=32] {'space'}, dimensions={0} | all-to-all | bytes 131072 | tf_op jit(solution)/shard_map/all_to_all | solution.py:522
  55.8 0.0 collective-permute-done.5.back
  55.8 0.0 collective-permute-done.4.near
  55.8 0.2 merge.1
  56.0 0.9 %collective-permute-start.6 = (bf16[208,512]{1,0:T(8,128)(2,1)S(1)}, bf16[208,512]{1,0:T(8,128)(2,1)S(1)}, u32[]{:S(2)}, u32[]{:S(2)}) collective-permute-start(bf16[208,512]{1,0:T(8,128)(2,1)S(1)} %get-tuple-element.43), channel_id=1, source_target_pairs={{0,32},{32,64},{64,96},{96,0},{1,33},{33,65},{65,97},{97,1},{2,34}... | collective-permute-start | bytes 638984 | tf_op jit(solution)/shard_map/ppermute | solution.py:580
  56.9 2.4 %collective-permute-start.7 = (bf16[208,512]{1,0:T(8,128)(2,1)S(1)}, bf16[208,512]{1,0:T(8,128)(2,1)S(1)}, u32[]{:S(2)}, u32[]{:S(2)}) collective-permute-start(bf16[208,512]{1,0:T(8,128)(2,1)S(1)} %get-tuple-element.44), channel_id=1, source_target_pairs={{0,96},{32,0},{64,32},{96,64},{1,97},{33,1},{65,33},{97,65},{2,98}... | collective-permute-start | bytes 638984 | tf_op jit(solution)/shard_map/ppermute | solution.py:580
  59.3 0.3 collective-permute-start.8
  59.7 5.3 %collective-permute-done.8.row_far = f32[1,1,512]{2,1,0:T(1,128)S(1)} collective-permute-done((f32[1,1,512]{2,1,0:T(1,128)S(1)}, f32[1,1,512]{2,1,0:T(1,128)S(1)}, u32[]{:S(2)}, u32[]{:S(2)}) %collective-permute-start.8) | collective-permute-done | bytes 2080 | tf_op jit(solution)/shard_map/ppermute | solution.py:580
  65.0 0.0 collective-permute-done.6.far0
  65.0 0.0 collective-permute-done.7.far1
  65.0 0.0 copy-done.3
  65.0 0.0 copy-done.4
  65.0 2.2 %settle.1 = bf16[8,192,512]{2,1,0:T(8,128)(2,1)} custom-call(bf16[2,192,512]{2,1,0:T(8,128)(2,1)S(1)} %get-tuple-element.41.own, bf16[2,192,512]{2,1,0:T(8,128)(2,1)S(1)} %collective-permute-done.4.near, bf16[208,512]{1,0:T(8,128)(2,1)S(1)} %collective-permute-done.6.far0, bf16[208,512]{1,0:T(8,128)(2,1)S(1)} %collective-permute-done.7.far1, ...), custom_call_target="tpu_custom_call" | custom-call | tf_op jit(solution)/shard_map/settle/pallas_call | solution.py:506
  (1 shorter events, 0.0 us)
Async XLA Ops:
  0.0 3.9 %copy-start = (bf16[16,96,512]{2,1,0:T(8,128)(2,1)S(1)}, bf16[16,96,512]{2,1,0:T(8,128)(2,1)}, u32[]{:S(2)}) copy-start(bf16[16,96,512]{2,1,0:T(8,128)(2,1)} %features.3) | copy-start | bytes 4718596
  2.1 9.6 %copy-start.1 = (bf16[27,96,96]{2,1,0:T(8,128)(2,1)S(1)}, bf16[27,96,96]{2,1,0:T(8,128)(2,1)}, u32[]{:S(2)}) copy-start(bf16[27,96,96]{2,1,0:T(8,128)(2,1)} %weight.2) | copy-start | bytes 1492996
  2.1 3.9 %collective-permute-start = (bf16[16,16,128]{2,1,0:T(8,128)(2,1)S(1)}, bf16[16,16,128]{2,1,0:T(8,128)(2,1)S(1)}, u32[]{:S(2)}, u32[]{:S(2)}) collective-permute-start(bf16[16,16,128]{2,1,0:T(8,128)(2,1)S(1)} %get-tuple-element.30), channel_id=1, source_target_pairs={{3,0},{0,1},{1,2},{2,3},{7,4},{4,5},{5,6},{6,7},{11,8},{8,9},{9,10... | collective-permute-start | bytes 196616 | tf_op jit(solution)/shard_map/ppermute | solution.py:546
  2.1 3.8 %collective-permute-start.1 = (bf16[16,16,128]{2,1,0:T(8,128)(2,1)S(1)}, bf16[16,16,128]{2,1,0:T(8,128)(2,1)S(1)}, u32[]{:S(2)}, u32[]{:S(2)}) collective-permute-start(bf16[16,16,128]{2,1,0:T(8,128)(2,1)S(1)} %get-tuple-element.31), channel_id=1, source_target_pairs={{1,0},{2,1},{3,2},{0,3},{5,4},{6,5},{7,6},{4,7},{9,8},{10,9},{11,1... | collective-permute-start | bytes 196616 | tf_op jit(solution)/shard_map/ppermute | solution.py:546
  6.0 14.4 %collective-permute-start.2 = (bf16[34,16,128]{2,1,0:T(8,128)(2,1)S(1)}, bf16[34,16,128]{2,1,0:T(8,128)(2,1)S(1)}, u32[]{:S(2)}, u32[]{:S(2)}) collective-permute-start(bf16[34,16,128]{2,1,0:T(8,128)(2,1)S(1)} %get-tuple-element.33), channel_id=1, source_target_pairs={{28,0},{29,1},{30,2},{31,3},{0,4},{1,5},{2,6},{3,7},{4,8},{5,9},{6... | collective-permute-start | bytes 417800 | tf_op jit(solution)/shard_map/ppermute | solution.py:546
  9.3 11.1 %collective-permute-start.3 = (bf16[34,16,128]{2,1,0:T(8,128)(2,1)S(1)}, bf16[34,16,128]{2,1,0:T(8,128)(2,1)S(1)}, u32[]{:S(2)}, u32[]{:S(2)}) collective-permute-start(bf16[34,16,128]{2,1,0:T(8,128)(2,1)S(1)} %get-tuple-element.34), channel_id=1, source_target_pairs={{4,0},{5,1},{6,2},{7,3},{8,4},{9,5},{10,6},{11,7},{12,8},{13,9},{1... | collective-permute-start | bytes 417800 | tf_op jit(solution)/shard_map/ppermute | solution.py:546
  11.7 8.7 %copy-start.5 = (s32[2,1]{0,1:T(1,128)S(1)}, s32[2,1]{0,1:T(1,128)}, u32[]{:S(2)}) copy-start(s32[2,1]{0,1:T(1,128)} %param.13) | copy-start | bytes 28
  20.5 20.2 %copy-start.2 = (bf16[8,192,96]{2,1,0:T(8,128)(2,1)S(1)}, bf16[8,192,96]{2,1,0:T(8,128)(2,1)}, u32[]{:S(2)}) copy-start(bf16[8,192,96]{2,1,0:T(8,128)(2,1)} %weight.3) | copy-start | bytes 884740
  20.5 20.2 %copy-start.6 = (f32[96]{0:T(128)S(1)}, f32[96]{0:T(128)}, u32[]{:S(2)}) copy-start(f32[96]{0:T(128)} %param.15) | copy-start | bytes 1156
  20.5 20.2 %copy-start.7 = (f32[96]{0:T(128)S(1)}, f32[96]{0:T(128)}, u32[]{:S(2)}) copy-start(f32[96]{0:T(128)} %param.16) | copy-start | bytes 1156
  40.6 24.3 %copy-start.3 = (f32[192]{0:T(256)S(1)}, f32[192]{0:T(256)}, u32[]{:S(2)}) copy-start(f32[192]{0:T(256)} %param.18) | copy-start | bytes 2308
  40.7 24.3 %copy-start.4 = (f32[192]{0:T(256)S(1)}, f32[192]{0:T(256)}, u32[]{:S(2)}) copy-start(f32[192]{0:T(256)} %param.19) | copy-start | bytes 2308
  42.8 13.1 %collective-permute-start.5 = (bf16[2,192,512]{2,1,0:T(8,128)(2,1)S(1)}, bf16[2,192,512]{2,1,0:T(8,128)(2,1)S(1)}, u32[]{:S(2)}, u32[]{:S(2)}) collective-permute-start(bf16[2,192,512]{2,1,0:T(8,128)(2,1)S(1)} %get-tuple-element.41.own), channel_id=1, source_target_pairs={{0,96},{32,0},{64,32},{96,64},{1,97},{33,1},{65,33},{97,65},{2,98}... | collective-permute-start | bytes 1179656 | tf_op jit(solution)/shard_map/ppermute | solution.py:580
  43.7 12.1 %collective-permute-start.4 = (bf16[2,192,512]{2,1,0:T(8,128)(2,1)S(1)}, bf16[2,192,512]{2,1,0:T(8,128)(2,1)S(1)}, u32[]{:S(2)}, u32[]{:S(2)}) collective-permute-start(bf16[2,192,512]{2,1,0:T(8,128)(2,1)S(1)} %get-tuple-element.41.own), channel_id=1, source_target_pairs={{0,32},{32,64},{64,96},{96,0},{1,33},{33,65},{65,97},{97,1},{2,34}... | collective-permute-start | bytes 1179656 | tf_op jit(solution)/shard_map/ppermute | solution.py:580
  56.0 8.9 %collective-permute-start.6 = (bf16[208,512]{1,0:T(8,128)(2,1)S(1)}, bf16[208,512]{1,0:T(8,128)(2,1)S(1)}, u32[]{:S(2)}, u32[]{:S(2)}) collective-permute-start(bf16[208,512]{1,0:T(8,128)(2,1)S(1)} %get-tuple-element.43), channel_id=1, source_target_pairs={{0,32},{32,64},{64,96},{96,0},{1,33},{33,65},{65,97},{97,1},{2,34}... | collective-permute-start | bytes 638984 | tf_op jit(solution)/shard_map/ppermute | solution.py:580
  56.9 8.0 %collective-permute-start.7 = (bf16[208,512]{1,0:T(8,128)(2,1)S(1)}, bf16[208,512]{1,0:T(8,128)(2,1)S(1)}, u32[]{:S(2)}, u32[]{:S(2)}) collective-permute-start(bf16[208,512]{1,0:T(8,128)(2,1)S(1)} %get-tuple-element.44), channel_id=1, source_target_pairs={{0,96},{32,0},{64,32},{96,64},{1,97},{33,1},{65,33},{97,65},{2,98}... | collective-permute-start | bytes 638984 | tf_op jit(solution)/shard_map/ppermute | solution.py:580
  59.3 5.6 %collective-permute-start.8 = (f32[1,1,512]{2,1,0:T(1,128)S(1)}, f32[1,1,512]{2,1,0:T(1,128)S(1)}, u32[]{:S(2)}, u32[]{:S(2)}) collective-permute-start(f32[1,1,512]{2,1,0:T(1,128)S(1)} %get-tuple-element.46.row_here), channel_id=1, source_target_pairs={{0,64},{32,96},{64,0},{96,32},{1,65},{33,97},{65,1},{97,33},{2,66}... | collective-permute-start | bytes 6152 | tf_op jit(solution)/shard_map/ppermute | solution.py:580
